TPU v7x, 256 devices: a whole 4x4x8 slice. The times are simulated.
256 devices in a mesh: head: 8 (over y, core), inner: 2 (over z_hi), outer: 16 (over z_lo, x).
Axes of the slice: x: 4, y: 4, z: 8 (z_hi: 2, z_lo: 4; z = z_hi * 4 + z_lo), core: 2. Of those that a mesh axis runs over, the one named last changes fastest.
Arguments:
- query: bfloat16 [16384, 48, 128], P(('head', 'inner', 'outer')), may hold values from -6 to 6
- keys: bfloat16 [16384, 8, 128], P(('head', 'inner', 'outer')), may hold values from -6 to 6
- values: bfloat16 [16384, 8, 128], P(('head', 'inner', 'outer')), may hold values from -6 to 6
- attn_out: bfloat16 [16384, 48, 128], P(('head', 'inner', 'outer')), may hold values from -1.5 to 1.5
- grad_out: bfloat16 [16384, 48, 128], P(('head', 'inner', 'outer')), may hold values from -6 to 6
- log_norm: float32 [16384, 48], P(('head', 'inner', 'outer'))
- block_order: int32 [256], replicated, may hold values from 0 to 255, as said below
Outputs:
- grad_query: bfloat16 [16384, 48, 128], P(('head', 'inner', 'outer'))
- grad_keys: bfloat16 [16384, 8, 128], P(('head', 'inner', 'outer'))
- grad_values: bfloat16 [16384, 8, 128], P(('head', 'inner', 'outer'))
Inputs may be any that keep to these rules, and one draw needn't show every extreme that they name: `block_order`: each place of the sequence's 256 blocks appears once.
All inputs are finite; a program needn't handle non-finite values.
Results may differ from a plain program's by a relative error of at most 0.0056.
Values may be sent and summed in bfloat16 or wider, within the bound.
No kernel may reach another device: no remote copies, remote signals or barrier semaphores. Data moves between devices by JAX's collectives and lax.ppermute only.
A program may use at most 128 MiB of HBM per device.

v0:
```python
import math

import jax
import jax.numpy as jnp
from jax import lax
from jax.experimental import pallas as pl
from jax.experimental.pallas import tpu as pltpu
from jax.sharding import PartitionSpec as P

LOG2E = math.log2(math.e)
NT = (((1,), (1,)), ((), ()))
NN = (((1,), (0,)), ((), ()))
TN = (((0,), (0,)), ((), ()))
f32 = jnp.float32
bf16 = jnp.bfloat16


def attention_part(tables, packed, kv_own, kv_partner, dq_start, keys_step, rows_step, name):
    src, parts, T, D = packed.shape
    heads = (parts - 1) // 2
    R = heads * T
    n = 2 * src
    U, W = keys_step * T, rows_step * R
    groups = n // keys_step
    scale = D ** (-0.5)
    lanes = R // D
    last = dq_start is not None

    def body(qid, qord, kid, kord, cnt, packed_ref, own_ref, partner_ref, *rest):
        if last:
            start_ref, dq_ref, gown_ref, gpartner_ref, *scratch = rest
            q_s, do_s, st_s, kv_s, g_s, k_s, v_s, dk_s, dv_s, dq_s = scratch
            dq_s[...] = start_ref[...]
        else:
            dq_s, gown_ref, gpartner_ref, *scratch = rest
            q_s, do_s, st_s, kv_s, g_s, k_s, v_s, dk_s, dv_s = scratch
            dq_s[...] = jnp.zeros_like(dq_s)
        kv_s[0:src] = own_ref[...]
        kv_s[src:n] = partner_ref[...]

        def prepare(i, carry):
            b = qid[i]
            at = pl.ds(pl.multiple_of(i * R, R), R)
            q_s[at] = packed_ref[b, 0:heads].reshape(R, D)
            do_s[at] = packed_ref[b, heads : 2 * heads].reshape(R, D)
            st = packed_ref[b, 2 * heads].astype(f32)
            st = st[0:8] + st[8:16] + st[16:24]
            st_s[i, 0:1] = jnp.concatenate([st[j : j + 1] for j in range(lanes)], axis=1)
            st_s[i, 1:2] = jnp.concatenate([st[j : j + 1] for j in range(lanes, 2 * lanes)], axis=1)
            return carry

        lax.fori_loop(0, src, prepare, 0)
        lead = lax.broadcasted_iota(jnp.int32, (T, R), 1) % T - lax.broadcasted_iota(
            jnp.int32, (T, R), 0
        )

        def group(g, carry):
            for j in range(keys_step):
                b = kid[g * keys_step + j]
                k_s[pl.ds(j * T, T)] = kv_s[b, 0]
                v_s[pl.ds(j * T, T)] = kv_s[b, 1]
            dk_s[...] = jnp.zeros_like(dk_s)
            dv_s[...] = jnp.zeros_like(dv_s)

            def step(i, inner):
                at = pl.ds(pl.multiple_of(i * W, W), W)
                q, do, k, v = q_s[at], do_s[at], k_s[...], v_s[...]
                s = lax.dot_general(k, q, NT, preferred_element_type=f32)
                dp = lax.dot_general(v, do, NT, preferred_element_type=f32)
                p_cols, ds_cols = [], []
                for h in range(rows_step):
                    row = i * rows_step + h
                    lse, delta, place = st_s[row, 0:1], st_s[row, 1:2], qord[row]
                    p_rows, ds_rows = [], []
                    for j in range(keys_step):
                        behind = (kord[g * keys_step + j] - place) * T
                        cut = (slice(j * T, (j + 1) * T), slice(h * R, (h + 1) * R))
                        p = jnp.where(
                            lead >= behind, jnp.exp2(s[cut] * (scale * LOG2E) - lse), 0.0
                        )
                        ds_rows.append((p * (dp[cut] - delta)).astype(bf16))
                        p_rows.append(p.astype(bf16))
                    p_cols.append(jnp.concatenate(p_rows, axis=0))
                    ds_cols.append(jnp.concatenate(ds_rows, axis=0))
                p, ds = jnp.concatenate(p_cols, axis=1), jnp.concatenate(ds_cols, axis=1)
                dv_s[...] += lax.dot_general(p, do, NN, preferred_element_type=f32)
                dk_s[...] += lax.dot_general(ds, q, NN, preferred_element_type=f32)
                dq_s[at] += lax.dot_general(ds, k, TN, preferred_element_type=f32)
                return inner

            lax.fori_loop(0, cnt[g], step, 0)
            for j in range(keys_step):
                b = kid[g * keys_step + j]
                g_s[b, 0] = (dk_s[pl.ds(j * T, T)] * scale).astype(g_s.dtype)
                g_s[b, 1] = dv_s[pl.ds(j * T, T)].astype(g_s.dtype)
            return carry

        lax.fori_loop(0, groups, group, 0)
        gown_ref[...] = g_s[0:src]
        gpartner_ref[...] = g_s[src:n]
        if last:

            def finish(i, carry):
                at = pl.ds(pl.multiple_of(i * R, R), R)
                dq_ref[qid[i]] = (dq_s[at] * scale).astype(bf16).reshape(heads, T, D)
                return carry

            lax.fori_loop(0, src, finish, 0)

    smem = pl.BlockSpec(memory_space=pltpu.SMEM)
    vmem = pl.BlockSpec(memory_space=pltpu.VMEM)
    dq_f32 = jax.ShapeDtypeStruct((src * R, D), f32)
    dq_out = jax.ShapeDtypeStruct((src, heads, T, D), bf16) if last else dq_f32
    g_type = f32 if last else bf16
    g_out = jax.ShapeDtypeStruct((src, 2, T, D), g_type)
    scratch = [
        pltpu.VMEM((src * R, D), bf16),
        pltpu.VMEM((src * R, D), bf16),
        pltpu.VMEM((src, 8, R), f32),
        pltpu.VMEM((n, 2, T, D), bf16),
        pltpu.VMEM((n, 2, T, D), g_type),
        pltpu.VMEM((U, D), bf16),
        pltpu.VMEM((U, D), bf16),
        pltpu.VMEM((U, D), f32),
        pltpu.VMEM((U, D), f32),
    ]
    arrays = [packed, kv_own, kv_partner]
    if last:
        scratch.append(pltpu.VMEM((src * R, D), f32))
        arrays.append(dq_start)
    return pl.pallas_call(
        body,
        out_shape=(dq_out, g_out, g_out),
        in_specs=[smem] * 5 + [vmem] * len(arrays),
        out_specs=(vmem,) * 3,
        scratch_shapes=scratch,
        compiler_params=pltpu.CompilerParams(vmem_limit_bytes=48 * 2**20),
        cost_estimate=pl.CostEstimate(
            flops=10 * src * R * n * T * D, bytes_accessed=6 * 2**20, transcendentals=src * R * n * T
        ),
        name=name,
    )(*tables, *arrays)


def sort_down(order):
    ids = jnp.arange(order.shape[0], dtype=jnp.int32)
    rank = jnp.sum((order[None, :] > order[:, None]).astype(jnp.int32), axis=1)
    hit = rank[None, :] == ids[:, None]
    return (
        jnp.sum(jnp.where(hit, ids[None, :], 0), axis=1),
        jnp.sum(jnp.where(hit, order[None, :], 0), axis=1),
    )


def pieces(x):
    high = lax.reduce_precision(x, 8, 7)
    rest = x - high
    middle = lax.reduce_precision(rest, 8, 7)
    return [v.astype(bf16) for v in (high, middle, rest - middle)]


def shards(query, keys, values, attn_out, grad_out, log_norm, block_order):
    heads = lax.axis_size("head")
    inners = lax.axis_size("inner")
    outers = lax.axis_size("outer")
    T, q_heads, D = query.shape
    group = q_heads // keys.shape[1]
    i, o = lax.axis_index("inner"), lax.axis_index("outer")

    ring = ("inner", "outer")
    place = lambda a, b: a * outers + b
    swap = [(place(1 - a, b), place(a, b)) for a in range(inners) for b in range(outers)]
    ahead = [
        (place(a, b), place(a, b + 1) if b + 1 < outers else place(1 - a, 0))
        for a in range(inners)
        for b in range(outers)
    ]
    back = [(b, a) for a, b in ahead]

    def exchange(x):
        return lax.all_to_all(x, "head", split_axis=0, concat_axis=0, tiled=True)

    def by_head(x):
        return x.reshape(T, heads, -1, D).transpose(1, 2, 0, 3)

    kv = exchange(jnp.concatenate([by_head(keys), by_head(values)], axis=1))
    kv_partner = lax.ppermute(kv, ring, swap)
    kv_far = lax.ppermute(kv, ring, ahead)
    kv_far_partner = lax.ppermute(kv_partner, ring, ahead)

    delta = jnp.sum(grad_out.astype(f32) * attn_out.astype(f32), axis=-1)
    stats = jnp.stack([log_norm * LOG2E, delta])
    lanes = group * T // D
    stats = stats.reshape(2, T, heads, group).transpose(2, 0, 3, 1).reshape(heads, 2 * lanes, D)
    stats = jnp.pad(stats, ((0, 0), (0, 8 - 2 * lanes), (0, 0)))
    stats = jnp.concatenate(pieces(stats), axis=1)
    stats = jnp.pad(stats, ((0, 0), (0, T - 24), (0, 0)))
    packed = exchange(
        jnp.concatenate([by_head(query), by_head(grad_out), stats[:, None]], axis=1)
    )

    table = block_order.reshape(heads, inners, outers)

    def places(a, b):
        return lax.dynamic_slice(table, (0, a, b), (heads, 1, 1)).reshape(heads)

    keys_step, rows_step = 8, 2
    q_id, q_order = sort_down(places(i, o))
    before = (o - 1) % outers
    turn = jnp.where(o == 0, 1 - i, i)

    def tables(a, b):
        k_id, k_order = sort_down(jnp.concatenate([places(a, b), places(1 - a, b)]))
        least = k_order.reshape(-1, keys_step)[:, -1]
        seen = jnp.sum((q_order[None, :] >= least[:, None]).astype(jnp.int32), axis=1)
        return q_id, q_order, k_id, k_order, (seen + rows_step - 1) // rows_step

    dq, far, far_partner = attention_part(
        tables(turn, before), packed, kv_far, kv_far_partner, None, keys_step, rows_step, "far_keys"
    )
    far_partner = lax.ppermute(far_partner, ring, back)
    far = lax.ppermute(far, ring, back)
    dq, near, near_partner = attention_part(
        tables(i, o), packed, kv, kv_partner, dq, keys_step, rows_step, "near_keys"
    )
    dq = exchange(dq)
    partner = lax.ppermute((near_partner + far_partner.astype(f32)).astype(bf16), ring, swap)
    grad = exchange((near + far.astype(f32) + partner.astype(f32)).astype(bf16))
    grad = grad.transpose(1, 2, 0, 3)
    return dq.reshape(q_heads, T, D).transpose(1, 0, 2), grad[0], grad[1]


def solution(mesh):
    rows = P(("head", "inner", "outer"))
    return jax.shard_map(
        shards,
        mesh=mesh,
        in_specs=(rows,) * 6 + (P(),),
        out_specs=(rows,) * 3,
        check_vma=False,
    )
```

profile of v0, /device:TPU:102, one launch (start us, length us, event | category | flops | bytes accessed | tf_op | source)
XLA Modules:
  0.0 112.2 jit_solution(339918974711502089)
XLA Ops:
  0.7 1.1 %copy_bitcast_fusion.1 = (bf16[8,1,64,128]{3,2,1,0:T(8,128)(2,1)S(1)}, bf16[8,1,64,128]{3,2,1,0:T(8,128)(2,1)S(1)}) fusion(bf16[64,8,128]{2,1,0:T(8,128)(2,1)} %param.9, bf16[64,8,128]{2,1,0:T(8,128)(2,1)} %param.8), kind=kLoop, calls=%fused_computation.15 | loop fusion | bytes 524288 | tf_op jit(solution)/shard_map/transpose | solution.py:184
  1.8 0.7 pad_maximum_fusion.1
  2.5 4.5 %all-to-all-start.1 = ((bf16[8,2,64,128]{3,2,1,0:T(8,128)(2,1)}), bf16[8,2,64,128]{3,2,1,0:T(8,128)(2,1)S(1)}, u32[]{:S(2)}, u32[]{:S(2)}) async-start(bf16[8,2,64,128]{3,2,1,0:T(8,128)(2,1)} %pad_maximum_fusion.1), calls=%async_computation.1 | async-start | bytes 524288 | tf_op jit(solution)/shard_map/all_to_all | solution.py:181
  7.0 0.7 broadcast_multiply_fusion
  7.7 0.2 copy.44
  8.0 0.5 multiply_reduce_fusion
  8.7 0.2 copy-done.3
  8.9 0.2 copy.43
  9.1 1.4 %pad_maximum_fusion = bf16[8,13,64,128]{3,2,1,0:T(8,128)(2,1)} fusion(bf16[8,1,64,128]{3,2,1,0:T(8,128)(2,1)S(1)} %fusion.5, bf16[8,6,64,128]{3,2,1,0:T(8,128)(2,1)S(1)} %bitcast.32, bf16[8,6,64,128]{3,2,1,0:T(8,128)(2,1)S(1)} %bitcast.33), kind=kLoop, calls=%fused_computation | loop fusion | flops 1703936 | bytes 3407872 | tf_op jit(solution)/shard_map/concatenate | solution.py:199
  10.5 4.0 %all-to-all-done.1.own_ref = bf16[8,2,64,128]{3,2,1,0:T(8,128)(2,1)S(1)} async-done(((bf16[8,2,64,128]{3,2,1,0:T(8,128)(2,1)}), bf16[8,2,64,128]{3,2,1,0:T(8,128)(2,1)S(1)}, u32[]{:S(2)}, u32[]{:S(2)}) %all-to-all-start.1) | async-done | bytes 262176 | tf_op jit(solution)/shard_map/all_to_all | solution.py:181
  14.5 3.6 %all-to-all-start = ((bf16[8,13,64,128]{3,2,1,0:T(8,128)(2,1)}), bf16[8,13,64,128]{3,2,1,0:T(8,128)(2,1)S(1)}, u32[]{:S(2)}, u32[]{:S(2)}) async-start(bf16[8,13,64,128]{3,2,1,0:T(8,128)(2,1)} %pad_maximum_fusion), calls=%async_computation | async-start | bytes 3407872 | tf_op jit(solution)/shard_map/all_to_all | solution.py:181
  18.3 0.7 dynamic-slice_reduce_fusion.1
  19.1 0.2 convert_reduce_fusion
  20.1 4.6 %collective-permute-start = (bf16[8,2,64,128]{3,2,1,0:T(8,128)(2,1)S(1)}, bf16[8,2,64,128]{3,2,1,0:T(8,128)(2,1)S(1)}, u32[]{:S(2)}, u32[]{:S(2)}) collective-permute-start(bf16[8,2,64,128]{3,2,1,0:T(8,128)(2,1)S(1)} %all-to-all-done.1.own_ref), channel_id=1, source_target_pairs={{16,0},{17,1},{18,2},{19,3},{20,4},{21,5},{22,6},{23,7},{24,8},{25... | collective-permute-start | bytes 786440 | tf_op jit(solution)/shard_map/ppermute | solution.py:187
  25.3 9.4 %collective-permute-done.partner_ref = bf16[8,2,64,128]{3,2,1,0:T(8,128)(2,1)S(1)} collective-permute-done((bf16[8,2,64,128]{3,2,1,0:T(8,128)(2,1)S(1)}, bf16[8,2,64,128]{3,2,1,0:T(8,128)(2,1)S(1)}, u32[]{:S(2)}, u32[]{:S(2)}) %collective-permute-start) | collective-permute-done | bytes 262176 | tf_op jit(solution)/shard_map/ppermute | solution.py:187
  34.7 6.0 %collective-permute-start.2 = (bf16[8,2,64,128]{3,2,1,0:T(8,128)(2,1)S(1)}, bf16[8,2,64,128]{3,2,1,0:T(8,128)(2,1)S(1)}, u32[]{:S(2)}, u32[]{:S(2)}) collective-permute-start(bf16[8,2,64,128]{3,2,1,0:T(8,128)(2,1)S(1)} %collective-permute-done.partner_ref), channel_id=1, source_target_pairs={{0,1},{1,2},{2,3},{3,4},{4,5},{5,6},{6,7},{7,8},{8,9},{9,10},{10,1... | collective-permute-start | bytes 786440 | tf_op jit(solution)/shard_map/ppermute | solution.py:189
  40.7 0.2 fusion.8
  40.9 1.6 %collective-permute-done.1.own_ref = bf16[8,2,64,128]{3,2,1,0:T(8,128)(2,1)S(1)} collective-permute-done((bf16[8,2,64,128]{3,2,1,0:T(8,128)(2,1)S(1)}, bf16[8,2,64,128]{3,2,1,0:T(8,128)(2,1)S(1)}, u32[]{:S(2)}, u32[]{:S(2)}) %collective-permute-start.1) | collective-permute-done | bytes 262176 | tf_op jit(solution)/shard_map/ppermute | solution.py:188
  42.5 5.6 %collective-permute-done.2.partner_ref = bf16[8,2,64,128]{3,2,1,0:T(8,128)(2,1)S(1)} collective-permute-done((bf16[8,2,64,128]{3,2,1,0:T(8,128)(2,1)S(1)}, bf16[8,2,64,128]{3,2,1,0:T(8,128)(2,1)S(1)}, u32[]{:S(2)}, u32[]{:S(2)}) %collective-permute-start.2) | collective-permute-done | bytes 262176 | tf_op jit(solution)/shard_map/ppermute | solution.py:189
  48.1 10.9 %far_keys.1 = (f32[3072,128]{1,0:T(8,128)S(1)}, bf16[8,2,64,128]{3,2,1,0:T(8,128)(2,1)S(1)}, bf16[8,2,64,128]{3,2,1,0:T(8,128)(2,1)}) custom-call(s32[8]{0:T(128)S(1)} %get-tuple-element.41.qid, s32[8]{0:T(128)S(1)} %get-tuple-element.40.qord, s32[16]{0:T(128)S(1)} %get-tuple-element.37.kid, s32[16]{0:T(128)S(1)} %get-tuple-element.36.kord, ...), custom_call_target="tpu_custom_call" | custom-call | flops 4026531840 | bytes 6291456 | tf_op jit(solution)/shard_map/far_keys/pallas_call | solution.py:131
  59.0 0.7 copy-done
  59.7 10.0 %near_keys.1 = (bf16[8,6,64,128]{3,2,1,0:T(8,128)(2,1)}, f32[8,2,64,128]{3,2,1,0:T(8,128)S(1)}, f32[8,2,64,128]{3,2,1,0:T(8,128)S(1)}) custom-call(s32[8]{0:T(128)S(1)} %get-tuple-element.41.qid, s32[8]{0:T(128)S(1)} %get-tuple-element.40.qord, s32[16]{0:T(128)S(1)} %get-tuple-element.39.kid, s32[16]{0:T(128)S(1)} %get-tuple-element.38.kord, ...), custom_call_target="tpu_custom_call" | custom-call | flops 4026531840 | bytes 6291456 | tf_op jit(solution)/shard_map/near_keys/pallas_call | solution.py:131
  69.6 4.5 %all-to-all-start.2 = ((bf16[8,6,64,128]{3,2,1,0:T(8,128)(2,1)}), bf16[8,6,64,128]{3,2,1,0:T(8,128)(2,1)S(1)}, u32[]{:S(2)}, u32[]{:S(2)}) async-start(bf16[8,6,64,128]{3,2,1,0:T(8,128)(2,1)} %get-tuple-element.10), calls=%async_computation.2 | async-start | bytes 1572864 | tf_op jit(solution)/shard_map/all_to_all | solution.py:181
  74.1 1.0 add_convert_fusion.1
  75.1 1.7 %collective-permute-start.5 = (bf16[8,2,64,128]{3,2,1,0:T(8,128)(2,1)S(1)}, bf16[8,2,64,128]{3,2,1,0:T(8,128)(2,1)S(1)}, u32[]{:S(2)}, u32[]{:S(2)}) collective-permute-start(bf16[8,2,64,128]{3,2,1,0:T(8,128)(2,1)S(1)} %add_convert_fusion.1), channel_id=1, source_target_pairs={{16,0},{17,1},{18,2},{19,3},{20,4},{21,5},{22,6},{23,7},{24,8},{25... | collective-permute-start | bytes 786440 | tf_op jit(solution)/shard_map/ppermute | solution.py:227
  76.8 21.0 %collective-permute-done.3 = bf16[8,2,64,128]{3,2,1,0:T(8,128)(2,1)S(1)} collective-permute-done((bf16[8,2,64,128]{3,2,1,0:T(8,128)(2,1)}, bf16[8,2,64,128]{3,2,1,0:T(8,128)(2,1)S(1)}, u32[]{:S(2)}, u32[]{:S(2)}) %collective-permute-start.3) | collective-permute-done | bytes 262176 | tf_op jit(solution)/shard_map/ppermute | solution.py:222
  97.9 0.8 add_convert_fusion
  98.7 4.4 %all-to-all-start.3 = ((bf16[8,2,64,128]{3,2,1,0:T(8,128)(2,1)}), bf16[8,2,64,128]{3,2,1,0:T(8,128)(2,1)S(1)}, u32[]{:S(2)}, u32[]{:S(2)}) async-start(bf16[8,2,64,128]{3,2,1,0:T(8,128)(2,1)} %add_convert_fusion), calls=%async_computation.3 | async-start | bytes 524288 | tf_op jit(solution)/shard_map/all_to_all | solution.py:181
  103.1 1.4 %copy.55 = bf16[48,64,128]{2,0,1:T(8,128)(2,1)} copy(bf16[48,64,128]{2,1,0:T(8,128)(2,1)S(1)} %bitcast.31) | data formatting | bytes 1572864 | tf_op jit(solution)/shard_map/reshape | solution.py:230
  104.5 6.2 %all-to-all-done.3 = bf16[8,2,64,128]{3,2,1,0:T(8,128)(2,1)S(1)} async-done(((bf16[8,2,64,128]{3,2,1,0:T(8,128)(2,1)}), bf16[8,2,64,128]{3,2,1,0:T(8,128)(2,1)S(1)}, u32[]{:S(2)}, u32[]{:S(2)}) %all-to-all-start.3) | async-done | bytes 262176 | tf_op jit(solution)/shard_map/all_to_all | solution.py:181
  110.7 0.7 copy.51
  111.4 0.7 copy.50
  (37 shorter events, 1.9 us)
Async XLA Ops:
  0.6 7.1 %copy-start.1 = (bf16[64,48,128]{2,1,0:T(8,128)(2,1)S(1)}, bf16[64,48,128]{2,1,0:T(8,128)(2,1)}, u32[]{:S(2)}) copy-start(bf16[64,48,128]{2,1,0:T(8,128)(2,1)} %param.11) | copy-start | bytes 2359300
  0.6 7.3 %copy-start.2 = (bf16[64,48,128]{2,1,0:T(8,128)(2,1)S(1)}, bf16[64,48,128]{2,1,0:T(8,128)(2,1)}, u32[]{:S(2)}) copy-start(bf16[64,48,128]{2,1,0:T(8,128)(2,1)} %param.10) | copy-start | bytes 2359300
  2.5 12.0 %all-to-all-start.1 = ((bf16[8,2,64,128]{3,2,1,0:T(8,128)(2,1)}), bf16[8,2,64,128]{3,2,1,0:T(8,128)(2,1)S(1)}, u32[]{:S(2)}, u32[]{:S(2)}) async-start(bf16[8,2,64,128]{3,2,1,0:T(8,128)(2,1)} %pad_maximum_fusion.1), calls=%async_computation.1 | async-start | bytes 524288 | tf_op jit(solution)/shard_map/all_to_all | solution.py:181
  7.7 1.1 %copy-start.3 = (bf16[64,48,128]{2,1,0:T(8,128)(2,1)S(1)}, bf16[64,48,128]{2,1,0:T(8,128)(2,1)}, u32[]{:S(2)}) copy-start(bf16[64,48,128]{2,1,0:T(8,128)(2,1)} %param.7) | copy-start | bytes 2359300
  10.5 7.6 %copy-start.4 = (s32[256]{0:T(256)S(1)}, s32[256]{0:T(256)}, u32[]{:S(2)}) copy-start(s32[256]{0:T(256)} %param.13) | copy-start | bytes 3076
  14.5 33.6 %all-to-all-start = ((bf16[8,13,64,128]{3,2,1,0:T(8,128)(2,1)}), bf16[8,13,64,128]{3,2,1,0:T(8,128)(2,1)S(1)}, u32[]{:S(2)}, u32[]{:S(2)}) async-start(bf16[8,13,64,128]{3,2,1,0:T(8,128)(2,1)} %pad_maximum_fusion), calls=%async_computation | async-start | bytes 3407872 | tf_op jit(solution)/shard_map/all_to_all | solution.py:181
  20.1 14.6 %collective-permute-start = (bf16[8,2,64,128]{3,2,1,0:T(8,128)(2,1)S(1)}, bf16[8,2,64,128]{3,2,1,0:T(8,128)(2,1)S(1)}, u32[]{:S(2)}, u32[]{:S(2)}) collective-permute-start(bf16[8,2,64,128]{3,2,1,0:T(8,128)(2,1)S(1)} %all-to-all-done.1.own_ref), channel_id=1, source_target_pairs={{16,0},{17,1},{18,2},{19,3},{20,4},{21,5},{22,6},{23,7},{24,8},{25... | collective-permute-start | bytes 786440 | tf_op jit(solution)/shard_map/ppermute | solution.py:187
  25.2 17.3 %collective-permute-start.1 = (bf16[8,2,64,128]{3,2,1,0:T(8,128)(2,1)S(1)}, bf16[8,2,64,128]{3,2,1,0:T(8,128)(2,1)S(1)}, u32[]{:S(2)}, u32[]{:S(2)}) collective-permute-start(bf16[8,2,64,128]{3,2,1,0:T(8,128)(2,1)S(1)} %all-to-all-done.1.own_ref), channel_id=1, source_target_pairs={{0,1},{1,2},{2,3},{3,4},{4,5},{5,6},{6,7},{7,8},{8,9},{9,10},{10,1... | collective-permute-start | bytes 786440 | tf_op jit(solution)/shard_map/ppermute | solution.py:188
  34.7 13.4 %collective-permute-start.2 = (bf16[8,2,64,128]{3,2,1,0:T(8,128)(2,1)S(1)}, bf16[8,2,64,128]{3,2,1,0:T(8,128)(2,1)S(1)}, u32[]{:S(2)}, u32[]{:S(2)}) collective-permute-start(bf16[8,2,64,128]{3,2,1,0:T(8,128)(2,1)S(1)} %collective-permute-done.partner_ref), channel_id=1, source_target_pairs={{0,1},{1,2},{2,3},{3,4},{4,5},{5,6},{6,7},{7,8},{8,9},{9,10},{10,1... | collective-permute-start | bytes 786440 | tf_op jit(solution)/shard_map/ppermute | solution.py:189
  59.0 0.7 copy-start
  59.7 14.4 %collective-permute-start.4 = (bf16[8,2,64,128]{3,2,1,0:T(8,128)(2,1)}, bf16[8,2,64,128]{3,2,1,0:T(8,128)(2,1)}, u32[]{:S(2)}, u32[]{:S(2)}) collective-permute-start(bf16[8,2,64,128]{3,2,1,0:T(8,128)(2,1)} %get-tuple-element.14), channel_id=1, source_target_pairs={{1,0},{2,1},{3,2},{4,3},{5,4},{6,5},{7,6},{8,7},{9,8},{10,9},{11,1... | collective-permute-start | bytes 786440 | tf_op jit(solution)/shard_map/ppermute | solution.py:221
  69.6 29.0 %all-to-all-start.2 = ((bf16[8,6,64,128]{3,2,1,0:T(8,128)(2,1)}), bf16[8,6,64,128]{3,2,1,0:T(8,128)(2,1)S(1)}, u32[]{:S(2)}, u32[]{:S(2)}) async-start(bf16[8,6,64,128]{3,2,1,0:T(8,128)(2,1)} %get-tuple-element.10), calls=%async_computation.2 | async-start | bytes 1572864 | tf_op jit(solution)/shard_map/all_to_all | solution.py:181
  74.1 23.8 %collective-permute-start.3 = (bf16[8,2,64,128]{3,2,1,0:T(8,128)(2,1)}, bf16[8,2,64,128]{3,2,1,0:T(8,128)(2,1)S(1)}, u32[]{:S(2)}, u32[]{:S(2)}) collective-permute-start(bf16[8,2,64,128]{3,2,1,0:T(8,128)(2,1)} %copy-done), channel_id=1, source_target_pairs={{1,0},{2,1},{3,2},{4,3},{5,4},{6,5},{7,6},{8,7},{9,8},{10,9},{11,1... | collective-permute-start | bytes 786440 | tf_op jit(solution)/shard_map/ppermute | solution.py:222
  75.1 22.7 %collective-permute-start.5 = (bf16[8,2,64,128]{3,2,1,0:T(8,128)(2,1)S(1)}, bf16[8,2,64,128]{3,2,1,0:T(8,128)(2,1)S(1)}, u32[]{:S(2)}, u32[]{:S(2)}) collective-permute-start(bf16[8,2,64,128]{3,2,1,0:T(8,128)(2,1)S(1)} %add_convert_fusion.1), channel_id=1, source_target_pairs={{16,0},{17,1},{18,2},{19,3},{20,4},{21,5},{22,6},{23,7},{24,8},{25... | collective-permute-start | bytes 786440 | tf_op jit(solution)/shard_map/ppermute | solution.py:227
  98.7 12.0 %all-to-all-start.3 = ((bf16[8,2,64,128]{3,2,1,0:T(8,128)(2,1)}), bf16[8,2,64,128]{3,2,1,0:T(8,128)(2,1)S(1)}, u32[]{:S(2)}, u32[]{:S(2)}) async-start(bf16[8,2,64,128]{3,2,1,0:T(8,128)(2,1)} %add_convert_fusion), calls=%async_computation.3 | async-start | bytes 524288 | tf_op jit(solution)/shard_map/all_to_all | solution.py:181
where the time goes:
time: 114 us; the launch traced here: 112 us
  waiting for transfers between devices  47.8 us (42%)
  starting transfers between devices  29.3 us (26%)
  Pallas kernels  20.8 us (18%)
  local copies, waits for them, and re-layouts  6.86 us (6%)
  other arithmetic  6.54 us (6%)
    ppermute x1, waiting for transfers between devices, shards(): far = lax.ppermute(far, ring, back)  21 us
    pallas_call x2, Pallas kernels, attention_part(): pl.pallas_call(body, out_shape=(dq_out, g_out, g_out), in_specs=[smem] *...  20.8 us
    all_to_all x4, starting transfers between devices, exchange(): return lax.all_to_all(x, 'head', split_axis=0, concat_axis=0, tiled=True)  17 us
    all_to_all x4, waiting for transfers between devices, exchange(): return lax.all_to_all(x, 'head', split_axis=0, concat_axis=0, tiled=True)  10.2 us
    ppermute x1, waiting for transfers between devices, shards(): kv_partner = lax.ppermute(kv, ring, swap)  9.41 us
    ppermute x1, starting transfers between devices, shards(): kv_far_partner = lax.ppermute(kv_partner, ring, ahead)  5.97 us
    ppermute x1, waiting for transfers between devices, shards(): kv_far_partner = lax.ppermute(kv_partner, ring, ahead)  5.58 us
    ppermute x1, starting transfers between devices, shards(): kv_partner = lax.ppermute(kv, ring, swap)  4.59 us
  transfers between devices with their start and end apart: 10, of which 6 were waited for; matrix products, arithmetic and copies ran while one was open for 8% of the time, Pallas kernels for 9%

commit v1 on v0

v1 whole, which is shorter than its diff:
```python
import math

import jax
import jax.numpy as jnp
from jax import lax
from jax.experimental import pallas as pl
from jax.experimental.pallas import tpu as pltpu
from jax.sharding import PartitionSpec as P

LOG2E = math.log2(math.e)
NT = (((1,), (1,)), ((), ()))
NN = (((1,), (0,)), ((), ()))
f32 = jnp.float32
bf16 = jnp.bfloat16


def attention_part(tables, packed, contexts, dq_start, last, keys_step, rows_step, g_types, name):
    src, parts, T, D = packed.shape
    heads = (parts - 1) // 2
    R = heads * T
    many = len(contexts)
    n = many * src
    U, W = keys_step * T, rows_step * R
    groups = n // keys_step
    scale = D ** (-0.5)
    lanes = R // D
    first = dq_start is None

    def body(qid, qord, kid, kord, cnt, packed_ref, *rest):
        kv_refs, rest = rest[:many], rest[many:]
        if not first:
            start_ref, *rest = rest
        out_ref, *rest = rest
        g_refs, rest = rest[:many], rest[many:]
        if many > 1:
            kv_s, g_s, *rest = rest
            for c in range(many):
                kv_s[c * src : (c + 1) * src] = kv_refs[c][...]
        else:
            kv_s, g_s = kv_refs[0], g_refs[0]
        st_s, k_s, v_s, kt_s, dk_s, dv_s, *rest = rest
        dq_s = rest[0] if last else out_ref
        dq_s[...] = jnp.zeros_like(dq_s) if first else start_ref[...]

        def prepare(i, carry):
            st = packed_ref[qid[i], 2 * heads].astype(f32)
            st = st[0:8] + st[8:16] + st[16:24]
            st_s[i, 0:1] = jnp.concatenate([st[j : j + 1] for j in range(lanes)], axis=1)
            st_s[i, 1:2] = jnp.concatenate([st[j : j + 1] for j in range(lanes, 2 * lanes)], axis=1)
            return carry

        lax.fori_loop(0, src, prepare, 0)
        lead = lax.broadcasted_iota(jnp.int32, (T, R), 1) % T - lax.broadcasted_iota(
            jnp.int32, (T, R), 0
        )

        def group(g, carry):
            for j in range(keys_step):
                b = kid[g * keys_step + j]
                k_s[pl.ds(j * T, T)] = kv_s[b, 0]
                v_s[pl.ds(j * T, T)] = kv_s[b, 1]
            kt_s[...] = k_s[...].T
            dk_s[...] = jnp.zeros_like(dk_s)
            dv_s[...] = jnp.zeros_like(dv_s)

            def step(i, inner):
                at = pl.ds(pl.multiple_of(i * W, W), W)
                ids = [qid[i * rows_step + h] for h in range(rows_step)]
                q = jnp.concatenate([packed_ref[b, 0:heads].reshape(R, D) for b in ids], axis=0)
                do = jnp.concatenate(
                    [packed_ref[b, heads : 2 * heads].reshape(R, D) for b in ids], axis=0
                )
                k, v = k_s[...], v_s[...]
                s = lax.dot_general(k, q, NT, preferred_element_type=f32)
                dp = lax.dot_general(v, do, NT, preferred_element_type=f32)
                p_cols, ds_cols = [], []
                for h in range(rows_step):
                    row = i * rows_step + h
                    lse, delta, place = st_s[row, 0:1], st_s[row, 1:2], qord[row]
                    p_rows, ds_rows = [], []
                    for j in range(keys_step):
                        behind = (kord[g * keys_step + j] - place) * T
                        cut = (slice(j * T, (j + 1) * T), slice(h * R, (h + 1) * R))
                        p = jnp.where(
                            lead >= behind, jnp.exp2(s[cut] * (scale * LOG2E) - lse), 0.0
                        )
                        ds_rows.append((p * (dp[cut] - delta)).astype(bf16))
                        p_rows.append(p.astype(bf16))
                    p_cols.append(jnp.concatenate(p_rows, axis=0))
                    ds_cols.append(jnp.concatenate(ds_rows, axis=0))
                p, ds = jnp.concatenate(p_cols, axis=1), jnp.concatenate(ds_cols, axis=1)
                dv_s[...] += lax.dot_general(p, do, NN, preferred_element_type=f32)
                dk_s[...] += lax.dot_general(ds, q, NN, preferred_element_type=f32)
                dq_s[:, at] += lax.dot_general(kt_s[...], ds, NN, preferred_element_type=f32)
                return inner

            lax.fori_loop(0, cnt[g], step, 0)
            for j in range(keys_step):
                b = kid[g * keys_step + j]
                g_s[b, 0] = (dk_s[pl.ds(j * T, T)] * scale).astype(g_s.dtype)
                g_s[b, 1] = dv_s[pl.ds(j * T, T)].astype(g_s.dtype)
            return carry

        lax.fori_loop(0, groups, group, 0)
        if many > 1:
            for c in range(many):
                g_refs[c][...] = g_s[c * src : (c + 1) * src].astype(g_refs[c].dtype)
        if last:
            for j in range(src):
                at = pl.ds(j * R, R)
                out_ref[qid[j]] = (dq_s[:, at].T * scale).astype(bf16).reshape(heads, T, D)

    smem = pl.BlockSpec(memory_space=pltpu.SMEM)
    vmem = pl.BlockSpec(memory_space=pltpu.VMEM)
    if last:
        dq_out = jax.ShapeDtypeStruct((src, heads, T, D), bf16)
    else:
        dq_out = jax.ShapeDtypeStruct((D, src * R), f32)
    g_outs = [jax.ShapeDtypeStruct((src, 2, T, D), t) for t in g_types]
    scratch = []
    if many > 1:
        scratch = [pltpu.VMEM((n, 2, T, D), bf16), pltpu.VMEM((n, 2, T, D), f32)]
    scratch += [
        pltpu.VMEM((src, 8, R), f32),
        pltpu.VMEM((U, D), bf16),
        pltpu.VMEM((U, D), bf16),
        pltpu.VMEM((D, U), bf16),
        pltpu.VMEM((U, D), f32),
        pltpu.VMEM((U, D), f32),
    ]
    if last:
        scratch.append(pltpu.VMEM((D, src * R), f32))
    arrays = [packed, *contexts] + ([] if first else [dq_start])
    return pl.pallas_call(
        body,
        out_shape=(dq_out, *g_outs),
        in_specs=[smem] * 5 + [vmem] * len(arrays),
        out_specs=(vmem,) * (1 + many),
        scratch_shapes=scratch,
        compiler_params=pltpu.CompilerParams(vmem_limit_bytes=32 * 2**20),
        cost_estimate=pl.CostEstimate(flops=1, bytes_accessed=1, transcendentals=0),
        name=name,
    )(*tables, *arrays)


def add_by_peer(me, *arrays):
    src, *rest = arrays[0].shape

    def body(me_ref, *refs):
        ins, outs = refs[: len(arrays)], refs[len(arrays) :]
        for j in range(src):
            at = me_ref[0] ^ j
            outs[j][...] = sum(r[at].astype(f32) for r in ins).astype(bf16)

    smem = pl.BlockSpec(memory_space=pltpu.SMEM)
    vmem = pl.BlockSpec(memory_space=pltpu.VMEM)
    return pl.pallas_call(
        body,
        out_shape=[jax.ShapeDtypeStruct(rest, bf16)] * src,
        in_specs=[smem] + [vmem] * len(arrays),
        out_specs=[vmem] * src,
        cost_estimate=pl.CostEstimate(flops=10**10, bytes_accessed=1, transcendentals=0),
        name="add_by_peer",
    )(me.reshape(1), *arrays)


def gather_grads(me, pieces):
    src = len(pieces)
    _, T, D = pieces[0].shape

    def body(me_ref, *refs):
        ins, outs, held, wide = refs[:src], refs[src : src + 2], refs[-2], refs[-1]
        for j in range(src):
            held[me_ref[0] ^ j] = ins[j][...]
        for c in range(2):
            for g in range(src):
                wide[:, g, :] = held[g, c].astype(f32)
            outs[c][...] = wide[...].astype(bf16)

    smem = pl.BlockSpec(memory_space=pltpu.SMEM)
    vmem = pl.BlockSpec(memory_space=pltpu.VMEM)
    return pl.pallas_call(
        body,
        out_shape=[jax.ShapeDtypeStruct((T, src, D), bf16)] * 2,
        in_specs=[smem] + [vmem] * src,
        out_specs=[vmem] * 2,
        scratch_shapes=[pltpu.VMEM((src, 2, T, D), bf16), pltpu.VMEM((T, src, D), f32)],
        name="gather_grads",
    )(me.reshape(1), *pieces)


def sort_down(order):
    ids = jnp.arange(order.shape[0], dtype=jnp.int32)
    rank = jnp.sum((order[None, :] > order[:, None]).astype(jnp.int32), axis=1)
    hit = rank[None, :] == ids[:, None]
    return (
        jnp.sum(jnp.where(hit, ids[None, :], 0), axis=1),
        jnp.sum(jnp.where(hit, order[None, :], 0), axis=1),
    )


def pieces(x):
    high = lax.reduce_precision(x, 8, 7)
    rest = x - high
    middle = lax.reduce_precision(rest, 8, 7)
    return [v.astype(bf16) for v in (high, middle, rest - middle)]


def shards(query, keys, values, attn_out, grad_out, log_norm, block_order):
    heads = lax.axis_size("head")
    inners = lax.axis_size("inner")
    outers = lax.axis_size("outer")
    T, q_heads, D = query.shape
    group = q_heads // keys.shape[1]
    i, o = lax.axis_index("inner"), lax.axis_index("outer")

    ring = ("inner", "outer")
    place = lambda a, b: a * outers + b
    swap = [(place(1 - a, b), place(a, b)) for a in range(inners) for b in range(outers)]
    ahead = [
        (place(a, b), place(a, b + 1) if b + 1 < outers else place(1 - a, 0))
        for a in range(inners)
        for b in range(outers)
    ]
    back = [(b, a) for a, b in ahead]

    def exchange(x):
        return lax.all_to_all(x, "head", split_axis=0, concat_axis=0, tiled=True)

    def by_head(x):
        return x.reshape(T, heads, -1, D).transpose(1, 2, 0, 3)

    kv = exchange(jnp.concatenate([by_head(keys), by_head(values)], axis=1))
    kv_partner = lax.ppermute(kv, ring, swap)
    kv_far = lax.ppermute(kv, ring, ahead)
    kv_far_partner = lax.ppermute(kv_partner, ring, ahead)

    delta = jnp.sum(grad_out.astype(f32) * attn_out.astype(f32), axis=-1)
    stats = jnp.stack([log_norm * LOG2E, delta])
    lanes = group * T // D
    stats = stats.reshape(2, T, heads, group).transpose(2, 0, 3, 1).reshape(heads, 2 * lanes, D)
    stats = jnp.pad(stats, ((0, 0), (0, 8 - 2 * lanes), (0, 0)))
    stats = jnp.concatenate(pieces(stats), axis=1)
    stats = jnp.pad(stats, ((0, 0), (0, T - 24), (0, 0)))

    table = block_order.reshape(heads, inners, outers)

    def places(a, b):
        return lax.dynamic_slice(table, (0, a, b), (heads, 1, 1)).reshape(heads)

    keys_step, rows_step = 4, 2
    q_id, q_order = sort_down(places(i, o))
    me = lax.axis_index("head")
    before = (o - 1) % outers
    turn = jnp.where(o == 0, 1 - i, i)

    def order_of(*spots):
        k_id, k_order = sort_down(jnp.concatenate([places(a, b) for a, b in spots]))
        least = k_order.reshape(-1, keys_step * len(spots))[:, -1]
        seen = jnp.sum((q_order[None, :] >= least[:, None]).astype(jnp.int32), axis=1)
        return q_id, q_order, k_id, k_order, (seen + rows_step - 1) // rows_step

    tables = {
        "near": order_of((i, o)),
        "far_partner": order_of((1 - turn, before)),
        "others": order_of((1 - i, o), (turn, before)),
    }
    stats, tables = lax.optimization_barrier((stats, tables))
    packed = exchange(
        jnp.concatenate([by_head(query), by_head(grad_out), stats[:, None]], axis=1)
    )

    def part(name, contexts, dq, last, g_types):
        return attention_part(
            tables[name], packed, contexts, dq, last, keys_step * len(contexts), rows_step, g_types, name
        )

    def to_peers(blocks):
        return [blocks[0]] + [
            lax.ppermute(blocks[j], "head", [(h, h ^ j) for h in range(heads)])
            for j in range(1, heads)
        ]

    dq, near = part("near", [kv], None, False, [f32])
    dq, far_partner = part("far_partner", [kv_far_partner], dq, False, [bf16])
    far_partner = lax.ppermute(far_partner, ring, back)
    dq, near_partner, far = part("others", [kv_partner, kv_far], dq, True, [f32, bf16])
    partner = (near_partner + far_partner.astype(f32)).astype(bf16)
    partner, far = lax.optimization_barrier((partner, far))
    partner = lax.ppermute(partner, ring, swap)
    far = lax.ppermute(far, ring, back)
    dq = exchange(dq)
    grad = to_peers(add_by_peer(me, near, far, partner))
    dq = dq.reshape(q_heads, T, D).transpose(1, 0, 2)
    dq, grad = lax.optimization_barrier((dq, grad))
    return dq, *gather_grads(me, grad)


def solution(mesh):
    rows = P(("head", "inner", "outer"))
    return jax.shard_map(
        shards,
        mesh=mesh,
        in_specs=(rows,) * 6 + (P(),),
        out_specs=(rows,) * 3,
        check_vma=False,
    )
```

time: 114 us -> 107 us (0.939)
  the two profiles are of different devices: /device:TPU:102 before, /device:TPU:32 now
where the time goes in v1:
time: 107 us; the launch traced here: 106 us
  starting transfers between devices  38.7 us (36%)
  waiting for transfers between devices  31 us (29%)
  Pallas kernels  23.6 us (22%)
  local copies, waits for them, and re-layouts  7.64 us (7%)
  other arithmetic  4.04 us (4%)
    pallas_call x3, Pallas kernels, attention_part(): pl.pallas_call(body, out_shape=(dq_out, *g_outs), in_specs=[smem] * 5 + [...  19.8 us
    ppermute x1, waiting for transfers between devices, shards(): partner = lax.ppermute(partner, ring, swap)  13.4 us
    ppermute x1, waiting for transfers between devices, shards(): kv_partner = lax.ppermute(kv, ring, swap)  12.6 us
    all_to_all x3, starting transfers between devices, exchange(): return lax.all_to_all(x, 'head', split_axis=0, concat_axis=0, tiled=True)  11.7 us
    ppermute x1, starting transfers between devices, shards(): partner = lax.ppermute(partner, ring, swap)  8.33 us
    ppermute x7, starting transfers between devices, to_peers(): lax.ppermute(blocks[j], 'head', [(h, h ^ j) for h in range(heads)])  8.08 us
    ppermute x1, starting transfers between devices, shards(): kv_partner = lax.ppermute(kv, ring, swap)  6.33 us
    unnamed x30, local copies, waits for them, and re-layouts  2.65 us
  transfers between devices with their start and end apart: 16, of which 7 were waited for; matrix products, arithmetic and copies ran while one was open for 7% of the time, Pallas kernels for 21%

profile of v1, /device:TPU:32, one launch (start us, length us, event | category | flops | bytes accessed | tf_op | source)
XLA Modules:
  0.0 105.9 jit_solution(9955247714613089980)
XLA Ops:
  0.7 1.1 %copy_bitcast_fusion.1 = (bf16[8,1,64,128]{3,2,1,0:T(8,128)(2,1)S(1)}, bf16[8,1,64,128]{3,2,1,0:T(8,128)(2,1)S(1)}) fusion(bf16[64,8,128]{2,1,0:T(8,128)(2,1)} %param.9, bf16[64,8,128]{2,1,0:T(8,128)(2,1)} %param.8), kind=kLoop, calls=%fused_computation.11 | loop fusion | bytes 524288 | tf_op jit(solution)/shard_map/transpose | solution.py:231
  1.8 0.7 pad_maximum_fusion.1
  2.5 4.5 %all-to-all-start.1 = ((bf16[8,2,64,128]{3,2,1,0:T(8,128)(2,1)}), bf16[8,2,64,128]{3,2,1,0:T(8,128)(2,1)S(1)}, u32[]{:S(2)}, u32[]{:S(2)}) async-start(bf16[8,2,64,128]{3,2,1,0:T(8,128)(2,1)} %pad_maximum_fusion.1), calls=%async_computation.1 | async-start | bytes 524288 | tf_op jit(solution)/shard_map/all_to_all | solution.py:228
  7.0 0.8 reshape.62
  7.8 0.7 dynamic-slice_reduce_fusion.1
  12.0 1.4 %pad_maximum_fusion = bf16[8,13,64,128]{3,2,1,0:T(8,128)(2,1)} fusion(bf16[8,1,64,128]{3,2,1,0:T(8,128)(2,1)S(1)} %bitcast.30, bf16[8,6,64,128]{3,2,1,0:T(8,128)(2,1)S(1)} %bitcast.27, bf16[8,6,64,128]{3,2,1,0:T(8,128)(2,1)S(1)} %bitcast.28), kind=kLoop, calls=%fused_computation | loop fusion | flops 1703936 | bytes 3407872 | tf_op jit(solution)/shard_map/concatenate | solution.py:270
  13.4 1.1 %all-to-all-done.1.rest_0_ = bf16[8,2,64,128]{3,2,1,0:T(8,128)(2,1)S(1)} async-done(((bf16[8,2,64,128]{3,2,1,0:T(8,128)(2,1)}), bf16[8,2,64,128]{3,2,1,0:T(8,128)(2,1)S(1)}, u32[]{:S(2)}, u32[]{:S(2)}) %all-to-all-start.1) | async-done | bytes 262176 | tf_op jit(solution)/shard_map/all_to_all | solution.py:228
  14.5 3.7 %all-to-all-start = ((bf16[8,13,64,128]{3,2,1,0:T(8,128)(2,1)}), bf16[8,13,64,128]{3,2,1,0:T(8,128)(2,1)S(1)}, u32[]{:S(2)}, u32[]{:S(2)}) async-start(bf16[8,13,64,128]{3,2,1,0:T(8,128)(2,1)} %pad_maximum_fusion), calls=%async_computation | async-start | bytes 3407872 | tf_op jit(solution)/shard_map/all_to_all | solution.py:228
  18.2 6.3 %collective-permute-start = (bf16[8,2,64,128]{3,2,1,0:T(8,128)(2,1)S(1)}, bf16[8,2,64,128]{3,2,1,0:T(8,128)(2,1)S(1)}, u32[]{:S(2)}, u32[]{:S(2)}) collective-permute-start(bf16[8,2,64,128]{3,2,1,0:T(8,128)(2,1)S(1)} %all-to-all-done.1.rest_0_), channel_id=1, source_target_pairs={{16,0},{17,1},{18,2},{19,3},{20,4},{21,5},{22,6},{23,7},{24,8},{25... | collective-permute-start | bytes 786440 | tf_op jit(solution)/shard_map/ppermute | solution.py:234
  24.6 12.6 %collective-permute-done.rest_0_ = bf16[8,2,64,128]{3,2,1,0:T(8,128)(2,1)S(1)} collective-permute-done((bf16[8,2,64,128]{3,2,1,0:T(8,128)(2,1)S(1)}, bf16[8,2,64,128]{3,2,1,0:T(8,128)(2,1)S(1)}, u32[]{:S(2)}, u32[]{:S(2)}) %collective-permute-start) | collective-permute-done | bytes 262176 | tf_op jit(solution)/shard_map/ppermute | solution.py:234
  37.2 1.5 %collective-permute-start.2 = (bf16[8,2,64,128]{3,2,1,0:T(8,128)(2,1)S(1)}, bf16[8,2,64,128]{3,2,1,0:T(8,128)(2,1)S(1)}, u32[]{:S(2)}, u32[]{:S(2)}) collective-permute-start(bf16[8,2,64,128]{3,2,1,0:T(8,128)(2,1)S(1)} %collective-permute-done.rest_0_), channel_id=1, source_target_pairs={{0,1},{1,2},{2,3},{3,4},{4,5},{5,6},{6,7},{7,8},{8,9},{9,10},{10,1... | collective-permute-start | bytes 786440 | tf_op jit(solution)/shard_map/ppermute | solution.py:236
  38.7 1.5 %collective-permute-start.1 = (bf16[8,2,64,128]{3,2,1,0:T(8,128)(2,1)S(1)}, bf16[8,2,64,128]{3,2,1,0:T(8,128)(2,1)S(1)}, u32[]{:S(2)}, u32[]{:S(2)}) collective-permute-start(bf16[8,2,64,128]{3,2,1,0:T(8,128)(2,1)S(1)} %all-to-all-done.1.rest_0_), channel_id=1, source_target_pairs={{0,1},{1,2},{2,3},{3,4},{4,5},{5,6},{6,7},{7,8},{8,9},{9,10},{10,1... | collective-permute-start | bytes 786440 | tf_op jit(solution)/shard_map/ppermute | solution.py:235
  40.2 1.0 all-to-all-done.packed_ref
  41.2 5.1 %near.1 = (f32[128,3072]{1,0:T(8,128)S(1)}, f32[8,2,64,128]{3,2,1,0:T(8,128)S(1)}) custom-call(s32[8]{0:T(128)S(1)} %get-tuple-element.60.qid.kid, s32[8]{0:T(128)S(1)} %get-tuple-element.61.qord.kord, s32[8]{0:T(128)S(1)} %get-tuple-element.60.qid.kid, s32[8]{0:T(128)S(1)} %get-tuple-element.61.qord.kord, s32[2]{0:T(128)S(1)} %get-tuple-element.62.cnt, ...), custom_call_target="tpu_custom_call" | custom-call | flops 1 | bytes 1 | tf_op jit(solution)/shard_map/near/pallas_call | solution.py:134
  46.4 0.8 copy-done
  47.2 1.4 %collective-permute-done.2.rest_0_ = bf16[8,2,64,128]{3,2,1,0:T(8,128)(2,1)S(1)} collective-permute-done((bf16[8,2,64,128]{3,2,1,0:T(8,128)(2,1)S(1)}, bf16[8,2,64,128]{3,2,1,0:T(8,128)(2,1)S(1)}, u32[]{:S(2)}, u32[]{:S(2)}) %collective-permute-start.2) | collective-permute-done | bytes 262176 | tf_op jit(solution)/shard_map/ppermute | solution.py:236
  48.5 5.1 %far_partner.1 = (f32[128,3072]{1,0:T(8,128)S(1)}, bf16[8,2,64,128]{3,2,1,0:T(8,128)(2,1)S(1)}) custom-call(s32[8]{0:T(128)S(1)} %get-tuple-element.60.qid.kid, s32[8]{0:T(128)S(1)} %get-tuple-element.61.qord.kord, s32[8]{0:T(128)S(1)} %get-tuple-element.55.kid, s32[8]{0:T(128)S(1)} %get-tuple-element.56.kord, s32[2]{0:T(128)S(1)} %and_select_fusion.2.cnt, ...), custom_call_target="tpu_custom_call" | custom-call | flops 1 | bytes 1 | tf_op jit(solution)/shard_map/far_partner/pallas_call | solution.py:134
  53.7 9.5 %others.1 = (bf16[8,6,64,128]{3,2,1,0:T(8,128)(2,1)}, f32[8,2,64,128]{3,2,1,0:T(8,128)S(1)}, bf16[8,2,64,128]{3,2,1,0:T(8,128)(2,1)S(1)}) custom-call(s32[8]{0:T(128)S(1)} %get-tuple-element.60.qid.kid, s32[8]{0:T(128)S(1)} %get-tuple-element.61.qord.kord, s32[16]{0:T(128)S(1)} %get-tuple-element.49.kid, s32[16]{0:T(128)S(1)} %get-tuple-element.50.kord, ...), custom_call_target="tpu_custom_call" | custom-call | flops 1 | bytes 1 | tf_op jit(solution)/shard_map/others/pallas_call | solution.py:134
  63.4 1.1 %collective-permute-start.4 = (bf16[8,2,64,128]{3,2,1,0:T(8,128)(2,1)S(1)}, bf16[8,2,64,128]{3,2,1,0:T(8,128)(2,1)S(1)}, u32[]{:S(2)}, u32[]{:S(2)}) collective-permute-start(bf16[8,2,64,128]{3,2,1,0:T(8,128)(2,1)S(1)} %get-tuple-element.70), channel_id=1, source_target_pairs={{1,0},{2,1},{3,2},{4,3},{5,4},{6,5},{7,6},{8,7},{9,8},{10,9},{11,1... | collective-permute-start | bytes 786440 | tf_op jit(solution)/shard_map/ppermute | solution.py:291
  64.5 8.3 %collective-permute-start.5 = (bf16[8,2,64,128]{3,2,1,0:T(8,128)(2,1)S(1)}, bf16[8,2,64,128]{3,2,1,0:T(8,128)(2,1)S(1)}, u32[]{:S(2)}, u32[]{:S(2)}) collective-permute-start(bf16[8,2,64,128]{3,2,1,0:T(8,128)(2,1)S(1)} %add_convert_fusion), channel_id=1, source_target_pairs={{16,0},{17,1},{18,2},{19,3},{20,4},{21,5},{22,6},{23,7},{24,8},{25... | collective-permute-start | bytes 786440 | tf_op jit(solution)/shard_map/ppermute | solution.py:290
  72.8 3.5 %all-to-all-start.2 = ((bf16[8,6,64,128]{3,2,1,0:T(8,128)(2,1)}), bf16[8,6,64,128]{3,2,1,0:T(8,128)(2,1)S(1)}, u32[]{:S(2)}, u32[]{:S(2)}) async-start(bf16[8,6,64,128]{3,2,1,0:T(8,128)(2,1)} %get-tuple-element.65), calls=%async_computation.2 | async-start | bytes 1572864 | tf_op jit(solution)/shard_map/all_to_all | solution.py:228
  76.4 13.4 %collective-permute-done.5.refs_2_ = bf16[8,2,64,128]{3,2,1,0:T(8,128)(2,1)S(1)} collective-permute-done((bf16[8,2,64,128]{3,2,1,0:T(8,128)(2,1)S(1)}, bf16[8,2,64,128]{3,2,1,0:T(8,128)(2,1)S(1)}, u32[]{:S(2)}, u32[]{:S(2)}) %collective-permute-start.5) | collective-permute-done | bytes 262176 | tf_op jit(solution)/shard_map/ppermute | solution.py:290
  89.8 0.7 copy-done.13
  90.5 1.9 %add_by_peer.1 = (bf16[2,64,128]{2,1,0:T(8,128)(2,1)}, bf16[2,64,128]{2,1,0:T(8,128)(2,1)}, bf16[2,64,128]{2,1,0:T(8,128)(2,1)}, bf16[2,64,128]{2,1,0:T(8,128)(2...) custom-call(s32[1]{0:T(128)} %bitcast.12.me_ref, ...), custom_call_target="tpu_custom_call" | custom-call | flops 10000000000 | bytes 1 | tf_op jit(solution)/shard_map/add_by_peer/pallas_call | solution.py:157
  93.1 1.2 %collective-permute-start.8 = (bf16[2,64,128]{2,1,0:T(8,128)(2,1)}, bf16[2,64,128]{2,1,0:T(8,128)(2,1)S(1)}, u32[]{:S(2)}, u32[]{:S(2)}) collective-permute-start(bf16[2,64,128]{2,1,0:T(8,128)(2,1)} %get-tuple-element.75), channel_id=1, source_target_pairs={{0,96},{32,64},{64,32},{96,0},{128,224},{160,192},{192,160},{224,1... | collective-permute-start | bytes 98312 | tf_op jit(solution)/shard_map/ppermute | solution.py:280
  94.3 0.9 collective-permute-start.9
  95.2 2.3 %collective-permute-start.10 = (bf16[2,64,128]{2,1,0:T(8,128)(2,1)}, bf16[2,64,128]{2,1,0:T(8,128)(2,1)S(1)}, u32[]{:S(2)}, u32[]{:S(2)}) collective-permute-start(bf16[2,64,128]{2,1,0:T(8,128)(2,1)} %get-tuple-element.77), channel_id=1, source_target_pairs={{0,160},{32,128},{64,224},{96,192},{128,32},{160,0},{192,96},{224,... | collective-permute-start | bytes 98312 | tf_op jit(solution)/shard_map/ppermute | solution.py:280
  97.5 1.2 %collective-permute-start.11 = (bf16[2,64,128]{2,1,0:T(8,128)(2,1)}, bf16[2,64,128]{2,1,0:T(8,128)(2,1)S(1)}, u32[]{:S(2)}, u32[]{:S(2)}) collective-permute-start(bf16[2,64,128]{2,1,0:T(8,128)(2,1)} %get-tuple-element.78), channel_id=1, source_target_pairs={{0,192},{32,224},{64,128},{96,160},{128,64},{160,96},{192,0},{224,... | collective-permute-start | bytes 98312 | tf_op jit(solution)/shard_map/ppermute | solution.py:280
  98.7 1.9 %collective-permute-start.12 = (bf16[2,64,128]{2,1,0:T(8,128)(2,1)}, bf16[2,64,128]{2,1,0:T(8,128)(2,1)S(1)}, u32[]{:S(2)}, u32[]{:S(2)}) collective-permute-start(bf16[2,64,128]{2,1,0:T(8,128)(2,1)} %get-tuple-element.79), channel_id=1, source_target_pairs={{0,224},{32,192},{64,160},{96,128},{128,96},{160,64},{192,32},{224... | collective-permute-start | bytes 98312 | tf_op jit(solution)/shard_map/ppermute | solution.py:280
  100.5 1.4 %copy.45 = bf16[48,64,128]{2,0,1:T(8,128)(2,1)} copy(bf16[48,64,128]{2,1,0:T(8,128)(2,1)S(1)} %bitcast.26) | data formatting | bytes 1572864 | tf_op jit(solution)/shard_map/reshape | solution.py:294
  102.0 0.9 collective-permute-done.11.refs_6_
  104.0 1.9 %gather_grads.1 = (bf16[64,8,128]{2,1,0:T(8,128)(2,1)}, bf16[64,8,128]{2,1,0:T(8,128)(2,1)}) custom-call(s32[1]{0:T(128)} %bitcast.12.me_ref, bf16[2,64,128]{2,1,0:T(8,128)(2,1)} %get-tuple-element.81.refs_0_, bf16[2,64,128]{2,1,0:T(8,128)(2,1)} %copy-done.4, bf16[2,64,128]{2,1,0:T(8,128)(2,1)} %copy-done.5, bf16[2,64,128]{2,1,0:T(8,128)(2,1)} %copy-done.6, ...), custom_call_target="tpu_custom_call" | custom-call | tf_op jit(solution)/shard_map/gather_grads/pallas_call | solution.py:182
  (68 shorter events, 5.4 us)
Async XLA Ops:
  0.6 10.0 %copy-start.11 = (f32[64,48]{0,1:T(8,128)S(1)}, f32[64,48]{0,1:T(8,128)}, u32[]{:S(2)}) copy-start(f32[64,48]{0,1:T(8,128)} %param.12) | copy-start | bytes 36868
  0.6 10.0 %copy-start.1 = (bf16[64,48,128]{2,1,0:T(8,128)(2,1)S(1)}, bf16[64,48,128]{2,1,0:T(8,128)(2,1)}, u32[]{:S(2)}) copy-start(bf16[64,48,128]{2,1,0:T(8,128)(2,1)} %param.11) | copy-start | bytes 2359300
  0.7 10.2 %copy-start.2 = (bf16[64,48,128]{2,1,0:T(8,128)(2,1)S(1)}, bf16[64,48,128]{2,1,0:T(8,128)(2,1)}, u32[]{:S(2)}) copy-start(bf16[64,48,128]{2,1,0:T(8,128)(2,1)} %param.10) | copy-start | bytes 2359300
  2.5 12.0 %all-to-all-start.1 = ((bf16[8,2,64,128]{3,2,1,0:T(8,128)(2,1)}), bf16[8,2,64,128]{3,2,1,0:T(8,128)(2,1)S(1)}, u32[]{:S(2)}, u32[]{:S(2)}) async-start(bf16[8,2,64,128]{3,2,1,0:T(8,128)(2,1)} %pad_maximum_fusion.1), calls=%async_computation.1 | async-start | bytes 524288 | tf_op jit(solution)/shard_map/all_to_all | solution.py:228
  10.7 1.1 %copy-start.3 = (bf16[64,48,128]{2,1,0:T(8,128)(2,1)S(1)}, bf16[64,48,128]{2,1,0:T(8,128)(2,1)}, u32[]{:S(2)}) copy-start(bf16[64,48,128]{2,1,0:T(8,128)(2,1)} %param.7) | copy-start | bytes 2359300
  14.5 26.7 %all-to-all-start = ((bf16[8,13,64,128]{3,2,1,0:T(8,128)(2,1)}), bf16[8,13,64,128]{3,2,1,0:T(8,128)(2,1)S(1)}, u32[]{:S(2)}, u32[]{:S(2)}) async-start(bf16[8,13,64,128]{3,2,1,0:T(8,128)(2,1)} %pad_maximum_fusion), calls=%async_computation | async-start | bytes 3407872 | tf_op jit(solution)/shard_map/all_to_all | solution.py:228
  18.2 19.0 %collective-permute-start = (bf16[8,2,64,128]{3,2,1,0:T(8,128)(2,1)S(1)}, bf16[8,2,64,128]{3,2,1,0:T(8,128)(2,1)S(1)}, u32[]{:S(2)}, u32[]{:S(2)}) collective-permute-start(bf16[8,2,64,128]{3,2,1,0:T(8,128)(2,1)S(1)} %all-to-all-done.1.rest_0_), channel_id=1, source_target_pairs={{16,0},{17,1},{18,2},{19,3},{20,4},{21,5},{22,6},{23,7},{24,8},{25... | collective-permute-start | bytes 786440 | tf_op jit(solution)/shard_map/ppermute | solution.py:234
  37.2 11.3 %collective-permute-start.2 = (bf16[8,2,64,128]{3,2,1,0:T(8,128)(2,1)S(1)}, bf16[8,2,64,128]{3,2,1,0:T(8,128)(2,1)S(1)}, u32[]{:S(2)}, u32[]{:S(2)}) collective-permute-start(bf16[8,2,64,128]{3,2,1,0:T(8,128)(2,1)S(1)} %collective-permute-done.rest_0_), channel_id=1, source_target_pairs={{0,1},{1,2},{2,3},{3,4},{4,5},{5,6},{6,7},{7,8},{8,9},{9,10},{10,1... | collective-permute-start | bytes 786440 | tf_op jit(solution)/shard_map/ppermute | solution.py:236
  38.7 15.1 %collective-permute-start.1 = (bf16[8,2,64,128]{3,2,1,0:T(8,128)(2,1)S(1)}, bf16[8,2,64,128]{3,2,1,0:T(8,128)(2,1)S(1)}, u32[]{:S(2)}, u32[]{:S(2)}) collective-permute-start(bf16[8,2,64,128]{3,2,1,0:T(8,128)(2,1)S(1)} %all-to-all-done.1.rest_0_), channel_id=1, source_target_pairs={{0,1},{1,2},{2,3},{3,4},{4,5},{5,6},{6,7},{7,8},{8,9},{9,10},{10,1... | collective-permute-start | bytes 786440 | tf_op jit(solution)/shard_map/ppermute | solution.py:235
  46.4 0.8 copy-start
  53.6 9.6 %collective-permute-start.3 = (bf16[8,2,64,128]{3,2,1,0:T(8,128)(2,1)S(1)}, bf16[8,2,64,128]{3,2,1,0:T(8,128)(2,1)S(1)}, u32[]{:S(2)}, u32[]{:S(2)}) collective-permute-start(bf16[8,2,64,128]{3,2,1,0:T(8,128)(2,1)S(1)} %get-tuple-element.68), channel_id=1, source_target_pairs={{1,0},{2,1},{3,2},{4,3},{5,4},{6,5},{7,6},{8,7},{9,8},{10,9},{11,1... | collective-permute-start | bytes 786440 | tf_op jit(solution)/shard_map/ppermute | solution.py:286
  63.4 13.0 %collective-permute-start.4 = (bf16[8,2,64,128]{3,2,1,0:T(8,128)(2,1)S(1)}, bf16[8,2,64,128]{3,2,1,0:T(8,128)(2,1)S(1)}, u32[]{:S(2)}, u32[]{:S(2)}) collective-permute-start(bf16[8,2,64,128]{3,2,1,0:T(8,128)(2,1)S(1)} %get-tuple-element.70), channel_id=1, source_target_pairs={{1,0},{2,1},{3,2},{4,3},{5,4},{6,5},{7,6},{8,7},{9,8},{10,9},{11,1... | collective-permute-start | bytes 786440 | tf_op jit(solution)/shard_map/ppermute | solution.py:291
  64.5 25.3 %collective-permute-start.5 = (bf16[8,2,64,128]{3,2,1,0:T(8,128)(2,1)S(1)}, bf16[8,2,64,128]{3,2,1,0:T(8,128)(2,1)S(1)}, u32[]{:S(2)}, u32[]{:S(2)}) collective-permute-start(bf16[8,2,64,128]{3,2,1,0:T(8,128)(2,1)S(1)} %add_convert_fusion), channel_id=1, source_target_pairs={{16,0},{17,1},{18,2},{19,3},{20,4},{21,5},{22,6},{23,7},{24,8},{25... | collective-permute-start | bytes 786440 | tf_op jit(solution)/shard_map/ppermute | solution.py:290
  72.8 27.7 %all-to-all-start.2 = ((bf16[8,6,64,128]{3,2,1,0:T(8,128)(2,1)}), bf16[8,6,64,128]{3,2,1,0:T(8,128)(2,1)S(1)}, u32[]{:S(2)}, u32[]{:S(2)}) async-start(bf16[8,6,64,128]{3,2,1,0:T(8,128)(2,1)} %get-tuple-element.65), calls=%async_computation.2 | async-start | bytes 1572864 | tf_op jit(solution)/shard_map/all_to_all | solution.py:228
  76.4 13.4 %copy-start.12 = (bf16[8,2,64,128]{3,2,1,0:T(8,128)(2,1)}, bf16[8,2,64,128]{3,2,1,0:T(8,128)(2,1)S(1)}, u32[]{:S(2)}) copy-start(bf16[8,2,64,128]{3,2,1,0:T(8,128)(2,1)S(1)} %collective-permute-done.4.refs_1_) | copy-start | bytes 786436
  89.8 0.7 copy-start.13
  92.4 5.1 %collective-permute-start.6 = (bf16[2,64,128]{2,1,0:T(8,128)(2,1)}, bf16[2,64,128]{2,1,0:T(8,128)(2,1)S(1)}, u32[]{:S(2)}, u32[]{:S(2)}) collective-permute-start(bf16[2,64,128]{2,1,0:T(8,128)(2,1)} %get-tuple-element.73), channel_id=1, source_target_pairs={{0,32},{32,0},{64,96},{96,64},{128,160},{160,128},{192,224},{224,1... | collective-permute-start | bytes 98312 | tf_op jit(solution)/shard_map/ppermute | solution.py:280
  92.4 6.2 %collective-permute-start.7 = (bf16[2,64,128]{2,1,0:T(8,128)(2,1)}, bf16[2,64,128]{2,1,0:T(8,128)(2,1)S(1)}, u32[]{:S(2)}, u32[]{:S(2)}) collective-permute-start(bf16[2,64,128]{2,1,0:T(8,128)(2,1)} %get-tuple-element.74), channel_id=1, source_target_pairs={{0,64},{32,96},{64,0},{96,32},{128,192},{160,224},{192,128},{224,1... | collective-permute-start | bytes 98312 | tf_op jit(solution)/shard_map/ppermute | solution.py:280
  93.1 8.8 %collective-permute-start.8 = (bf16[2,64,128]{2,1,0:T(8,128)(2,1)}, bf16[2,64,128]{2,1,0:T(8,128)(2,1)S(1)}, u32[]{:S(2)}, u32[]{:S(2)}) collective-permute-start(bf16[2,64,128]{2,1,0:T(8,128)(2,1)} %get-tuple-element.75), channel_id=1, source_target_pairs={{0,96},{32,64},{64,32},{96,0},{128,224},{160,192},{192,160},{224,1... | collective-permute-start | bytes 98312 | tf_op jit(solution)/shard_map/ppermute | solution.py:280
  94.3 7.6 %collective-permute-start.9 = (bf16[2,64,128]{2,1,0:T(8,128)(2,1)}, bf16[2,64,128]{2,1,0:T(8,128)(2,1)S(1)}, u32[]{:S(2)}, u32[]{:S(2)}) collective-permute-start(bf16[2,64,128]{2,1,0:T(8,128)(2,1)} %get-tuple-element.76), channel_id=1, source_target_pairs={{0,128},{32,160},{64,192},{96,224},{128,0},{160,32},{192,64},{224,... | collective-permute-start | bytes 98312 | tf_op jit(solution)/shard_map/ppermute | solution.py:280
  95.2 6.7 %collective-permute-start.10 = (bf16[2,64,128]{2,1,0:T(8,128)(2,1)}, bf16[2,64,128]{2,1,0:T(8,128)(2,1)S(1)}, u32[]{:S(2)}, u32[]{:S(2)}) collective-permute-start(bf16[2,64,128]{2,1,0:T(8,128)(2,1)} %get-tuple-element.77), channel_id=1, source_target_pairs={{0,160},{32,128},{64,224},{96,192},{128,32},{160,0},{192,96},{224,... | collective-permute-start | bytes 98312 | tf_op jit(solution)/shard_map/ppermute | solution.py:280
  97.5 5.9 %copy-start.4 = (bf16[2,64,128]{2,1,0:T(8,128)(2,1)}, bf16[2,64,128]{2,1,0:T(8,128)(2,1)S(1)}, u32[]{:S(2)}) copy-start(bf16[2,64,128]{2,1,0:T(8,128)(2,1)S(1)} %collective-permute-done.6.refs_1_) | copy-start | bytes 98308
  97.5 5.3 %collective-permute-start.11 = (bf16[2,64,128]{2,1,0:T(8,128)(2,1)}, bf16[2,64,128]{2,1,0:T(8,128)(2,1)S(1)}, u32[]{:S(2)}, u32[]{:S(2)}) collective-permute-start(bf16[2,64,128]{2,1,0:T(8,128)(2,1)} %get-tuple-element.78), channel_id=1, source_target_pairs={{0,192},{32,224},{64,128},{96,160},{128,64},{160,96},{192,0},{224,... | collective-permute-start | bytes 98312 | tf_op jit(solution)/shard_map/ppermute | solution.py:280
  98.7 4.8 %copy-start.5 = (bf16[2,64,128]{2,1,0:T(8,128)(2,1)}, bf16[2,64,128]{2,1,0:T(8,128)(2,1)S(1)}, u32[]{:S(2)}) copy-start(bf16[2,64,128]{2,1,0:T(8,128)(2,1)S(1)} %collective-permute-done.7.refs_2_) | copy-start | bytes 98308
  98.7 4.8 %collective-permute-start.12 = (bf16[2,64,128]{2,1,0:T(8,128)(2,1)}, bf16[2,64,128]{2,1,0:T(8,128)(2,1)S(1)}, u32[]{:S(2)}, u32[]{:S(2)}) collective-permute-start(bf16[2,64,128]{2,1,0:T(8,128)(2,1)} %get-tuple-element.79), channel_id=1, source_target_pairs={{0,224},{32,192},{64,160},{96,128},{128,96},{160,64},{192,32},{224... | collective-permute-start | bytes 98312 | tf_op jit(solution)/shard_map/ppermute | solution.py:280
  101.9 1.5 %copy-start.6 = (bf16[2,64,128]{2,1,0:T(8,128)(2,1)}, bf16[2,64,128]{2,1,0:T(8,128)(2,1)S(1)}, u32[]{:S(2)}) copy-start(bf16[2,64,128]{2,1,0:T(8,128)(2,1)S(1)} %collective-permute-done.8.refs_3_) | copy-start | bytes 98308
  101.9 1.5 %copy-start.7 = (bf16[2,64,128]{2,1,0:T(8,128)(2,1)}, bf16[2,64,128]{2,1,0:T(8,128)(2,1)S(1)}, u32[]{:S(2)}) copy-start(bf16[2,64,128]{2,1,0:T(8,128)(2,1)S(1)} %collective-permute-done.9.refs_4_) | copy-start | bytes 98308
  101.9 1.5 %copy-start.8 = (bf16[2,64,128]{2,1,0:T(8,128)(2,1)}, bf16[2,64,128]{2,1,0:T(8,128)(2,1)S(1)}, u32[]{:S(2)}) copy-start(bf16[2,64,128]{2,1,0:T(8,128)(2,1)S(1)} %collective-permute-done.10.refs_5_) | copy-start | bytes 98308
  102.8 0.6 copy-start.9
  103.4 0.6 copy-start.10

commit v2 on v1

v2 whole, which is shorter than its diff:
```python
import math

import jax
import jax.numpy as jnp
from jax import lax
from jax.experimental import pallas as pl
from jax.experimental.pallas import tpu as pltpu
from jax.sharding import PartitionSpec as P

LOG2E = math.log2(math.e)
NT = (((1,), (1,)), ((), ()))
NN = (((1,), (0,)), ((), ()))
f32 = jnp.float32
bf16 = jnp.bfloat16


def attention_part(
    tables, row, packed, contexts, dq_starts, last, keys_step, rows_step, heads, g_types, name
):
    src, _, T, D = contexts[0].shape
    R = heads * T
    many = len(contexts)
    n = many * src
    U, W = keys_step * T, rows_step * R
    groups = n // keys_step
    scale = D ** (-0.5)
    lanes = R // D

    def body(table, packed_ref, *rest):
        kv_refs, rest = rest[:many], rest[many:]
        start_refs, rest = rest[: len(dq_starts)], rest[len(dq_starts) :]
        out_ref, *rest = rest
        g_refs, rest = rest[:many], rest[many:]
        if many > 1:
            kv_s, g_s, *rest = rest
            for c in range(many):
                kv_s[c * src : (c + 1) * src] = kv_refs[c][...]
        else:
            kv_s, g_s = kv_refs[0], g_refs[0]
        st_s, k_s, v_s, kt_s, dk_s, dv_s, *rest = rest
        dq_s = rest[0] if last else out_ref
        dq_s[...] = sum((r[...] for r in start_refs), jnp.zeros_like(dq_s))
        kid = lambda j: table[row, j]
        kord = lambda j: table[row + 1, j]

        def prepare(i, carry):
            st = packed_ref[table[0, i], 2 * R :].astype(f32)
            st = st[0:8] + st[8:16] + st[16:24]
            st_s[i, 0:1] = jnp.concatenate([st[j : j + 1] for j in range(lanes)], axis=1)
            st_s[i, 1:2] = jnp.concatenate([st[j : j + 1] for j in range(lanes, 2 * lanes)], axis=1)
            return carry

        lax.fori_loop(0, src, prepare, 0)
        lead = lax.broadcasted_iota(jnp.int32, (T, R), 1) % T - lax.broadcasted_iota(
            jnp.int32, (T, R), 0
        )

        def group(g, carry):
            for j in range(keys_step):
                b = kid(g * keys_step + j)
                k_s[pl.ds(j * T, T)] = kv_s[b, 0]
                v_s[pl.ds(j * T, T)] = kv_s[b, 1]
            kt_s[...] = k_s[...].T
            dk_s[...] = jnp.zeros_like(dk_s)
            dv_s[...] = jnp.zeros_like(dv_s)

            def step(i, inner):
                at = pl.ds(pl.multiple_of(i * W, W), W)
                ids = [table[0, i * rows_step + h] for h in range(rows_step)]
                q = jnp.concatenate([packed_ref[b, 0:R] for b in ids], axis=0)
                do = jnp.concatenate([packed_ref[b, R : 2 * R] for b in ids], axis=0)
                k, v = k_s[...], v_s[...]
                s = lax.dot_general(k, q, NT, preferred_element_type=f32)
                dp = lax.dot_general(v, do, NT, preferred_element_type=f32)
                p_cols, ds_cols = [], []
                for h in range(rows_step):
                    at_row = i * rows_step + h
                    lse, delta, place = st_s[at_row, 0:1], st_s[at_row, 1:2], table[1, at_row]
                    p_rows, ds_rows = [], []
                    for j in range(keys_step):
                        behind = (kord(g * keys_step + j) - place) * T
                        cut = (slice(j * T, (j + 1) * T), slice(h * R, (h + 1) * R))
                        p = jnp.where(
                            lead >= behind, jnp.exp2(s[cut] * (scale * LOG2E) - lse), 0.0
                        )
                        ds_rows.append((p * (dp[cut] - delta)).astype(bf16))
                        p_rows.append(p.astype(bf16))
                    p_cols.append(jnp.concatenate(p_rows, axis=0))
                    ds_cols.append(jnp.concatenate(ds_rows, axis=0))
                p, ds = jnp.concatenate(p_cols, axis=1), jnp.concatenate(ds_cols, axis=1)
                dv_s[...] += lax.dot_general(p, do, NN, preferred_element_type=f32)
                dk_s[...] += lax.dot_general(ds, q, NN, preferred_element_type=f32)
                dq_s[:, at] += lax.dot_general(kt_s[...], ds, NN, preferred_element_type=f32)
                return inner

            steps = (table[row + 2, g] + rows_step - 1) // rows_step
            lax.fori_loop(0, steps, step, 0)
            for j in range(keys_step):
                b = kid(g * keys_step + j)
                g_s[b, 0] = (dk_s[pl.ds(j * T, T)] * scale).astype(g_s.dtype)
                g_s[b, 1] = dv_s[pl.ds(j * T, T)].astype(g_s.dtype)
            return carry

        lax.fori_loop(0, groups, group, 0)
        if many > 1:
            for c in range(many):
                g_refs[c][...] = g_s[c * src : (c + 1) * src].astype(g_refs[c].dtype)
        if last:
            for j in range(src):
                at = pl.ds(j * R, R)
                out_ref[table[0, j]] = (dq_s[:, at].T * scale).astype(bf16).reshape(heads, T, D)

    smem = pl.BlockSpec(memory_space=pltpu.SMEM)
    vmem = pl.BlockSpec(memory_space=pltpu.VMEM)
    if last:
        dq_out = jax.ShapeDtypeStruct((src, heads, T, D), bf16)
    else:
        dq_out = jax.ShapeDtypeStruct((D, src * R), f32)
    g_outs = [jax.ShapeDtypeStruct((src, 2, T, D), t) for t in g_types]
    scratch = []
    if many > 1:
        scratch = [pltpu.VMEM((n, 2, T, D), bf16), pltpu.VMEM((n, 2, T, D), f32)]
    scratch += [
        pltpu.VMEM((src, 8, R), f32),
        pltpu.VMEM((U, D), bf16),
        pltpu.VMEM((U, D), bf16),
        pltpu.VMEM((D, U), bf16),
        pltpu.VMEM((U, D), f32),
        pltpu.VMEM((U, D), f32),
    ]
    if last:
        scratch.append(pltpu.VMEM((D, src * R), f32))
    arrays = [packed, *contexts, *dq_starts]
    return pl.pallas_call(
        body,
        out_shape=(dq_out, *g_outs),
        in_specs=[smem] + [vmem] * len(arrays),
        out_specs=(vmem,) * (1 + many),
        scratch_shapes=scratch,
        compiler_params=pltpu.CompilerParams(vmem_limit_bytes=32 * 2**20),
        cost_estimate=pl.CostEstimate(flops=1, bytes_accessed=1, transcendentals=0),
        name=name,
    )(tables, *arrays)


def add_by_peer(*arrays):
    src, *rest = arrays[0].shape

    def body(*refs):
        ins, outs = refs[: len(arrays)], refs[len(arrays) :]
        me = lax.axis_index("head")
        for j in range(src):
            at = me ^ j
            outs[j][...] = sum(r[at].astype(f32) for r in ins).astype(bf16)

    vmem = pl.BlockSpec(memory_space=pltpu.VMEM)
    return pl.pallas_call(
        body,
        out_shape=[jax.ShapeDtypeStruct(rest, bf16)] * src,
        in_specs=[vmem] * len(arrays),
        out_specs=[vmem] * src,
        cost_estimate=pl.CostEstimate(flops=10**10, bytes_accessed=1, transcendentals=0),
        name="add_by_peer",
    )(*arrays)


def gather_grads(pieces):
    src = len(pieces)
    _, T, D = pieces[0].shape

    def body(*refs):
        me = lax.axis_index("head")
        ins, outs, held, wide = refs[:src], refs[src : src + 2], refs[-2], refs[-1]
        for j in range(src):
            held[me ^ j] = ins[j][...]
        for c in range(2):
            for g in range(src):
                wide[:, g, :] = held[g, c].astype(f32)
            outs[c][...] = wide[...].astype(bf16)

    vmem = pl.BlockSpec(memory_space=pltpu.VMEM)
    return pl.pallas_call(
        body,
        out_shape=[jax.ShapeDtypeStruct((T, src, D), bf16)] * 2,
        in_specs=[vmem] * src,
        out_specs=[vmem] * 2,
        scratch_shapes=[pltpu.VMEM((src, 2, T, D), bf16), pltpu.VMEM((T, src, D), f32)],
        name="gather_grads",
    )(*pieces)


def order_tables(block_order, spots_of, heads, inners, outers, keys_step):
    wide = 128

    def body(order_ref, out_ref):
        table = order_ref[...]
        sub = lax.broadcasted_iota(jnp.int32, table.shape, 0)
        spot = lax.broadcasted_iota(jnp.int32, table.shape, 1)

        def sort(spots):
            n = heads * len(spots)
            down = jnp.concatenate(
                [
                    jnp.sum(jnp.where(spot == a * outers + b, table, 0), axis=1, keepdims=True)
                    for a, b in spots
                ],
                axis=0,
            )
            s = lax.broadcasted_iota(jnp.int32, (n, wide), 0)
            lane = lax.broadcasted_iota(jnp.int32, (n, wide), 1)
            across = jnp.sum(jnp.where(s == lane, down, 0), axis=0, keepdims=True)
            ahead = jnp.where((across > down) & (lane < n), 1, 0)
            hit = jnp.sum(ahead, axis=1, keepdims=True) == lane
            ids = jnp.sum(jnp.where(hit, s, 0), axis=0, keepdims=True)
            return ids, jnp.sum(jnp.where(hit, down, 0), axis=0, keepdims=True)

        own, lists = spots_of()
        q_id, q_order = sort([own])
        rows = [q_id, q_order]
        lane = lax.broadcasted_iota(jnp.int32, (1, wide), 1)
        for spots in lists:
            ids, order = sort(spots)
            step = keys_step * len(spots)
            seen = jnp.zeros((1, wide), jnp.int32)
            for g in range(heads * len(spots) // step):
                least = jnp.sum(
                    jnp.where(lane == (g + 1) * step - 1, order, 0), axis=1, keepdims=True
                )
                count = jnp.sum(
                    jnp.where((q_order >= least) & (lane < heads), 1, 0), axis=1, keepdims=True
                )
                seen = jnp.where(lane == g, count, seen)
            rows += [ids, order, seen]
        rows.append(jnp.zeros((16 - len(rows), wide), jnp.int32))
        out_ref[...] = jnp.concatenate(rows, axis=0)

    vmem = pl.BlockSpec(memory_space=pltpu.VMEM)
    return pl.pallas_call(
        body,
        out_shape=jax.ShapeDtypeStruct((16, wide), jnp.int32),
        in_specs=[vmem],
        out_specs=vmem,
        name="order_tables",
    )(block_order.reshape(heads, inners * outers))


def pieces(x):
    high = lax.reduce_precision(x, 8, 7)
    rest = x - high
    middle = lax.reduce_precision(rest, 8, 7)
    return [v.astype(bf16) for v in (high, middle, rest - middle)]


def shards(query, keys, values, attn_out, grad_out, log_norm, block_order):
    heads = lax.axis_size("head")
    inners = lax.axis_size("inner")
    outers = lax.axis_size("outer")
    T, q_heads, D = query.shape
    group = q_heads // keys.shape[1]

    ring = ("inner", "outer")
    place = lambda a, b: a * outers + b
    swap = [(place(1 - a, b), place(a, b)) for a in range(inners) for b in range(outers)]
    ahead = [
        (place(a, b), place(a, b + 1) if b + 1 < outers else place(1 - a, 0))
        for a in range(inners)
        for b in range(outers)
    ]
    across = [(dict(swap)[a], b) for a, b in ahead]
    back = [(b, a) for a, b in ahead]

    def exchange(x):
        return lax.all_to_all(x, "head", split_axis=0, concat_axis=0, tiled=True)

    def by_head(x):
        return x.reshape(T, heads, -1, D).transpose(1, 2, 0, 3)

    kv = exchange(jnp.concatenate([by_head(keys), by_head(values)], axis=1))
    kv_far_partner = lax.ppermute(kv, ring, across)
    kv_far = lax.ppermute(kv, ring, ahead)
    kv_after, kv_far_partner = lax.optimization_barrier((kv, kv_far_partner))
    kv_partner = lax.ppermute(kv_after, ring, swap)

    delta = jnp.sum(grad_out.astype(f32) * attn_out.astype(f32), axis=-1)
    stats = jnp.stack([log_norm * LOG2E, delta])
    lanes = group * T // D
    stats = stats.reshape(2, T, heads, group).transpose(2, 0, 3, 1).reshape(heads, 2 * lanes, D)
    stats = jnp.pad(stats, ((0, 0), (0, 8 - 2 * lanes), (0, 0)))
    stats = jnp.concatenate(pieces(stats), axis=1)
    stats = jnp.pad(stats, ((0, 0), (0, 8), (0, 0)))
    keys_step, rows_step = 4, 2
    names = ["far_partner", "far", "near_partner", "near"]

    def spots_of():
        a, b = lax.axis_index("inner"), lax.axis_index("outer")
        before = jnp.where(b == 0, outers - 1, b - 1)
        turn = jnp.where(b == 0, 1 - a, a)
        lists = [[(1 - turn, before)], [(turn, before)], [(1 - a, b)], [(a, b)]]
        return (a, b), lists

    tables = order_tables(block_order, spots_of, heads, inners, outers, keys_step)
    rows_of = lambda x: by_head(x).reshape(heads, group * T, D)
    stats, tables = lax.optimization_barrier((stats, tables))
    packed = exchange(jnp.concatenate([rows_of(query), rows_of(grad_out), stats], axis=1))
    def part(name, contexts, dq_starts, last, g_types):
        return attention_part(
            tables,
            2 + 3 * names.index(name),
            packed,
            contexts,
            dq_starts,
            last,
            keys_step * len(contexts),
            rows_step,
            group,
            g_types,
            name,
        )

    def to_peers(blocks):
        return [blocks[0]] + [
            lax.ppermute(blocks[j], "head", [(h, h ^ j) for h in range(heads)])
            for j in range(1, heads)
        ]

    dq, far_partner = part("far_partner", [kv_far_partner], [], False, [bf16])
    far_partner = lax.ppermute(far_partner, ring, back)
    starts = [dq]
    packed, dq = lax.optimization_barrier((packed, dq))
    dq, far = part("far", [kv_far], [], False, [bf16])
    far = lax.ppermute(far, ring, back)
    starts.append(dq)
    packed, dq = lax.optimization_barrier((packed, dq))
    dq, near_partner = part("near_partner", [kv_partner], starts, False, [f32])
    partner = (near_partner + far_partner.astype(f32)).astype(bf16)
    partner = lax.ppermute(partner, ring, swap)
    dq, near = part("near", [kv], [dq], True, [f32])
    dq = exchange(dq)
    grad = to_peers(add_by_peer(near, partner, far))
    dq = dq.reshape(q_heads, T, D).transpose(1, 0, 2)
    dq, grad = lax.optimization_barrier((dq, grad))
    return dq, *gather_grads(grad)


def solution(mesh):
    rows = P(("head", "inner", "outer"))
    return jax.shard_map(
        shards,
        mesh=mesh,
        in_specs=(rows,) * 6 + (P(),),
        out_specs=(rows,) * 3,
        check_vma=False,
    )
```

time: 107 us -> 103 us (0.963)
  waiting for transfers between devices: 31 us -> 25.2 us
  Pallas kernels: 23.6 us -> 25.6 us
  starting transfers between devices: 38.7 us -> 40.6 us
    ppermute x1, waiting for transfers between devices: 13.4 us -> 1.9 us  [shards(): partner = lax.ppermute(partner, ring, swap)]
    ppermute x2, starting transfers between devices: 7.82 us -> 14 us  [the longest x1 7.22 us: shards(): kv_far_partner = lax.ppermute(kv, ring, across)]
    ppermute x2, waiting for transfers between devices: 14 us -> 18.1 us  [the longest x1 16 us: shards(): kv_far_partner = lax.ppermute(kv, ring, across)]
    ppermute x1, starting transfers between devices: 8.33 us -> 5.02 us  [shards(): partner = lax.ppermute(partner, ring, swap)]
    ppermute x7, waiting for transfers between devices: 1.48 us -> 4.01 us  [to_peers(): lax.ppermute(blocks[j], 'head', [(h, h ^ j) for h in range(heads)])]
    pallas_call x3 -> x5, Pallas kernels: 19.8 us -> 21.8 us  [the longest x4 20.2 us: attention_part(): pl.pallas_call(body, out_shape=(dq_out, *g_outs), in_specs=[smem] + [vmem...]
    reduce_sum x7 -> x0, other arithmetic: 1.2 us -> none  [the longest x3 0.55 us: sort_down(): rank = jnp.sum((order[None, :] > order[:, None]).astype(jnp.int32), axis=1)]
  transfers between devices with their start and end apart: 16 -> 16, of which waited for: 7 -> 8; matrix products, arithmetic and copies ran while one was open for 7% -> 6% of each run, Pallas kernels for 21% -> 23%
where the time goes in v2:
time: 103 us; the launch traced here: 102 us
  starting transfers between devices  40.6 us (39%)
  Pallas kernels  25.6 us (25%)
  waiting for transfers between devices  25.2 us (24%)
  local copies, waits for them, and re-layouts  6.72 us (7%)
  other arithmetic  3.36 us (3%)
    pallas_call x4, Pallas kernels, attention_part(): pl.pallas_call(body, out_shape=(dq_out, *g_outs), in_specs=[smem] + [vmem...  20.2 us
    ppermute x1, waiting for transfers between devices, shards(): kv_far_partner = lax.ppermute(kv, ring, across)  16 us
    all_to_all x3, starting transfers between devices, exchange(): return lax.all_to_all(x, 'head', split_axis=0, concat_axis=0, tiled=True)  12.4 us
    ppermute x7, starting transfers between devices, to_peers(): lax.ppermute(blocks[j], 'head', [(h, h ^ j) for h in range(heads)])  7.63 us
    ppermute x1, starting transfers between devices, shards(): kv_far_partner = lax.ppermute(kv, ring, across)  7.22 us
    ppermute x1, starting transfers between devices, shards(): kv_partner = lax.ppermute(kv_after, ring, swap)  6.75 us
    ppermute x1, starting transfers between devices, shards(): partner = lax.ppermute(partner, ring, swap)  5.02 us
    ppermute x7, waiting for transfers between devices, to_peers(): lax.ppermute(blocks[j], 'head', [(h, h ^ j) for h in range(heads)])  4.01 us
  transfers between devices with their start and end apart: 16, of which 8 were waited for; matrix products, arithmetic and copies ran while one was open for 6% of the time, Pallas kernels for 23%

profile of v2, /device:TPU:32, one launch (start us, length us, event | category | flops | bytes accessed | tf_op | source)
XLA Modules:
  0.0 102.4 jit_solution(16661037248635040680)
XLA Ops:
  0.7 1.1 %copy_bitcast_fusion.1 = (bf16[8,1,64,128]{3,2,1,0:T(8,128)(2,1)S(1)}, bf16[8,1,64,128]{3,2,1,0:T(8,128)(2,1)S(1)}) fusion(bf16[64,8,128]{2,1,0:T(8,128)(2,1)} %param.9, bf16[64,8,128]{2,1,0:T(8,128)(2,1)} %param.8), kind=kLoop, calls=%fused_computation.9 | loop fusion | bytes 524288 | tf_op jit(solution)/shard_map/transpose | solution.py:276
  1.8 0.7 pad_maximum_fusion.1
  2.5 4.5 %all-to-all-start.1 = ((bf16[8,2,64,128]{3,2,1,0:T(8,128)(2,1)}), bf16[8,2,64,128]{3,2,1,0:T(8,128)(2,1)S(1)}, u32[]{:S(2)}, u32[]{:S(2)}) async-start(bf16[8,2,64,128]{3,2,1,0:T(8,128)(2,1)} %pad_maximum_fusion.1), calls=%async_computation.1 | async-start | bytes 524288 | tf_op jit(solution)/shard_map/all_to_all | solution.py:273
  7.0 1.3 %reshape.39.order_ref = s32[8,32]{1,0:T(8,128)} reshape(s32[256]{0:T(256)} %param.13) | data formatting | bytes 2048 | tf_op jit(solution)/shard_map/reshape | solution.py:244
  8.3 1.7 %order_tables.1.table = s32[16,128]{1,0:T(8,128)} custom-call(s32[8,32]{1,0:T(8,128)} %reshape.39.order_ref), custom_call_target="tpu_custom_call" | custom-call | tf_op jit(solution)/shard_map/order_tables/pallas_call | solution.py:238
  10.0 0.7 broadcast_multiply_fusion
  12.1 1.3 %pad_maximum_fusion = bf16[8,800,128]{2,1,0:T(8,128)(2,1)} fusion(bf16[8,32,128]{2,1,0:T(8,128)(2,1)S(1)} %fusion.4, bf16[8,384,128]{2,1,0:T(8,128)(2,1)S(1)} %bitcast.29, bf16[8,384,128]{2,1,0:T(8,128)(2,1)S(1)} %bitcast.30), kind=kLoop, calls=%fused_computation | loop fusion | flops 4915200 | bytes 3276800 | tf_op jit(solution)/shard_map/concatenate | solution.py:304
  13.4 1.1 %all-to-all-done.1.rest_0_ = bf16[8,2,64,128]{3,2,1,0:T(8,128)(2,1)S(1)} async-done(((bf16[8,2,64,128]{3,2,1,0:T(8,128)(2,1)}), bf16[8,2,64,128]{3,2,1,0:T(8,128)(2,1)S(1)}, u32[]{:S(2)}, u32[]{:S(2)}) %all-to-all-start.1) | async-done | bytes 262176 | tf_op jit(solution)/shard_map/all_to_all | solution.py:273
  14.5 3.8 %all-to-all-start = ((bf16[8,800,128]{2,1,0:T(8,128)(2,1)}), bf16[8,800,128]{2,1,0:T(8,128)(2,1)S(1)}, u32[]{:S(2)}, u32[]{:S(2)}) async-start(bf16[8,800,128]{2,1,0:T(8,128)(2,1)} %pad_maximum_fusion), calls=%async_computation | async-start | bytes 3276800 | tf_op jit(solution)/shard_map/all_to_all | solution.py:273
  18.3 7.2 %collective-permute-start = (bf16[8,2,64,128]{3,2,1,0:T(8,128)(2,1)S(1)}, bf16[8,2,64,128]{3,2,1,0:T(8,128)(2,1)S(1)}, u32[]{:S(2)}, u32[]{:S(2)}) collective-permute-start(bf16[8,2,64,128]{3,2,1,0:T(8,128)(2,1)S(1)} %all-to-all-done.1.rest_0_), channel_id=1, source_target_pairs={{16,1},{17,2},{18,3},{19,4},{20,5},{21,6},{22,7},{23,8},{24,9},{25... | collective-permute-start | bytes 786440 | tf_op jit(solution)/shard_map/ppermute | solution.py:279
  25.6 1.5 %collective-permute-start.1 = (bf16[8,2,64,128]{3,2,1,0:T(8,128)(2,1)S(1)}, bf16[8,2,64,128]{3,2,1,0:T(8,128)(2,1)S(1)}, u32[]{:S(2)}, u32[]{:S(2)}) collective-permute-start(bf16[8,2,64,128]{3,2,1,0:T(8,128)(2,1)S(1)} %all-to-all-done.1.rest_0_), channel_id=1, source_target_pairs={{0,1},{1,2},{2,3},{3,4},{4,5},{5,6},{6,7},{7,8},{8,9},{9,10},{10,1... | collective-permute-start | bytes 786440 | tf_op jit(solution)/shard_map/ppermute | solution.py:280
  27.0 16.0 %collective-permute-done.rest_0_ = bf16[8,2,64,128]{3,2,1,0:T(8,128)(2,1)S(1)} collective-permute-done((bf16[8,2,64,128]{3,2,1,0:T(8,128)(2,1)S(1)}, bf16[8,2,64,128]{3,2,1,0:T(8,128)(2,1)S(1)}, u32[]{:S(2)}, u32[]{:S(2)}) %collective-permute-start) | collective-permute-done | bytes 262176 | tf_op jit(solution)/shard_map/ppermute | solution.py:279
  43.1 6.7 %collective-permute-start.2 = (bf16[8,2,64,128]{3,2,1,0:T(8,128)(2,1)S(1)}, bf16[8,2,64,128]{3,2,1,0:T(8,128)(2,1)S(1)}, u32[]{:S(2)}, u32[]{:S(2)}) collective-permute-start(bf16[8,2,64,128]{3,2,1,0:T(8,128)(2,1)S(1)} %all-to-all-done.1.rest_0_), channel_id=1, source_target_pairs={{16,0},{17,1},{18,2},{19,3},{20,4},{21,5},{22,6},{23,7},{24,8},{25... | collective-permute-start | bytes 786440 | tf_op jit(solution)/shard_map/ppermute | solution.py:282
  49.8 5.2 %far_partner.1 = (f32[128,3072]{1,0:T(8,128)S(1)}, bf16[8,2,64,128]{3,2,1,0:T(8,128)(2,1)S(1)}) custom-call(s32[16,128]{1,0:T(8,128)S(1)} %copy-done, bf16[8,800,128]{2,1,0:T(8,128)(2,1)S(1)} %all-to-all-done.packed_ref, bf16[8,2,64,128]{3,2,1,0:T(8,128)(2,1)S(1)} %collective-permute-done.rest_0_), custom_call_target="tpu_custom_call" | custom-call | flops 1 | bytes 1 | tf_op jit(solution)/shard_map/far_partner/pallas_call | solution.py:134
  55.1 4.5 %far.1 = (f32[128,3072]{1,0:T(8,128)S(1)}, bf16[8,2,64,128]{3,2,1,0:T(8,128)(2,1)S(1)}) custom-call(s32[16,128]{1,0:T(8,128)S(1)} %copy-done, bf16[8,800,128]{2,1,0:T(8,128)(2,1)S(1)} %all-to-all-done.packed_ref, bf16[8,2,64,128]{3,2,1,0:T(8,128)(2,1)S(1)} %collective-permute-done.1.rest_0_), custom_call_target="tpu_custom_call" | custom-call | flops 1 | bytes 1 | tf_op jit(solution)/shard_map/far/pallas_call | solution.py:134
  59.7 2.1 %collective-permute-done.2.rest_0_ = bf16[8,2,64,128]{3,2,1,0:T(8,128)(2,1)S(1)} collective-permute-done((bf16[8,2,64,128]{3,2,1,0:T(8,128)(2,1)S(1)}, bf16[8,2,64,128]{3,2,1,0:T(8,128)(2,1)S(1)}, u32[]{:S(2)}, u32[]{:S(2)}) %collective-permute-start.2) | collective-permute-done | bytes 262176 | tf_op jit(solution)/shard_map/ppermute | solution.py:282
  61.8 3.9 %near_partner.1 = (f32[128,3072]{1,0:T(8,128)S(1)}, f32[8,2,64,128]{3,2,1,0:T(8,128)S(1)}) custom-call(s32[16,128]{1,0:T(8,128)S(1)} %copy-done, bf16[8,800,128]{2,1,0:T(8,128)(2,1)S(1)} %all-to-all-done.packed_ref, bf16[8,2,64,128]{3,2,1,0:T(8,128)(2,1)S(1)} %collective-permute-done.2.rest_0_, f32[128,3072]{1,0:T(8,128)S(1)} %get-tuple-element.39.rest_1_, ...), custom_call_target="tpu_custom_call" | custom-call | flops 1 | bytes 1 | tf_op jit(solution)/shard_map/near_partner/pallas_call | solution.py:134
  65.8 5.0 %collective-permute-start.4 = (bf16[8,2,64,128]{3,2,1,0:T(8,128)(2,1)S(1)}, bf16[8,2,64,128]{3,2,1,0:T(8,128)(2,1)S(1)}, u32[]{:S(2)}, u32[]{:S(2)}) collective-permute-start(bf16[8,2,64,128]{3,2,1,0:T(8,128)(2,1)S(1)} %add_convert_fusion), channel_id=1, source_target_pairs={{16,0},{17,1},{18,2},{19,3},{20,4},{21,5},{22,6},{23,7},{24,8},{25... | collective-permute-start | bytes 786440 | tf_op jit(solution)/shard_map/ppermute | solution.py:336
  70.8 6.6 %near.1 = (bf16[8,6,64,128]{3,2,1,0:T(8,128)(2,1)}, f32[8,2,64,128]{3,2,1,0:T(8,128)S(1)}) custom-call(s32[16,128]{1,0:T(8,128)S(1)} %copy-done, bf16[8,800,128]{2,1,0:T(8,128)(2,1)S(1)} %all-to-all-done.packed_ref, bf16[8,2,64,128]{3,2,1,0:T(8,128)(2,1)S(1)} %all-to-all-done.1.rest_0_, f32[128,3072]{1,0:T(8,128)S(1)} %get-tuple-element.44.rest_1_), custom_call_target="tpu_custom_call" | custom-call | flops 1 | bytes 1 | tf_op jit(solution)/shard_map/near/pallas_call | solution.py:134
  77.4 0.8 copy-done.1
  78.2 4.1 %all-to-all-start.2 = ((bf16[8,6,64,128]{3,2,1,0:T(8,128)(2,1)}), bf16[8,6,64,128]{3,2,1,0:T(8,128)(2,1)S(1)}, u32[]{:S(2)}, u32[]{:S(2)}) async-start(bf16[8,6,64,128]{3,2,1,0:T(8,128)(2,1)} %get-tuple-element.45), calls=%async_computation.2 | async-start | bytes 1572864 | tf_op jit(solution)/shard_map/all_to_all | solution.py:273
  82.3 1.9 %collective-permute-done.4.refs_1_ = bf16[8,2,64,128]{3,2,1,0:T(8,128)(2,1)S(1)} collective-permute-done((bf16[8,2,64,128]{3,2,1,0:T(8,128)(2,1)S(1)}, bf16[8,2,64,128]{3,2,1,0:T(8,128)(2,1)S(1)}, u32[]{:S(2)}, u32[]{:S(2)}) %collective-permute-start.4) | collective-permute-done | bytes 262176 | tf_op jit(solution)/shard_map/ppermute | solution.py:336
  84.9 1.9 %add_by_peer.1 = (bf16[2,64,128]{2,1,0:T(8,128)(2,1)}, bf16[2,64,128]{2,1,0:T(8,128)(2,1)}, bf16[2,64,128]{2,1,0:T(8,128)(2,1)}, bf16[2,64,128]{2,1,0:T(8,128)(2...) custom-call(f32[8,2,64,128]{3,2,1,0:T(8,128)} %copy-done.1, ...), custom_call_target="tpu_custom_call" | custom-call | flops 10000000000 | bytes 1 | tf_op jit(solution)/shard_map/add_by_peer/pallas_call | solution.py:157
  87.4 1.3 %collective-permute-start.8 = (bf16[2,64,128]{2,1,0:T(8,128)(2,1)}, bf16[2,64,128]{2,1,0:T(8,128)(2,1)S(1)}, u32[]{:S(2)}, u32[]{:S(2)}) collective-permute-start(bf16[2,64,128]{2,1,0:T(8,128)(2,1)} %get-tuple-element.53), channel_id=1, source_target_pairs={{0,96},{32,64},{64,32},{96,0},{128,224},{160,192},{192,160},{224,1... | collective-permute-start | bytes 98312 | tf_op jit(solution)/shard_map/ppermute | solution.py:322
  88.7 2.0 %collective-permute-start.9 = (bf16[2,64,128]{2,1,0:T(8,128)(2,1)}, bf16[2,64,128]{2,1,0:T(8,128)(2,1)S(1)}, u32[]{:S(2)}, u32[]{:S(2)}) collective-permute-start(bf16[2,64,128]{2,1,0:T(8,128)(2,1)} %get-tuple-element.54), channel_id=1, source_target_pairs={{0,128},{32,160},{64,192},{96,224},{128,0},{160,32},{192,64},{224,... | collective-permute-start | bytes 98312 | tf_op jit(solution)/shard_map/ppermute | solution.py:322
  90.7 1.2 %collective-permute-start.10 = (bf16[2,64,128]{2,1,0:T(8,128)(2,1)}, bf16[2,64,128]{2,1,0:T(8,128)(2,1)S(1)}, u32[]{:S(2)}, u32[]{:S(2)}) collective-permute-start(bf16[2,64,128]{2,1,0:T(8,128)(2,1)} %get-tuple-element.55), channel_id=1, source_target_pairs={{0,160},{32,128},{64,224},{96,192},{128,32},{160,0},{192,96},{224,... | collective-permute-start | bytes 98312 | tf_op jit(solution)/shard_map/ppermute | solution.py:322
  91.9 1.7 %collective-permute-start.11 = (bf16[2,64,128]{2,1,0:T(8,128)(2,1)}, bf16[2,64,128]{2,1,0:T(8,128)(2,1)S(1)}, u32[]{:S(2)}, u32[]{:S(2)}) collective-permute-start(bf16[2,64,128]{2,1,0:T(8,128)(2,1)} %get-tuple-element.56), channel_id=1, source_target_pairs={{0,192},{32,224},{64,128},{96,160},{128,64},{160,96},{192,0},{224,... | collective-permute-start | bytes 98312 | tf_op jit(solution)/shard_map/ppermute | solution.py:322
  93.6 1.5 %collective-permute-done.7.refs_2_ = bf16[2,64,128]{2,1,0:T(8,128)(2,1)S(1)} collective-permute-done((bf16[2,64,128]{2,1,0:T(8,128)(2,1)}, bf16[2,64,128]{2,1,0:T(8,128)(2,1)S(1)}, u32[]{:S(2)}, u32[]{:S(2)}) %collective-permute-start.7) | collective-permute-done | bytes 32800 | tf_op jit(solution)/shard_map/ppermute | solution.py:322
  95.1 0.8 collective-permute-start.12
  95.9 1.4 %copy.32 = bf16[48,64,128]{2,0,1:T(8,128)(2,1)} copy(bf16[48,64,128]{2,1,0:T(8,128)(2,1)S(1)} %bitcast.28) | data formatting | bytes 1572864 | tf_op jit(solution)/shard_map/reshape | solution.py:340
  98.5 1.4 %collective-permute-done.12.refs_7_ = bf16[2,64,128]{2,1,0:T(8,128)(2,1)S(1)} collective-permute-done((bf16[2,64,128]{2,1,0:T(8,128)(2,1)}, bf16[2,64,128]{2,1,0:T(8,128)(2,1)S(1)}, u32[]{:S(2)}, u32[]{:S(2)}) %collective-permute-start.12) | collective-permute-done | bytes 32800 | tf_op jit(solution)/shard_map/ppermute | solution.py:322
  100.5 1.9 %gather_grads.1 = (bf16[64,8,128]{2,1,0:T(8,128)(2,1)}, bf16[64,8,128]{2,1,0:T(8,128)(2,1)}) custom-call(bf16[2,64,128]{2,1,0:T(8,128)(2,1)} %get-tuple-element.59.refs_0_, bf16[2,64,128]{2,1,0:T(8,128)(2,1)} %copy-done.5, bf16[2,64,128]{2,1,0:T(8,128)(2,1)} %copy-done.6, bf16[2,64,128]{2,1,0:T(8,128)(2,1)} %copy-done.7, bf16[2,64,128]{2,1,0:T(8,128)(2,1)} %copy-done.8, ...), custom_call_target="tpu_custom_call" | custom-call | tf_op jit(solution)/shard_map/gather_grads/pallas_call | solution.py:182
  (53 shorter events, 4.5 us)
Async XLA Ops:
  0.6 10.1 %copy-start.2 = (bf16[64,48,128]{2,1,0:T(8,128)(2,1)S(1)}, bf16[64,48,128]{2,1,0:T(8,128)(2,1)}, u32[]{:S(2)}) copy-start(bf16[64,48,128]{2,1,0:T(8,128)(2,1)} %param.11) | copy-start | bytes 2359300
  0.6 10.3 %copy-start.3 = (bf16[64,48,128]{2,1,0:T(8,128)(2,1)S(1)}, bf16[64,48,128]{2,1,0:T(8,128)(2,1)}, u32[]{:S(2)}) copy-start(bf16[64,48,128]{2,1,0:T(8,128)(2,1)} %param.10) | copy-start | bytes 2359300
  2.5 12.0 %all-to-all-start.1 = ((bf16[8,2,64,128]{3,2,1,0:T(8,128)(2,1)}), bf16[8,2,64,128]{3,2,1,0:T(8,128)(2,1)S(1)}, u32[]{:S(2)}, u32[]{:S(2)}) async-start(bf16[8,2,64,128]{3,2,1,0:T(8,128)(2,1)} %pad_maximum_fusion.1), calls=%async_computation.1 | async-start | bytes 524288 | tf_op jit(solution)/shard_map/all_to_all | solution.py:273
  10.7 1.1 %copy-start.4 = (bf16[64,48,128]{2,1,0:T(8,128)(2,1)S(1)}, bf16[64,48,128]{2,1,0:T(8,128)(2,1)}, u32[]{:S(2)}) copy-start(bf16[64,48,128]{2,1,0:T(8,128)(2,1)} %param.7) | copy-start | bytes 2359300
  13.4 36.4 %copy-start = (s32[16,128]{1,0:T(8,128)S(1)}, s32[16,128]{1,0:T(8,128)}, u32[]{:S(2)}) copy-start(s32[16,128]{1,0:T(8,128)} %order_tables.1.table) | copy-start | bytes 24580
  14.5 35.3 %all-to-all-start = ((bf16[8,800,128]{2,1,0:T(8,128)(2,1)}), bf16[8,800,128]{2,1,0:T(8,128)(2,1)S(1)}, u32[]{:S(2)}, u32[]{:S(2)}) async-start(bf16[8,800,128]{2,1,0:T(8,128)(2,1)} %pad_maximum_fusion), calls=%async_computation | async-start | bytes 3276800 | tf_op jit(solution)/shard_map/all_to_all | solution.py:273
  18.3 24.7 %collective-permute-start = (bf16[8,2,64,128]{3,2,1,0:T(8,128)(2,1)S(1)}, bf16[8,2,64,128]{3,2,1,0:T(8,128)(2,1)S(1)}, u32[]{:S(2)}, u32[]{:S(2)}) collective-permute-start(bf16[8,2,64,128]{3,2,1,0:T(8,128)(2,1)S(1)} %all-to-all-done.1.rest_0_), channel_id=1, source_target_pairs={{16,1},{17,2},{18,3},{19,4},{20,5},{21,6},{22,7},{23,8},{24,9},{25... | collective-permute-start | bytes 786440 | tf_op jit(solution)/shard_map/ppermute | solution.py:279
  25.6 29.6 %collective-permute-start.1 = (bf16[8,2,64,128]{3,2,1,0:T(8,128)(2,1)S(1)}, bf16[8,2,64,128]{3,2,1,0:T(8,128)(2,1)S(1)}, u32[]{:S(2)}, u32[]{:S(2)}) collective-permute-start(bf16[8,2,64,128]{3,2,1,0:T(8,128)(2,1)S(1)} %all-to-all-done.1.rest_0_), channel_id=1, source_target_pairs={{0,1},{1,2},{2,3},{3,4},{4,5},{5,6},{6,7},{7,8},{8,9},{9,10},{10,1... | collective-permute-start | bytes 786440 | tf_op jit(solution)/shard_map/ppermute | solution.py:280
  43.1 18.7 %collective-permute-start.2 = (bf16[8,2,64,128]{3,2,1,0:T(8,128)(2,1)S(1)}, bf16[8,2,64,128]{3,2,1,0:T(8,128)(2,1)S(1)}, u32[]{:S(2)}, u32[]{:S(2)}) collective-permute-start(bf16[8,2,64,128]{3,2,1,0:T(8,128)(2,1)S(1)} %all-to-all-done.1.rest_0_), channel_id=1, source_target_pairs={{16,0},{17,1},{18,2},{19,3},{20,4},{21,5},{22,6},{23,7},{24,8},{25... | collective-permute-start | bytes 786440 | tf_op jit(solution)/shard_map/ppermute | solution.py:282
  55.0 10.7 %collective-permute-start.3 = (bf16[8,2,64,128]{3,2,1,0:T(8,128)(2,1)S(1)}, bf16[8,2,64,128]{3,2,1,0:T(8,128)(2,1)S(1)}, u32[]{:S(2)}, u32[]{:S(2)}) collective-permute-start(bf16[8,2,64,128]{3,2,1,0:T(8,128)(2,1)S(1)} %get-tuple-element.48), channel_id=1, source_target_pairs={{1,0},{2,1},{3,2},{4,3},{5,4},{6,5},{7,6},{8,7},{9,8},{10,9},{11,1... | collective-permute-start | bytes 786440 | tf_op jit(solution)/shard_map/ppermute | solution.py:327
  59.7 22.6 %collective-permute-start.5 = (bf16[8,2,64,128]{3,2,1,0:T(8,128)(2,1)S(1)}, bf16[8,2,64,128]{3,2,1,0:T(8,128)(2,1)S(1)}, u32[]{:S(2)}, u32[]{:S(2)}) collective-permute-start(bf16[8,2,64,128]{3,2,1,0:T(8,128)(2,1)S(1)} %get-tuple-element.49), channel_id=1, source_target_pairs={{1,0},{2,1},{3,2},{4,3},{5,4},{6,5},{7,6},{8,7},{9,8},{10,9},{11,1... | collective-permute-start | bytes 786440 | tf_op jit(solution)/shard_map/ppermute | solution.py:331
  65.8 18.4 %collective-permute-start.4 = (bf16[8,2,64,128]{3,2,1,0:T(8,128)(2,1)S(1)}, bf16[8,2,64,128]{3,2,1,0:T(8,128)(2,1)S(1)}, u32[]{:S(2)}, u32[]{:S(2)}) collective-permute-start(bf16[8,2,64,128]{3,2,1,0:T(8,128)(2,1)S(1)} %add_convert_fusion), channel_id=1, source_target_pairs={{16,0},{17,1},{18,2},{19,3},{20,4},{21,5},{22,6},{23,7},{24,8},{25... | collective-permute-start | bytes 786440 | tf_op jit(solution)/shard_map/ppermute | solution.py:336
  77.4 0.8 copy-start.1
  78.2 17.8 %all-to-all-start.2 = ((bf16[8,6,64,128]{3,2,1,0:T(8,128)(2,1)}), bf16[8,6,64,128]{3,2,1,0:T(8,128)(2,1)S(1)}, u32[]{:S(2)}, u32[]{:S(2)}) async-start(bf16[8,6,64,128]{3,2,1,0:T(8,128)(2,1)} %get-tuple-element.45), calls=%async_computation.2 | async-start | bytes 1572864 | tf_op jit(solution)/shard_map/all_to_all | solution.py:273
  82.3 1.9 %copy-start.12 = (bf16[8,2,64,128]{3,2,1,0:T(8,128)(2,1)}, bf16[8,2,64,128]{3,2,1,0:T(8,128)(2,1)S(1)}, u32[]{:S(2)}) copy-start(bf16[8,2,64,128]{3,2,1,0:T(8,128)(2,1)S(1)} %collective-permute-done.5.refs_2_) | copy-start | bytes 786436
  84.2 0.7 copy-start.13
  86.8 5.1 %collective-permute-start.6 = (bf16[2,64,128]{2,1,0:T(8,128)(2,1)}, bf16[2,64,128]{2,1,0:T(8,128)(2,1)S(1)}, u32[]{:S(2)}, u32[]{:S(2)}) collective-permute-start(bf16[2,64,128]{2,1,0:T(8,128)(2,1)} %get-tuple-element.51), channel_id=1, source_target_pairs={{0,32},{32,0},{64,96},{96,64},{128,160},{160,128},{192,224},{224,1... | collective-permute-start | bytes 98312 | tf_op jit(solution)/shard_map/ppermute | solution.py:322
  86.8 8.3 %collective-permute-start.7 = (bf16[2,64,128]{2,1,0:T(8,128)(2,1)}, bf16[2,64,128]{2,1,0:T(8,128)(2,1)S(1)}, u32[]{:S(2)}, u32[]{:S(2)}) collective-permute-start(bf16[2,64,128]{2,1,0:T(8,128)(2,1)} %get-tuple-element.52), channel_id=1, source_target_pairs={{0,64},{32,96},{64,0},{96,32},{128,192},{160,224},{192,128},{224,1... | collective-permute-start | bytes 98312 | tf_op jit(solution)/shard_map/ppermute | solution.py:322
  87.4 9.9 %collective-permute-start.8 = (bf16[2,64,128]{2,1,0:T(8,128)(2,1)}, bf16[2,64,128]{2,1,0:T(8,128)(2,1)S(1)}, u32[]{:S(2)}, u32[]{:S(2)}) collective-permute-start(bf16[2,64,128]{2,1,0:T(8,128)(2,1)} %get-tuple-element.53), channel_id=1, source_target_pairs={{0,96},{32,64},{64,32},{96,0},{128,224},{160,192},{192,160},{224,1... | collective-permute-start | bytes 98312 | tf_op jit(solution)/shard_map/ppermute | solution.py:322
  88.7 9.3 %collective-permute-start.9 = (bf16[2,64,128]{2,1,0:T(8,128)(2,1)}, bf16[2,64,128]{2,1,0:T(8,128)(2,1)S(1)}, u32[]{:S(2)}, u32[]{:S(2)}) collective-permute-start(bf16[2,64,128]{2,1,0:T(8,128)(2,1)} %get-tuple-element.54), channel_id=1, source_target_pairs={{0,128},{32,160},{64,192},{96,224},{128,0},{160,32},{192,64},{224,... | collective-permute-start | bytes 98312 | tf_op jit(solution)/shard_map/ppermute | solution.py:322
  90.7 7.3 %collective-permute-start.10 = (bf16[2,64,128]{2,1,0:T(8,128)(2,1)}, bf16[2,64,128]{2,1,0:T(8,128)(2,1)S(1)}, u32[]{:S(2)}, u32[]{:S(2)}) collective-permute-start(bf16[2,64,128]{2,1,0:T(8,128)(2,1)} %get-tuple-element.55), channel_id=1, source_target_pairs={{0,160},{32,128},{64,224},{96,192},{128,32},{160,0},{192,96},{224,... | collective-permute-start | bytes 98312 | tf_op jit(solution)/shard_map/ppermute | solution.py:322
  91.9 8.0 %copy-start.5 = (bf16[2,64,128]{2,1,0:T(8,128)(2,1)}, bf16[2,64,128]{2,1,0:T(8,128)(2,1)S(1)}, u32[]{:S(2)}) copy-start(bf16[2,64,128]{2,1,0:T(8,128)(2,1)S(1)} %collective-permute-done.6.refs_1_) | copy-start | bytes 98308
  91.9 6.6 %collective-permute-start.11 = (bf16[2,64,128]{2,1,0:T(8,128)(2,1)}, bf16[2,64,128]{2,1,0:T(8,128)(2,1)S(1)}, u32[]{:S(2)}, u32[]{:S(2)}) collective-permute-start(bf16[2,64,128]{2,1,0:T(8,128)(2,1)} %get-tuple-element.56), channel_id=1, source_target_pairs={{0,192},{32,224},{64,128},{96,160},{128,64},{160,96},{192,0},{224,... | collective-permute-start | bytes 98312 | tf_op jit(solution)/shard_map/ppermute | solution.py:322
  95.1 4.8 %copy-start.6 = (bf16[2,64,128]{2,1,0:T(8,128)(2,1)}, bf16[2,64,128]{2,1,0:T(8,128)(2,1)S(1)}, u32[]{:S(2)}) copy-start(bf16[2,64,128]{2,1,0:T(8,128)(2,1)S(1)} %collective-permute-done.7.refs_2_) | copy-start | bytes 98308
  95.1 4.8 %collective-permute-start.12 = (bf16[2,64,128]{2,1,0:T(8,128)(2,1)}, bf16[2,64,128]{2,1,0:T(8,128)(2,1)S(1)}, u32[]{:S(2)}, u32[]{:S(2)}) collective-permute-start(bf16[2,64,128]{2,1,0:T(8,128)(2,1)} %get-tuple-element.57), channel_id=1, source_target_pairs={{0,224},{32,192},{64,160},{96,128},{128,96},{160,64},{192,32},{224... | collective-permute-start | bytes 98312 | tf_op jit(solution)/shard_map/ppermute | solution.py:322
  97.3 2.5 %copy-start.7 = (bf16[2,64,128]{2,1,0:T(8,128)(2,1)}, bf16[2,64,128]{2,1,0:T(8,128)(2,1)S(1)}, u32[]{:S(2)}) copy-start(bf16[2,64,128]{2,1,0:T(8,128)(2,1)S(1)} %collective-permute-done.8.refs_3_) | copy-start | bytes 98308
  98.0 1.9 %copy-start.8 = (bf16[2,64,128]{2,1,0:T(8,128)(2,1)}, bf16[2,64,128]{2,1,0:T(8,128)(2,1)S(1)}, u32[]{:S(2)}) copy-start(bf16[2,64,128]{2,1,0:T(8,128)(2,1)S(1)} %collective-permute-done.9.refs_4_) | copy-start | bytes 98308
  98.0 1.9 %copy-start.9 = (bf16[2,64,128]{2,1,0:T(8,128)(2,1)}, bf16[2,64,128]{2,1,0:T(8,128)(2,1)S(1)}, u32[]{:S(2)}) copy-start(bf16[2,64,128]{2,1,0:T(8,128)(2,1)S(1)} %collective-permute-done.10.refs_5_) | copy-start | bytes 98308
  98.5 1.4 %copy-start.10 = (bf16[2,64,128]{2,1,0:T(8,128)(2,1)}, bf16[2,64,128]{2,1,0:T(8,128)(2,1)S(1)}, u32[]{:S(2)}) copy-start(bf16[2,64,128]{2,1,0:T(8,128)(2,1)S(1)} %collective-permute-done.11.refs_6_) | copy-start | bytes 98308
  99.9 0.6 copy-start.11

commit v3 on v2

--- a/solution.py
+++ b/solution.py
@@ -10,6 +10,7 @@
 LOG2E = math.log2(math.e)
 NT = (((1,), (1,)), ((), ()))
 NN = (((1,), (0,)), ((), ()))
+PARAMS = pltpu.CompilerParams(vmem_limit_bytes=32 * 2**20)
 f32 = jnp.float32
 bf16 = jnp.bfloat16
 
@@ -106,14 +107,21 @@
             for c in range(many):
                 g_refs[c][...] = g_s[c * src : (c + 1) * src].astype(g_refs[c].dtype)
         if last:
+            stage, sems = rest[1:]
+            copies = []
             for j in range(src):
-                at = pl.ds(j * R, R)
-                out_ref[table[0, j]] = (dq_s[:, at].T * scale).astype(bf16).reshape(heads, T, D)
+                stage[j] = (dq_s[:, j * R : (j + 1) * R].T * scale).astype(bf16)
+                copies.append(
+                    pltpu.make_async_copy(stage.at[j], out_ref.at[table[0, j]], sems.at[j])
+                )
+                copies[-1].start()
+            for copy in copies:
+                copy.wait()
 
     smem = pl.BlockSpec(memory_space=pltpu.SMEM)
     vmem = pl.BlockSpec(memory_space=pltpu.VMEM)
     if last:
-        dq_out = jax.ShapeDtypeStruct((src, heads, T, D), bf16)
+        dq_out = jax.ShapeDtypeStruct((src, R, D), bf16)
     else:
         dq_out = jax.ShapeDtypeStruct((D, src * R), f32)
     g_outs = [jax.ShapeDtypeStruct((src, 2, T, D), t) for t in g_types]
@@ -129,15 +137,19 @@
         pltpu.VMEM((U, D), f32),
     ]
     if last:
-        scratch.append(pltpu.VMEM((D, src * R), f32))
+        scratch += [
+            pltpu.VMEM((D, src * R), f32),
+            pltpu.VMEM((src, R, D), bf16),
+            pltpu.SemaphoreType.DMA((src,)),
+        ]
     arrays = [packed, *contexts, *dq_starts]
     return pl.pallas_call(
         body,
         out_shape=(dq_out, *g_outs),
         in_specs=[smem] + [vmem] * len(arrays),
-        out_specs=(vmem,) * (1 + many),
+        out_specs=(pl.BlockSpec(memory_space=pltpu.HBM) if last else vmem,) + (vmem,) * many,
         scratch_shapes=scratch,
-        compiler_params=pltpu.CompilerParams(vmem_limit_bytes=32 * 2**20),
+        compiler_params=PARAMS,
         cost_estimate=pl.CostEstimate(flops=1, bytes_accessed=1, transcendentals=0),
         name=name,
     )(tables, *arrays)
@@ -160,6 +172,7 @@
         in_specs=[vmem] * len(arrays),
         out_specs=[vmem] * src,
         cost_estimate=pl.CostEstimate(flops=10**10, bytes_accessed=1, transcendentals=0),
+        compiler_params=PARAMS,
         name="add_by_peer",
     )(*arrays)
 
@@ -185,6 +198,7 @@
         in_specs=[vmem] * src,
         out_specs=[vmem] * 2,
         scratch_shapes=[pltpu.VMEM((src, 2, T, D), bf16), pltpu.VMEM((T, src, D), f32)],
+        compiler_params=PARAMS,
         name="gather_grads",
     )(*pieces)
 
@@ -193,22 +207,16 @@
     wide = 128
 
     def body(order_ref, out_ref):
-        table = order_ref[...]
-        sub = lax.broadcasted_iota(jnp.int32, table.shape, 0)
-        spot = lax.broadcasted_iota(jnp.int32, table.shape, 1)
-
         def sort(spots):
             n = heads * len(spots)
-            down = jnp.concatenate(
-                [
-                    jnp.sum(jnp.where(spot == a * outers + b, table, 0), axis=1, keepdims=True)
-                    for a, b in spots
-                ],
-                axis=0,
-            )
             s = lax.broadcasted_iota(jnp.int32, (n, wide), 0)
             lane = lax.broadcasted_iota(jnp.int32, (n, wide), 1)
-            across = jnp.sum(jnp.where(s == lane, down, 0), axis=0, keepdims=True)
+            down, across = jnp.zeros_like(s), jnp.zeros_like(s)
+            for c, (a, b) in enumerate(spots):
+                for h in range(heads):
+                    place = order_ref[(h * inners + a) * outers + b]
+                    down = jnp.where(s == c * heads + h, place, down)
+                    across = jnp.where(lane == c * heads + h, place, across)
             ahead = jnp.where((across > down) & (lane < n), 1, 0)
             hit = jnp.sum(ahead, axis=1, keepdims=True) == lane
             ids = jnp.sum(jnp.where(hit, s, 0), axis=0, keepdims=True)
@@ -234,14 +242,14 @@
         rows.append(jnp.zeros((16 - len(rows), wide), jnp.int32))
         out_ref[...] = jnp.concatenate(rows, axis=0)
 
-    vmem = pl.BlockSpec(memory_space=pltpu.VMEM)
     return pl.pallas_call(
         body,
         out_shape=jax.ShapeDtypeStruct((16, wide), jnp.int32),
-        in_specs=[vmem],
-        out_specs=vmem,
+        in_specs=[pl.BlockSpec(memory_space=pltpu.SMEM)],
+        out_specs=pl.BlockSpec(memory_space=pltpu.VMEM),
+        compiler_params=PARAMS,
         name="order_tables",
-    )(block_order.reshape(heads, inners * outers))
+    )(block_order)
 
 
 def pieces(x):

time: 103 us -> 99.4 us (0.965)
  local copies, waits for them, and re-layouts: 6.72 us -> 3.95 us
  starting transfers between devices: 40.6 us -> 38.4 us
  waiting for transfers between devices: 25.2 us -> 26.8 us
    ppermute x1, starting transfers between devices: 5.02 us -> 2.24 us  [shards(): partner = lax.ppermute(partner, ring, swap)]
    pallas_call x4, Pallas kernels: 20.2 us -> 22.7 us  [attention_part(): pl.pallas_call(body, out_shape=(dq_out, *g_outs), in_specs=[smem] + [vmem...]
    ppermute x1, waiting for transfers between devices: 1.9 us -> 4.19 us  [shards(): partner = lax.ppermute(partner, ring, swap)]
    pallas_call x1, Pallas kernels: 1.92 us -> 0.08 us  [add_by_peer(): pl.pallas_call(body, out_shape=[jax.ShapeDtypeStruct(rest, bf16)] * src,...]
    ppermute x1, waiting for transfers between devices: 2.08 us -> 0.63 us  [shards(): kv_partner = lax.ppermute(kv_after, ring, swap)]
    all_to_all x3, waiting for transfers between devices: 1.14 us -> 2.58 us  [exchange(): return lax.all_to_all(x, 'head', split_axis=0, concat_axis=0, tiled=True)]
    unnamed x30 -> x10, local copies, waits for them, and re-layouts: 2.7 us -> 1.26 us
    reshape x1 -> x0, local copies, waits for them, and re-layouts: 1.35 us -> none  [order_tables(): block_order.reshape(heads, inners * outers)]
  transfers between devices with their start and end apart: 16 -> 16, of which waited for: 8 -> 7; matrix products, arithmetic and copies ran while one was open for 6% -> 5% of each run, Pallas kernels for 23% -> 24%
where the time goes in v3:
time: 99.4 us; the launch traced here: 98 us
  starting transfers between devices  38.4 us (39%)
  waiting for transfers between devices  26.8 us (27%)
  Pallas kernels  24.7 us (25%)
  local copies, waits for them, and re-layouts  3.95 us (4%)
  other arithmetic  3.38 us (3%)
    pallas_call x4, Pallas kernels, attention_part(): pl.pallas_call(body, out_shape=(dq_out, *g_outs), in_specs=[smem] + [vmem...  22.7 us
    ppermute x1, waiting for transfers between devices, shards(): kv_far_partner = lax.ppermute(kv, ring, across)  15.8 us
    all_to_all x3, starting transfers between devices, exchange(): return lax.all_to_all(x, 'head', split_axis=0, concat_axis=0, tiled=True)  12.3 us
    ppermute x7, starting transfers between devices, to_peers(): lax.ppermute(blocks[j], 'head', [(h, h ^ j) for h in range(heads)])  8.11 us
    ppermute x1, starting transfers between devices, shards(): kv_far_partner = lax.ppermute(kv, ring, across)  7.29 us
    ppermute x1, starting transfers between devices, shards(): kv_partner = lax.ppermute(kv_after, ring, swap)  6.75 us
    ppermute x1, waiting for transfers between devices, shards(): partner = lax.ppermute(partner, ring, swap)  4.19 us
    ppermute x7, waiting for transfers between devices, to_peers(): lax.ppermute(blocks[j], 'head', [(h, h ^ j) for h in range(heads)])  3.58 us
  transfers between devices with their start and end apart: 16, of which 7 were waited for; matrix products, arithmetic and copies ran while one was open for 5% of the time, Pallas kernels for 24%

profile of v3, /device:TPU:32, one launch (start us, length us, event | category | flops | bytes accessed | tf_op | source)
XLA Modules:
  0.0 98.0 jit_solution(16555722216360336667)
XLA Ops:
  0.7 1.1 %copy_bitcast_fusion.1 = (bf16[8,1,64,128]{3,2,1,0:T(8,128)(2,1)S(1)}, bf16[8,1,64,128]{3,2,1,0:T(8,128)(2,1)S(1)}) fusion(bf16[64,8,128]{2,1,0:T(8,128)(2,1)} %param.9, bf16[64,8,128]{2,1,0:T(8,128)(2,1)} %param.8), kind=kLoop, calls=%fused_computation.9 | loop fusion | bytes 524288 | tf_op jit(solution)/shard_map/transpose | solution.py:284
  1.8 0.7 pad_maximum_fusion.1
  2.5 4.5 %all-to-all-start.1 = ((bf16[8,2,64,128]{3,2,1,0:T(8,128)(2,1)}), bf16[8,2,64,128]{3,2,1,0:T(8,128)(2,1)S(1)}, u32[]{:S(2)}, u32[]{:S(2)}) async-start(bf16[8,2,64,128]{3,2,1,0:T(8,128)(2,1)} %pad_maximum_fusion.1), calls=%async_computation.1 | async-start | bytes 524288 | tf_op jit(solution)/shard_map/all_to_all | solution.py:281
  7.0 0.7 copy-done
  7.7 0.9 order_tables.1.table
  8.5 0.7 broadcast_multiply_fusion
  10.6 1.3 %pad_maximum_fusion = bf16[8,800,128]{2,1,0:T(8,128)(2,1)} fusion(bf16[8,32,128]{2,1,0:T(8,128)(2,1)S(1)} %fusion.4, bf16[8,384,128]{2,1,0:T(8,128)(2,1)S(1)} %bitcast.29, bf16[8,384,128]{2,1,0:T(8,128)(2,1)S(1)} %bitcast.30), kind=kLoop, calls=%fused_computation | loop fusion | flops 4915200 | bytes 3276800 | tf_op jit(solution)/shard_map/concatenate | solution.py:312
  11.9 2.6 %all-to-all-done.1.rest_0_ = bf16[8,2,64,128]{3,2,1,0:T(8,128)(2,1)S(1)} async-done(((bf16[8,2,64,128]{3,2,1,0:T(8,128)(2,1)}), bf16[8,2,64,128]{3,2,1,0:T(8,128)(2,1)S(1)}, u32[]{:S(2)}, u32[]{:S(2)}) %all-to-all-start.1) | async-done | bytes 262176 | tf_op jit(solution)/shard_map/all_to_all | solution.py:281
  14.5 3.6 %all-to-all-start = ((bf16[8,800,128]{2,1,0:T(8,128)(2,1)}), bf16[8,800,128]{2,1,0:T(8,128)(2,1)S(1)}, u32[]{:S(2)}, u32[]{:S(2)}) async-start(bf16[8,800,128]{2,1,0:T(8,128)(2,1)} %pad_maximum_fusion), calls=%async_computation | async-start | bytes 3276800 | tf_op jit(solution)/shard_map/all_to_all | solution.py:281
  18.1 7.3 %collective-permute-start = (bf16[8,2,64,128]{3,2,1,0:T(8,128)(2,1)S(1)}, bf16[8,2,64,128]{3,2,1,0:T(8,128)(2,1)S(1)}, u32[]{:S(2)}, u32[]{:S(2)}) collective-permute-start(bf16[8,2,64,128]{3,2,1,0:T(8,128)(2,1)S(1)} %all-to-all-done.1.rest_0_), channel_id=1, source_target_pairs={{16,1},{17,2},{18,3},{19,4},{20,5},{21,6},{22,7},{23,8},{24,9},{25... | collective-permute-start | bytes 786440 | tf_op jit(solution)/shard_map/ppermute | solution.py:287
  25.4 1.5 %collective-permute-start.1 = (bf16[8,2,64,128]{3,2,1,0:T(8,128)(2,1)S(1)}, bf16[8,2,64,128]{3,2,1,0:T(8,128)(2,1)S(1)}, u32[]{:S(2)}, u32[]{:S(2)}) collective-permute-start(bf16[8,2,64,128]{3,2,1,0:T(8,128)(2,1)S(1)} %all-to-all-done.1.rest_0_), channel_id=1, source_target_pairs={{0,1},{1,2},{2,3},{3,4},{4,5},{5,6},{6,7},{7,8},{8,9},{9,10},{10,1... | collective-permute-start | bytes 786440 | tf_op jit(solution)/shard_map/ppermute | solution.py:288
  26.9 15.8 %collective-permute-done.rest_0_ = bf16[8,2,64,128]{3,2,1,0:T(8,128)(2,1)S(1)} collective-permute-done((bf16[8,2,64,128]{3,2,1,0:T(8,128)(2,1)S(1)}, bf16[8,2,64,128]{3,2,1,0:T(8,128)(2,1)S(1)}, u32[]{:S(2)}, u32[]{:S(2)}) %collective-permute-start) | collective-permute-done | bytes 262176 | tf_op jit(solution)/shard_map/ppermute | solution.py:287
  42.8 6.7 %collective-permute-start.2 = (bf16[8,2,64,128]{3,2,1,0:T(8,128)(2,1)S(1)}, bf16[8,2,64,128]{3,2,1,0:T(8,128)(2,1)S(1)}, u32[]{:S(2)}, u32[]{:S(2)}) collective-permute-start(bf16[8,2,64,128]{3,2,1,0:T(8,128)(2,1)S(1)} %all-to-all-done.1.rest_0_), channel_id=1, source_target_pairs={{16,0},{17,1},{18,2},{19,3},{20,4},{21,5},{22,6},{23,7},{24,8},{25... | collective-permute-start | bytes 786440 | tf_op jit(solution)/shard_map/ppermute | solution.py:290
  49.5 5.2 %far_partner.1 = (f32[128,3072]{1,0:T(8,128)S(1)}, bf16[8,2,64,128]{3,2,1,0:T(8,128)(2,1)S(1)}) custom-call(s32[16,128]{1,0:T(8,128)S(1)} %order_tables.1.table, bf16[8,800,128]{2,1,0:T(8,128)(2,1)S(1)} %all-to-all-done.packed_ref, bf16[8,2,64,128]{3,2,1,0:T(8,128)(2,1)S(1)} %collective-permute-done.rest_0_), custom_call_target="tpu_custom_call" | custom-call | flops 1 | bytes 1 | tf_op jit(solution)/shard_map/far_partner/pallas_call | solution.py:146
  54.8 5.2 %far.1 = (f32[128,3072]{1,0:T(8,128)S(1)}, bf16[8,2,64,128]{3,2,1,0:T(8,128)(2,1)S(1)}) custom-call(s32[16,128]{1,0:T(8,128)S(1)} %order_tables.1.table, bf16[8,800,128]{2,1,0:T(8,128)(2,1)S(1)} %all-to-all-done.packed_ref, bf16[8,2,64,128]{3,2,1,0:T(8,128)(2,1)S(1)} %collective-permute-done.1.rest_0_), custom_call_target="tpu_custom_call" | custom-call | flops 1 | bytes 1 | tf_op jit(solution)/shard_map/far/pallas_call | solution.py:146
  60.1 0.6 collective-permute-done.2.rest_0_
  60.7 5.9 %near_partner.1 = (f32[128,3072]{1,0:T(8,128)S(1)}, f32[8,2,64,128]{3,2,1,0:T(8,128)S(1)}) custom-call(s32[16,128]{1,0:T(8,128)S(1)} %order_tables.1.table, bf16[8,800,128]{2,1,0:T(8,128)(2,1)S(1)} %all-to-all-done.packed_ref, bf16[8,2,64,128]{3,2,1,0:T(8,128)(2,1)S(1)} %collective-permute-done.2.rest_0_, f32[128,3072]{1,0:T(8,128)S(1)} %get-tuple-element.39.rest_1_, ...), custom_call_target="tpu_custom_call" | custom-call | flops 1 | bytes 1 | tf_op jit(solution)/shard_map/near_partner/pallas_call | solution.py:146
  66.8 2.2 %collective-permute-start.4 = (bf16[8,2,64,128]{3,2,1,0:T(8,128)(2,1)S(1)}, bf16[8,2,64,128]{3,2,1,0:T(8,128)(2,1)S(1)}, u32[]{:S(2)}, u32[]{:S(2)}) collective-permute-start(bf16[8,2,64,128]{3,2,1,0:T(8,128)(2,1)S(1)} %add_convert_fusion), channel_id=1, source_target_pairs={{16,0},{17,1},{18,2},{19,3},{20,4},{21,5},{22,6},{23,7},{24,8},{25... | collective-permute-start | bytes 786440 | tf_op jit(solution)/shard_map/ppermute | solution.py:344
  69.0 6.4 %near.1 = (bf16[8,384,128]{2,1,0:T(8,128)(2,1)}, f32[8,2,64,128]{3,2,1,0:T(8,128)S(1)}) custom-call(s32[16,128]{1,0:T(8,128)S(1)} %order_tables.1.table, bf16[8,800,128]{2,1,0:T(8,128)(2,1)S(1)} %all-to-all-done.packed_ref, bf16[8,2,64,128]{3,2,1,0:T(8,128)(2,1)S(1)} %all-to-all-done.1.rest_0_, f32[128,3072]{1,0:T(8,128)S(1)} %get-tuple-element.44.rest_1_), custom_call_target="tpu_custom_call" | custom-call | flops 1 | bytes 1 | tf_op jit(solution)/shard_map/near/pallas_call | solution.py:146
  75.4 4.2 %all-to-all-start.2 = ((bf16[8,384,128]{2,1,0:T(8,128)(2,1)}), bf16[8,384,128]{2,1,0:T(8,128)(2,1)S(1)}, u32[]{:S(2)}, u32[]{:S(2)}) async-start(bf16[8,384,128]{2,1,0:T(8,128)(2,1)} %get-tuple-element.45), calls=%async_computation.2 | async-start | bytes 1572864 | tf_op jit(solution)/shard_map/all_to_all | solution.py:281
  79.6 4.2 %collective-permute-done.4.refs_1_ = bf16[8,2,64,128]{3,2,1,0:T(8,128)(2,1)S(1)} collective-permute-done((bf16[8,2,64,128]{3,2,1,0:T(8,128)(2,1)S(1)}, bf16[8,2,64,128]{3,2,1,0:T(8,128)(2,1)S(1)}, u32[]{:S(2)}, u32[]{:S(2)}) %collective-permute-start.4) | collective-permute-done | bytes 262176 | tf_op jit(solution)/shard_map/ppermute | solution.py:344
  84.0 1.2 %collective-permute-start.7 = (bf16[2,64,128]{2,1,0:T(8,128)(2,1)S(1)}, bf16[2,64,128]{2,1,0:T(8,128)(2,1)S(1)}, u32[]{:S(2)}, u32[]{:S(2)}) collective-permute-start(bf16[2,64,128]{2,1,0:T(8,128)(2,1)S(1)} %get-tuple-element.52), channel_id=1, source_target_pairs={{0,64},{32,96},{64,0},{96,32},{128,192},{160,224},{192,128},{224,1... | collective-permute-start | bytes 98312 | tf_op jit(solution)/shard_map/ppermute | solution.py:330
  85.2 0.7 collective-permute-start.8
  85.9 2.4 %collective-permute-start.9 = (bf16[2,64,128]{2,1,0:T(8,128)(2,1)S(1)}, bf16[2,64,128]{2,1,0:T(8,128)(2,1)S(1)}, u32[]{:S(2)}, u32[]{:S(2)}) collective-permute-start(bf16[2,64,128]{2,1,0:T(8,128)(2,1)S(1)} %get-tuple-element.54), channel_id=1, source_target_pairs={{0,128},{32,160},{64,192},{96,224},{128,0},{160,32},{192,64},{224,... | collective-permute-start | bytes 98312 | tf_op jit(solution)/shard_map/ppermute | solution.py:330
  88.3 0.8 collective-permute-start.10
  89.1 2.1 %collective-permute-start.11 = (bf16[2,64,128]{2,1,0:T(8,128)(2,1)S(1)}, bf16[2,64,128]{2,1,0:T(8,128)(2,1)S(1)}, u32[]{:S(2)}, u32[]{:S(2)}) collective-permute-start(bf16[2,64,128]{2,1,0:T(8,128)(2,1)S(1)} %get-tuple-element.56), channel_id=1, source_target_pairs={{0,192},{32,224},{64,128},{96,160},{128,64},{160,96},{192,0},{224,... | collective-permute-start | bytes 98312 | tf_op jit(solution)/shard_map/ppermute | solution.py:330
  91.2 1.3 %collective-permute-done.7.refs_2_ = bf16[2,64,128]{2,1,0:T(8,128)(2,1)S(1)} collective-permute-done((bf16[2,64,128]{2,1,0:T(8,128)(2,1)S(1)}, bf16[2,64,128]{2,1,0:T(8,128)(2,1)S(1)}, u32[]{:S(2)}, u32[]{:S(2)}) %collective-permute-start.7) | collective-permute-done | bytes 32800 | tf_op jit(solution)/shard_map/ppermute | solution.py:330
  92.5 0.8 collective-permute-start.12
  93.3 1.4 %copy.32 = bf16[48,64,128]{2,0,1:T(8,128)(2,1)} copy(bf16[48,64,128]{2,1,0:T(8,128)(2,1)S(1)} %bitcast.28) | data formatting | bytes 1572864 | tf_op jit(solution)/shard_map/reshape | solution.py:348
  94.7 0.6 collective-permute-done.9.refs_4_
  95.3 1.8 %collective-permute-done.12.refs_7_ = bf16[2,64,128]{2,1,0:T(8,128)(2,1)S(1)} collective-permute-done((bf16[2,64,128]{2,1,0:T(8,128)(2,1)S(1)}, bf16[2,64,128]{2,1,0:T(8,128)(2,1)S(1)}, u32[]{:S(2)}, u32[]{:S(2)}) %collective-permute-start.12) | collective-permute-done | bytes 32800 | tf_op jit(solution)/shard_map/ppermute | solution.py:330
  97.0 1.0 %gather_grads.1 = (bf16[64,8,128]{2,1,0:T(8,128)(2,1)}, bf16[64,8,128]{2,1,0:T(8,128)(2,1)}) custom-call(bf16[2,64,128]{2,1,0:T(8,128)(2,1)S(1)} %get-tuple-element.59.refs_0_, bf16[2,64,128]{2,1,0:T(8,128)(2,1)S(1)} %collective-permute-done.6.refs_1_, bf16[2,64,128]{2,1,0:T(8,128)(2,1)S(1)} %collective-permute-done.7.refs_2_, ...), custom_call_target="tpu_custom_call" | custom-call | tf_op jit(solution)/shard_map/gather_grads/pallas_call | solution.py:195
  (32 shorter events, 1.7 us)
Async XLA Ops:
  0.6 8.7 %copy-start.1 = (bf16[64,48,128]{2,1,0:T(8,128)(2,1)S(1)}, bf16[64,48,128]{2,1,0:T(8,128)(2,1)}, u32[]{:S(2)}) copy-start(bf16[64,48,128]{2,1,0:T(8,128)(2,1)} %param.11) | copy-start | bytes 2359300
  0.6 8.9 %copy-start.2 = (bf16[64,48,128]{2,1,0:T(8,128)(2,1)S(1)}, bf16[64,48,128]{2,1,0:T(8,128)(2,1)}, u32[]{:S(2)}) copy-start(bf16[64,48,128]{2,1,0:T(8,128)(2,1)} %param.10) | copy-start | bytes 2359300
  2.5 12.0 %all-to-all-start.1 = ((bf16[8,2,64,128]{3,2,1,0:T(8,128)(2,1)}), bf16[8,2,64,128]{3,2,1,0:T(8,128)(2,1)S(1)}, u32[]{:S(2)}, u32[]{:S(2)}) async-start(bf16[8,2,64,128]{3,2,1,0:T(8,128)(2,1)} %pad_maximum_fusion.1), calls=%async_computation.1 | async-start | bytes 524288 | tf_op jit(solution)/shard_map/all_to_all | solution.py:281
  7.0 0.7 copy-start
  9.3 1.1 %copy-start.3 = (bf16[64,48,128]{2,1,0:T(8,128)(2,1)S(1)}, bf16[64,48,128]{2,1,0:T(8,128)(2,1)}, u32[]{:S(2)}) copy-start(bf16[64,48,128]{2,1,0:T(8,128)(2,1)} %param.7) | copy-start | bytes 2359300
  14.5 35.0 %all-to-all-start = ((bf16[8,800,128]{2,1,0:T(8,128)(2,1)}), bf16[8,800,128]{2,1,0:T(8,128)(2,1)S(1)}, u32[]{:S(2)}, u32[]{:S(2)}) async-start(bf16[8,800,128]{2,1,0:T(8,128)(2,1)} %pad_maximum_fusion), calls=%async_computation | async-start | bytes 3276800 | tf_op jit(solution)/shard_map/all_to_all | solution.py:281
  18.1 24.6 %collective-permute-start = (bf16[8,2,64,128]{3,2,1,0:T(8,128)(2,1)S(1)}, bf16[8,2,64,128]{3,2,1,0:T(8,128)(2,1)S(1)}, u32[]{:S(2)}, u32[]{:S(2)}) collective-permute-start(bf16[8,2,64,128]{3,2,1,0:T(8,128)(2,1)S(1)} %all-to-all-done.1.rest_0_), channel_id=1, source_target_pairs={{16,1},{17,2},{18,3},{19,4},{20,5},{21,6},{22,7},{23,8},{24,9},{25... | collective-permute-start | bytes 786440 | tf_op jit(solution)/shard_map/ppermute | solution.py:287
  25.4 29.4 %collective-permute-start.1 = (bf16[8,2,64,128]{3,2,1,0:T(8,128)(2,1)S(1)}, bf16[8,2,64,128]{3,2,1,0:T(8,128)(2,1)S(1)}, u32[]{:S(2)}, u32[]{:S(2)}) collective-permute-start(bf16[8,2,64,128]{3,2,1,0:T(8,128)(2,1)S(1)} %all-to-all-done.1.rest_0_), channel_id=1, source_target_pairs={{0,1},{1,2},{2,3},{3,4},{4,5},{5,6},{6,7},{7,8},{8,9},{9,10},{10,1... | collective-permute-start | bytes 786440 | tf_op jit(solution)/shard_map/ppermute | solution.py:288
  42.8 18.0 %collective-permute-start.2 = (bf16[8,2,64,128]{3,2,1,0:T(8,128)(2,1)S(1)}, bf16[8,2,64,128]{3,2,1,0:T(8,128)(2,1)S(1)}, u32[]{:S(2)}, u32[]{:S(2)}) collective-permute-start(bf16[8,2,64,128]{3,2,1,0:T(8,128)(2,1)S(1)} %all-to-all-done.1.rest_0_), channel_id=1, source_target_pairs={{16,0},{17,1},{18,2},{19,3},{20,4},{21,5},{22,6},{23,7},{24,8},{25... | collective-permute-start | bytes 786440 | tf_op jit(solution)/shard_map/ppermute | solution.py:290
  54.7 12.0 %collective-permute-start.3 = (bf16[8,2,64,128]{3,2,1,0:T(8,128)(2,1)S(1)}, bf16[8,2,64,128]{3,2,1,0:T(8,128)(2,1)S(1)}, u32[]{:S(2)}, u32[]{:S(2)}) collective-permute-start(bf16[8,2,64,128]{3,2,1,0:T(8,128)(2,1)S(1)} %get-tuple-element.48), channel_id=1, source_target_pairs={{1,0},{2,1},{3,2},{4,3},{5,4},{6,5},{7,6},{8,7},{9,8},{10,9},{11,1... | collective-permute-start | bytes 786440 | tf_op jit(solution)/shard_map/ppermute | solution.py:335
  60.0 19.6 %collective-permute-start.5 = (bf16[8,2,64,128]{3,2,1,0:T(8,128)(2,1)S(1)}, bf16[8,2,64,128]{3,2,1,0:T(8,128)(2,1)S(1)}, u32[]{:S(2)}, u32[]{:S(2)}) collective-permute-start(bf16[8,2,64,128]{3,2,1,0:T(8,128)(2,1)S(1)} %get-tuple-element.49), channel_id=1, source_target_pairs={{1,0},{2,1},{3,2},{4,3},{5,4},{6,5},{7,6},{8,7},{9,8},{10,9},{11,1... | collective-permute-start | bytes 786440 | tf_op jit(solution)/shard_map/ppermute | solution.py:339
  66.8 17.1 %collective-permute-start.4 = (bf16[8,2,64,128]{3,2,1,0:T(8,128)(2,1)S(1)}, bf16[8,2,64,128]{3,2,1,0:T(8,128)(2,1)S(1)}, u32[]{:S(2)}, u32[]{:S(2)}) collective-permute-start(bf16[8,2,64,128]{3,2,1,0:T(8,128)(2,1)S(1)} %add_convert_fusion), channel_id=1, source_target_pairs={{16,0},{17,1},{18,2},{19,3},{20,4},{21,5},{22,6},{23,7},{24,8},{25... | collective-permute-start | bytes 786440 | tf_op jit(solution)/shard_map/ppermute | solution.py:344
  75.4 17.9 %all-to-all-start.2 = ((bf16[8,384,128]{2,1,0:T(8,128)(2,1)}), bf16[8,384,128]{2,1,0:T(8,128)(2,1)S(1)}, u32[]{:S(2)}, u32[]{:S(2)}) async-start(bf16[8,384,128]{2,1,0:T(8,128)(2,1)} %get-tuple-element.45), calls=%async_computation.2 | async-start | bytes 1572864 | tf_op jit(solution)/shard_map/all_to_all | solution.py:281
  83.9 5.2 %collective-permute-start.6 = (bf16[2,64,128]{2,1,0:T(8,128)(2,1)S(1)}, bf16[2,64,128]{2,1,0:T(8,128)(2,1)S(1)}, u32[]{:S(2)}, u32[]{:S(2)}) collective-permute-start(bf16[2,64,128]{2,1,0:T(8,128)(2,1)S(1)} %get-tuple-element.51), channel_id=1, source_target_pairs={{0,32},{32,0},{64,96},{96,64},{128,160},{160,128},{192,224},{224,1... | collective-permute-start | bytes 98312 | tf_op jit(solution)/shard_map/ppermute | solution.py:330
  84.0 8.4 %collective-permute-start.7 = (bf16[2,64,128]{2,1,0:T(8,128)(2,1)S(1)}, bf16[2,64,128]{2,1,0:T(8,128)(2,1)S(1)}, u32[]{:S(2)}, u32[]{:S(2)}) collective-permute-start(bf16[2,64,128]{2,1,0:T(8,128)(2,1)S(1)} %get-tuple-element.52), channel_id=1, source_target_pairs={{0,64},{32,96},{64,0},{96,32},{128,192},{160,224},{192,128},{224,1... | collective-permute-start | bytes 98312 | tf_op jit(solution)/shard_map/ppermute | solution.py:330
  85.2 9.5 %collective-permute-start.8 = (bf16[2,64,128]{2,1,0:T(8,128)(2,1)S(1)}, bf16[2,64,128]{2,1,0:T(8,128)(2,1)S(1)}, u32[]{:S(2)}, u32[]{:S(2)}) collective-permute-start(bf16[2,64,128]{2,1,0:T(8,128)(2,1)S(1)} %get-tuple-element.53), channel_id=1, source_target_pairs={{0,96},{32,64},{64,32},{96,0},{128,224},{160,192},{192,160},{224,1... | collective-permute-start | bytes 98312 | tf_op jit(solution)/shard_map/ppermute | solution.py:330
  85.9 9.4 %collective-permute-start.9 = (bf16[2,64,128]{2,1,0:T(8,128)(2,1)S(1)}, bf16[2,64,128]{2,1,0:T(8,128)(2,1)S(1)}, u32[]{:S(2)}, u32[]{:S(2)}) collective-permute-start(bf16[2,64,128]{2,1,0:T(8,128)(2,1)S(1)} %get-tuple-element.54), channel_id=1, source_target_pairs={{0,128},{32,160},{64,192},{96,224},{128,0},{160,32},{192,64},{224,... | collective-permute-start | bytes 98312 | tf_op jit(solution)/shard_map/ppermute | solution.py:330
  88.3 7.0 %collective-permute-start.10 = (bf16[2,64,128]{2,1,0:T(8,128)(2,1)S(1)}, bf16[2,64,128]{2,1,0:T(8,128)(2,1)S(1)}, u32[]{:S(2)}, u32[]{:S(2)}) collective-permute-start(bf16[2,64,128]{2,1,0:T(8,128)(2,1)S(1)} %get-tuple-element.55), channel_id=1, source_target_pairs={{0,160},{32,128},{64,224},{96,192},{128,32},{160,0},{192,96},{224,... | collective-permute-start | bytes 98312 | tf_op jit(solution)/shard_map/ppermute | solution.py:330
  89.1 6.2 %collective-permute-start.11 = (bf16[2,64,128]{2,1,0:T(8,128)(2,1)S(1)}, bf16[2,64,128]{2,1,0:T(8,128)(2,1)S(1)}, u32[]{:S(2)}, u32[]{:S(2)}) collective-permute-start(bf16[2,64,128]{2,1,0:T(8,128)(2,1)S(1)} %get-tuple-element.56), channel_id=1, source_target_pairs={{0,192},{32,224},{64,128},{96,160},{128,64},{160,96},{192,0},{224,... | collective-permute-start | bytes 98312 | tf_op jit(solution)/shard_map/ppermute | solution.py:330
  92.5 4.6 %collective-permute-start.12 = (bf16[2,64,128]{2,1,0:T(8,128)(2,1)S(1)}, bf16[2,64,128]{2,1,0:T(8,128)(2,1)S(1)}, u32[]{:S(2)}, u32[]{:S(2)}) collective-permute-start(bf16[2,64,128]{2,1,0:T(8,128)(2,1)S(1)} %get-tuple-element.57), channel_id=1, source_target_pairs={{0,224},{32,192},{64,160},{96,128},{128,96},{160,64},{192,32},{224... | collective-permute-start | bytes 98312 | tf_op jit(solution)/shard_map/ppermute | solution.py:330

commit v4 on v3

--- a/solution.py
+++ b/solution.py
@@ -110,7 +110,7 @@
             stage, sems = rest[1:]
             copies = []
             for j in range(src):
-                stage[j] = (dq_s[:, j * R : (j + 1) * R].T * scale).astype(bf16)
+                stage[j] = (dq_s[:, j * R : (j + 1) * R] * scale).astype(bf16).T
                 copies.append(
                     pltpu.make_async_copy(stage.at[j], out_ref.at[table[0, j]], sems.at[j])
                 )
@@ -296,7 +296,7 @@
     stats = jnp.pad(stats, ((0, 0), (0, 8 - 2 * lanes), (0, 0)))
     stats = jnp.concatenate(pieces(stats), axis=1)
     stats = jnp.pad(stats, ((0, 0), (0, 8), (0, 0)))
-    keys_step, rows_step = 4, 2
+    keys_step, rows_step = 4, 4
     names = ["far_partner", "far", "near_partner", "near"]
 
     def spots_of():

time: 99.4 us -> 98.2 us (0.988)
  no operation moved by 1% of the time
where the time goes in v4:
time: 98.2 us; the launch traced here: 97.7 us
  starting transfers between devices  38.5 us (39%)
  waiting for transfers between devices  26.5 us (27%)
  Pallas kernels  24.5 us (25%)
  local copies, waits for them, and re-layouts  3.95 us (4%)
  other arithmetic  3.38 us (3%)
    pallas_call x4, Pallas kernels, attention_part(): pl.pallas_call(body, out_shape=(dq_out, *g_outs), in_specs=[smem] + [vmem...  22.6 us
    ppermute x1, waiting for transfers between devices, shards(): kv_far_partner = lax.ppermute(kv, ring, across)  15.8 us
    all_to_all x3, starting transfers between devices, exchange(): return lax.all_to_all(x, 'head', split_axis=0, concat_axis=0, tiled=True)  12.4 us
    ppermute x7, starting transfers between devices, to_peers(): lax.ppermute(blocks[j], 'head', [(h, h ^ j) for h in range(heads)])  8.12 us
    ppermute x1, starting transfers between devices, shards(): kv_far_partner = lax.ppermute(kv, ring, across)  7.29 us
    ppermute x1, starting transfers between devices, shards(): kv_partner = lax.ppermute(kv_after, ring, swap)  6.75 us
    ppermute x1, waiting for transfers between devices, shards(): partner = lax.ppermute(partner, ring, swap)  4.18 us
    ppermute x7, waiting for transfers between devices, to_peers(): lax.ppermute(blocks[j], 'head', [(h, h ^ j) for h in range(heads)])  3.59 us
  transfers between devices with their start and end apart: 16, of which 7 were waited for; matrix products, arithmetic and copies ran while one was open for 5% of the time, Pallas kernels for 24%

profile of v4, /device:TPU:32, one launch (start us, length us, event | category | flops | bytes accessed | tf_op | source)
XLA Modules:
  0.0 97.7 jit_solution(8350146377251170674)
XLA Ops:
  0.7 1.1 %copy_bitcast_fusion.1 = (bf16[8,1,64,128]{3,2,1,0:T(8,128)(2,1)S(1)}, bf16[8,1,64,128]{3,2,1,0:T(8,128)(2,1)S(1)}) fusion(bf16[64,8,128]{2,1,0:T(8,128)(2,1)} %param.9, bf16[64,8,128]{2,1,0:T(8,128)(2,1)} %param.8), kind=kLoop, calls=%fused_computation.9 | loop fusion | bytes 524288 | tf_op jit(solution)/shard_map/transpose | solution.py:284
  1.8 0.7 pad_maximum_fusion.1
  2.5 4.5 %all-to-all-start.1 = ((bf16[8,2,64,128]{3,2,1,0:T(8,128)(2,1)}), bf16[8,2,64,128]{3,2,1,0:T(8,128)(2,1)S(1)}, u32[]{:S(2)}, u32[]{:S(2)}) async-start(bf16[8,2,64,128]{3,2,1,0:T(8,128)(2,1)} %pad_maximum_fusion.1), calls=%async_computation.1 | async-start | bytes 524288 | tf_op jit(solution)/shard_map/all_to_all | solution.py:281
  7.0 0.7 copy-done
  7.7 0.9 order_tables.1.table
  8.5 0.7 broadcast_multiply_fusion
  9.5 0.5 multiply_reduce_fusion
  10.6 1.3 %pad_maximum_fusion = bf16[8,800,128]{2,1,0:T(8,128)(2,1)} fusion(bf16[8,32,128]{2,1,0:T(8,128)(2,1)S(1)} %fusion.4, bf16[8,384,128]{2,1,0:T(8,128)(2,1)S(1)} %bitcast.29, bf16[8,384,128]{2,1,0:T(8,128)(2,1)S(1)} %bitcast.30), kind=kLoop, calls=%fused_computation | loop fusion | flops 4915200 | bytes 3276800 | tf_op jit(solution)/shard_map/concatenate | solution.py:312
  11.9 2.6 %all-to-all-done.1.rest_0_ = bf16[8,2,64,128]{3,2,1,0:T(8,128)(2,1)S(1)} async-done(((bf16[8,2,64,128]{3,2,1,0:T(8,128)(2,1)}), bf16[8,2,64,128]{3,2,1,0:T(8,128)(2,1)S(1)}, u32[]{:S(2)}, u32[]{:S(2)}) %all-to-all-start.1) | async-done | bytes 262176 | tf_op jit(solution)/shard_map/all_to_all | solution.py:281
  14.5 3.6 %all-to-all-start = ((bf16[8,800,128]{2,1,0:T(8,128)(2,1)}), bf16[8,800,128]{2,1,0:T(8,128)(2,1)S(1)}, u32[]{:S(2)}, u32[]{:S(2)}) async-start(bf16[8,800,128]{2,1,0:T(8,128)(2,1)} %pad_maximum_fusion), calls=%async_computation | async-start | bytes 3276800 | tf_op jit(solution)/shard_map/all_to_all | solution.py:281
  18.1 7.3 %collective-permute-start = (bf16[8,2,64,128]{3,2,1,0:T(8,128)(2,1)S(1)}, bf16[8,2,64,128]{3,2,1,0:T(8,128)(2,1)S(1)}, u32[]{:S(2)}, u32[]{:S(2)}) collective-permute-start(bf16[8,2,64,128]{3,2,1,0:T(8,128)(2,1)S(1)} %all-to-all-done.1.rest_0_), channel_id=1, source_target_pairs={{16,1},{17,2},{18,3},{19,4},{20,5},{21,6},{22,7},{23,8},{24,9},{25... | collective-permute-start | bytes 786440 | tf_op jit(solution)/shard_map/ppermute | solution.py:287
  25.4 1.5 %collective-permute-start.1 = (bf16[8,2,64,128]{3,2,1,0:T(8,128)(2,1)S(1)}, bf16[8,2,64,128]{3,2,1,0:T(8,128)(2,1)S(1)}, u32[]{:S(2)}, u32[]{:S(2)}) collective-permute-start(bf16[8,2,64,128]{3,2,1,0:T(8,128)(2,1)S(1)} %all-to-all-done.1.rest_0_), channel_id=1, source_target_pairs={{0,1},{1,2},{2,3},{3,4},{4,5},{5,6},{6,7},{7,8},{8,9},{9,10},{10,1... | collective-permute-start | bytes 786440 | tf_op jit(solution)/shard_map/ppermute | solution.py:288
  26.9 15.8 %collective-permute-done.rest_0_ = bf16[8,2,64,128]{3,2,1,0:T(8,128)(2,1)S(1)} collective-permute-done((bf16[8,2,64,128]{3,2,1,0:T(8,128)(2,1)S(1)}, bf16[8,2,64,128]{3,2,1,0:T(8,128)(2,1)S(1)}, u32[]{:S(2)}, u32[]{:S(2)}) %collective-permute-start) | collective-permute-done | bytes 262176 | tf_op jit(solution)/shard_map/ppermute | solution.py:287
  42.8 6.7 %collective-permute-start.2 = (bf16[8,2,64,128]{3,2,1,0:T(8,128)(2,1)S(1)}, bf16[8,2,64,128]{3,2,1,0:T(8,128)(2,1)S(1)}, u32[]{:S(2)}, u32[]{:S(2)}) collective-permute-start(bf16[8,2,64,128]{3,2,1,0:T(8,128)(2,1)S(1)} %all-to-all-done.1.rest_0_), channel_id=1, source_target_pairs={{16,0},{17,1},{18,2},{19,3},{20,4},{21,5},{22,6},{23,7},{24,8},{25... | collective-permute-start | bytes 786440 | tf_op jit(solution)/shard_map/ppermute | solution.py:290
  49.5 4.8 %far_partner.1 = (f32[128,3072]{1,0:T(8,128)S(1)}, bf16[8,2,64,128]{3,2,1,0:T(8,128)(2,1)S(1)}) custom-call(s32[16,128]{1,0:T(8,128)S(1)} %order_tables.1.table, bf16[8,800,128]{2,1,0:T(8,128)(2,1)S(1)} %all-to-all-done.packed_ref, bf16[8,2,64,128]{3,2,1,0:T(8,128)(2,1)S(1)} %collective-permute-done.rest_0_), custom_call_target="tpu_custom_call" | custom-call | flops 1 | bytes 1 | tf_op jit(solution)/shard_map/far_partner/pallas_call | solution.py:146
  54.4 6.0 %far.1 = (f32[128,3072]{1,0:T(8,128)S(1)}, bf16[8,2,64,128]{3,2,1,0:T(8,128)(2,1)S(1)}) custom-call(s32[16,128]{1,0:T(8,128)S(1)} %order_tables.1.table, bf16[8,800,128]{2,1,0:T(8,128)(2,1)S(1)} %all-to-all-done.packed_ref, bf16[8,2,64,128]{3,2,1,0:T(8,128)(2,1)S(1)} %collective-permute-done.1.rest_0_), custom_call_target="tpu_custom_call" | custom-call | flops 1 | bytes 1 | tf_op jit(solution)/shard_map/far/pallas_call | solution.py:146
  60.8 6.0 %near_partner.1 = (f32[128,3072]{1,0:T(8,128)S(1)}, f32[8,2,64,128]{3,2,1,0:T(8,128)S(1)}) custom-call(s32[16,128]{1,0:T(8,128)S(1)} %order_tables.1.table, bf16[8,800,128]{2,1,0:T(8,128)(2,1)S(1)} %all-to-all-done.packed_ref, bf16[8,2,64,128]{3,2,1,0:T(8,128)(2,1)S(1)} %collective-permute-done.2.rest_0_, f32[128,3072]{1,0:T(8,128)S(1)} %get-tuple-element.39.rest_1_, ...), custom_call_target="tpu_custom_call" | custom-call | flops 1 | bytes 1 | tf_op jit(solution)/shard_map/near_partner/pallas_call | solution.py:146
  66.9 2.3 %collective-permute-start.4 = (bf16[8,2,64,128]{3,2,1,0:T(8,128)(2,1)S(1)}, bf16[8,2,64,128]{3,2,1,0:T(8,128)(2,1)S(1)}, u32[]{:S(2)}, u32[]{:S(2)}) collective-permute-start(bf16[8,2,64,128]{3,2,1,0:T(8,128)(2,1)S(1)} %add_convert_fusion), channel_id=1, source_target_pairs={{16,0},{17,1},{18,2},{19,3},{20,4},{21,5},{22,6},{23,7},{24,8},{25... | collective-permute-start | bytes 786440 | tf_op jit(solution)/shard_map/ppermute | solution.py:344
  69.2 5.8 %near.1 = (bf16[8,384,128]{2,1,0:T(8,128)(2,1)}, f32[8,2,64,128]{3,2,1,0:T(8,128)S(1)}) custom-call(s32[16,128]{1,0:T(8,128)S(1)} %order_tables.1.table, bf16[8,800,128]{2,1,0:T(8,128)(2,1)S(1)} %all-to-all-done.packed_ref, bf16[8,2,64,128]{3,2,1,0:T(8,128)(2,1)S(1)} %all-to-all-done.1.rest_0_, f32[128,3072]{1,0:T(8,128)S(1)} %get-tuple-element.44.rest_1_), custom_call_target="tpu_custom_call" | custom-call | flops 1 | bytes 1 | tf_op jit(solution)/shard_map/near/pallas_call | solution.py:146
  75.0 4.3 %all-to-all-start.2 = ((bf16[8,384,128]{2,1,0:T(8,128)(2,1)}), bf16[8,384,128]{2,1,0:T(8,128)(2,1)S(1)}, u32[]{:S(2)}, u32[]{:S(2)}) async-start(bf16[8,384,128]{2,1,0:T(8,128)(2,1)} %get-tuple-element.45), calls=%async_computation.2 | async-start | bytes 1572864 | tf_op jit(solution)/shard_map/all_to_all | solution.py:281
  79.3 4.2 %collective-permute-done.4.refs_1_ = bf16[8,2,64,128]{3,2,1,0:T(8,128)(2,1)S(1)} collective-permute-done((bf16[8,2,64,128]{3,2,1,0:T(8,128)(2,1)S(1)}, bf16[8,2,64,128]{3,2,1,0:T(8,128)(2,1)S(1)}, u32[]{:S(2)}, u32[]{:S(2)}) %collective-permute-start.4) | collective-permute-done | bytes 262176 | tf_op jit(solution)/shard_map/ppermute | solution.py:344
  83.7 1.0 %collective-permute-start.7 = (bf16[2,64,128]{2,1,0:T(8,128)(2,1)S(1)}, bf16[2,64,128]{2,1,0:T(8,128)(2,1)S(1)}, u32[]{:S(2)}, u32[]{:S(2)}) collective-permute-start(bf16[2,64,128]{2,1,0:T(8,128)(2,1)S(1)} %get-tuple-element.52), channel_id=1, source_target_pairs={{0,64},{32,96},{64,0},{96,32},{128,192},{160,224},{192,128},{224,1... | collective-permute-start | bytes 98312 | tf_op jit(solution)/shard_map/ppermute | solution.py:330
  84.7 0.9 collective-permute-start.8
  85.6 2.3 %collective-permute-start.9 = (bf16[2,64,128]{2,1,0:T(8,128)(2,1)S(1)}, bf16[2,64,128]{2,1,0:T(8,128)(2,1)S(1)}, u32[]{:S(2)}, u32[]{:S(2)}) collective-permute-start(bf16[2,64,128]{2,1,0:T(8,128)(2,1)S(1)} %get-tuple-element.54), channel_id=1, source_target_pairs={{0,128},{32,160},{64,192},{96,224},{128,0},{160,32},{192,64},{224,... | collective-permute-start | bytes 98312 | tf_op jit(solution)/shard_map/ppermute | solution.py:330
  87.9 0.9 collective-permute-start.10
  88.8 2.1 %collective-permute-start.11 = (bf16[2,64,128]{2,1,0:T(8,128)(2,1)S(1)}, bf16[2,64,128]{2,1,0:T(8,128)(2,1)S(1)}, u32[]{:S(2)}, u32[]{:S(2)}) collective-permute-start(bf16[2,64,128]{2,1,0:T(8,128)(2,1)S(1)} %get-tuple-element.56), channel_id=1, source_target_pairs={{0,192},{32,224},{64,128},{96,160},{128,64},{160,96},{192,0},{224,... | collective-permute-start | bytes 98312 | tf_op jit(solution)/shard_map/ppermute | solution.py:330
  90.9 1.3 %collective-permute-done.7.refs_2_ = bf16[2,64,128]{2,1,0:T(8,128)(2,1)S(1)} collective-permute-done((bf16[2,64,128]{2,1,0:T(8,128)(2,1)S(1)}, bf16[2,64,128]{2,1,0:T(8,128)(2,1)S(1)}, u32[]{:S(2)}, u32[]{:S(2)}) %collective-permute-start.7) | collective-permute-done | bytes 32800 | tf_op jit(solution)/shard_map/ppermute | solution.py:330
  92.2 0.8 collective-permute-start.12
  93.0 1.4 %copy.32 = bf16[48,64,128]{2,0,1:T(8,128)(2,1)} copy(bf16[48,64,128]{2,1,0:T(8,128)(2,1)S(1)} %bitcast.28) | data formatting | bytes 1572864 | tf_op jit(solution)/shard_map/reshape | solution.py:348
  94.4 0.6 collective-permute-done.9.refs_4_
  95.0 1.8 %collective-permute-done.12.refs_7_ = bf16[2,64,128]{2,1,0:T(8,128)(2,1)S(1)} collective-permute-done((bf16[2,64,128]{2,1,0:T(8,128)(2,1)S(1)}, bf16[2,64,128]{2,1,0:T(8,128)(2,1)S(1)}, u32[]{:S(2)}, u32[]{:S(2)}) %collective-permute-start.12) | collective-permute-done | bytes 32800 | tf_op jit(solution)/shard_map/ppermute | solution.py:330
  96.7 1.0 %gather_grads.1 = (bf16[64,8,128]{2,1,0:T(8,128)(2,1)}, bf16[64,8,128]{2,1,0:T(8,128)(2,1)}) custom-call(bf16[2,64,128]{2,1,0:T(8,128)(2,1)S(1)} %get-tuple-element.59.refs_0_, bf16[2,64,128]{2,1,0:T(8,128)(2,1)S(1)} %collective-permute-done.6.refs_1_, bf16[2,64,128]{2,1,0:T(8,128)(2,1)S(1)} %collective-permute-done.7.refs_2_, ...), custom_call_target="tpu_custom_call" | custom-call | tf_op jit(solution)/shard_map/gather_grads/pallas_call | solution.py:195
  (32 shorter events, 1.5 us)
Async XLA Ops:
  0.6 8.7 %copy-start.1 = (bf16[64,48,128]{2,1,0:T(8,128)(2,1)S(1)}, bf16[64,48,128]{2,1,0:T(8,128)(2,1)}, u32[]{:S(2)}) copy-start(bf16[64,48,128]{2,1,0:T(8,128)(2,1)} %param.11) | copy-start | bytes 2359300
  0.6 8.9 %copy-start.2 = (bf16[64,48,128]{2,1,0:T(8,128)(2,1)S(1)}, bf16[64,48,128]{2,1,0:T(8,128)(2,1)}, u32[]{:S(2)}) copy-start(bf16[64,48,128]{2,1,0:T(8,128)(2,1)} %param.10) | copy-start | bytes 2359300
  2.5 12.0 %all-to-all-start.1 = ((bf16[8,2,64,128]{3,2,1,0:T(8,128)(2,1)}), bf16[8,2,64,128]{3,2,1,0:T(8,128)(2,1)S(1)}, u32[]{:S(2)}, u32[]{:S(2)}) async-start(bf16[8,2,64,128]{3,2,1,0:T(8,128)(2,1)} %pad_maximum_fusion.1), calls=%async_computation.1 | async-start | bytes 524288 | tf_op jit(solution)/shard_map/all_to_all | solution.py:281
  7.0 0.7 copy-start
  9.3 1.1 %copy-start.3 = (bf16[64,48,128]{2,1,0:T(8,128)(2,1)S(1)}, bf16[64,48,128]{2,1,0:T(8,128)(2,1)}, u32[]{:S(2)}) copy-start(bf16[64,48,128]{2,1,0:T(8,128)(2,1)} %param.7) | copy-start | bytes 2359300
  14.5 35.0 %all-to-all-start = ((bf16[8,800,128]{2,1,0:T(8,128)(2,1)}), bf16[8,800,128]{2,1,0:T(8,128)(2,1)S(1)}, u32[]{:S(2)}, u32[]{:S(2)}) async-start(bf16[8,800,128]{2,1,0:T(8,128)(2,1)} %pad_maximum_fusion), calls=%async_computation | async-start | bytes 3276800 | tf_op jit(solution)/shard_map/all_to_all | solution.py:281
  18.1 24.6 %collective-permute-start = (bf16[8,2,64,128]{3,2,1,0:T(8,128)(2,1)S(1)}, bf16[8,2,64,128]{3,2,1,0:T(8,128)(2,1)S(1)}, u32[]{:S(2)}, u32[]{:S(2)}) collective-permute-start(bf16[8,2,64,128]{3,2,1,0:T(8,128)(2,1)S(1)} %all-to-all-done.1.rest_0_), channel_id=1, source_target_pairs={{16,1},{17,2},{18,3},{19,4},{20,5},{21,6},{22,7},{23,8},{24,9},{25... | collective-permute-start | bytes 786440 | tf_op jit(solution)/shard_map/ppermute | solution.py:287
  25.4 29.0 %collective-permute-start.1 = (bf16[8,2,64,128]{3,2,1,0:T(8,128)(2,1)S(1)}, bf16[8,2,64,128]{3,2,1,0:T(8,128)(2,1)S(1)}, u32[]{:S(2)}, u32[]{:S(2)}) collective-permute-start(bf16[8,2,64,128]{3,2,1,0:T(8,128)(2,1)S(1)} %all-to-all-done.1.rest_0_), channel_id=1, source_target_pairs={{0,1},{1,2},{2,3},{3,4},{4,5},{5,6},{6,7},{7,8},{8,9},{9,10},{10,1... | collective-permute-start | bytes 786440 | tf_op jit(solution)/shard_map/ppermute | solution.py:288
  42.8 18.0 %collective-permute-start.2 = (bf16[8,2,64,128]{3,2,1,0:T(8,128)(2,1)S(1)}, bf16[8,2,64,128]{3,2,1,0:T(8,128)(2,1)S(1)}, u32[]{:S(2)}, u32[]{:S(2)}) collective-permute-start(bf16[8,2,64,128]{3,2,1,0:T(8,128)(2,1)S(1)} %all-to-all-done.1.rest_0_), channel_id=1, source_target_pairs={{16,0},{17,1},{18,2},{19,3},{20,4},{21,5},{22,6},{23,7},{24,8},{25... | collective-permute-start | bytes 786440 | tf_op jit(solution)/shard_map/ppermute | solution.py:290
  54.3 12.5 %collective-permute-start.3 = (bf16[8,2,64,128]{3,2,1,0:T(8,128)(2,1)S(1)}, bf16[8,2,64,128]{3,2,1,0:T(8,128)(2,1)S(1)}, u32[]{:S(2)}, u32[]{:S(2)}) collective-permute-start(bf16[8,2,64,128]{3,2,1,0:T(8,128)(2,1)S(1)} %get-tuple-element.48), channel_id=1, source_target_pairs={{1,0},{2,1},{3,2},{4,3},{5,4},{6,5},{7,6},{8,7},{9,8},{10,9},{11,1... | collective-permute-start | bytes 786440 | tf_op jit(solution)/shard_map/ppermute | solution.py:335
  60.4 19.0 %collective-permute-start.5 = (bf16[8,2,64,128]{3,2,1,0:T(8,128)(2,1)S(1)}, bf16[8,2,64,128]{3,2,1,0:T(8,128)(2,1)S(1)}, u32[]{:S(2)}, u32[]{:S(2)}) collective-permute-start(bf16[8,2,64,128]{3,2,1,0:T(8,128)(2,1)S(1)} %get-tuple-element.49), channel_id=1, source_target_pairs={{1,0},{2,1},{3,2},{4,3},{5,4},{6,5},{7,6},{8,7},{9,8},{10,9},{11,1... | collective-permute-start | bytes 786440 | tf_op jit(solution)/shard_map/ppermute | solution.py:339
  66.9 16.6 %collective-permute-start.4 = (bf16[8,2,64,128]{3,2,1,0:T(8,128)(2,1)S(1)}, bf16[8,2,64,128]{3,2,1,0:T(8,128)(2,1)S(1)}, u32[]{:S(2)}, u32[]{:S(2)}) collective-permute-start(bf16[8,2,64,128]{3,2,1,0:T(8,128)(2,1)S(1)} %add_convert_fusion), channel_id=1, source_target_pairs={{16,0},{17,1},{18,2},{19,3},{20,4},{21,5},{22,6},{23,7},{24,8},{25... | collective-permute-start | bytes 786440 | tf_op jit(solution)/shard_map/ppermute | solution.py:344
  75.0 18.0 %all-to-all-start.2 = ((bf16[8,384,128]{2,1,0:T(8,128)(2,1)}), bf16[8,384,128]{2,1,0:T(8,128)(2,1)S(1)}, u32[]{:S(2)}, u32[]{:S(2)}) async-start(bf16[8,384,128]{2,1,0:T(8,128)(2,1)} %get-tuple-element.45), calls=%async_computation.2 | async-start | bytes 1572864 | tf_op jit(solution)/shard_map/all_to_all | solution.py:281
  83.6 5.2 %collective-permute-start.6 = (bf16[2,64,128]{2,1,0:T(8,128)(2,1)S(1)}, bf16[2,64,128]{2,1,0:T(8,128)(2,1)S(1)}, u32[]{:S(2)}, u32[]{:S(2)}) collective-permute-start(bf16[2,64,128]{2,1,0:T(8,128)(2,1)S(1)} %get-tuple-element.51), channel_id=1, source_target_pairs={{0,32},{32,0},{64,96},{96,64},{128,160},{160,128},{192,224},{224,1... | collective-permute-start | bytes 98312 | tf_op jit(solution)/shard_map/ppermute | solution.py:330
  83.7 8.5 %collective-permute-start.7 = (bf16[2,64,128]{2,1,0:T(8,128)(2,1)S(1)}, bf16[2,64,128]{2,1,0:T(8,128)(2,1)S(1)}, u32[]{:S(2)}, u32[]{:S(2)}) collective-permute-start(bf16[2,64,128]{2,1,0:T(8,128)(2,1)S(1)} %get-tuple-element.52), channel_id=1, source_target_pairs={{0,64},{32,96},{64,0},{96,32},{128,192},{160,224},{192,128},{224,1... | collective-permute-start | bytes 98312 | tf_op jit(solution)/shard_map/ppermute | solution.py:330
  84.7 9.7 %collective-permute-start.8 = (bf16[2,64,128]{2,1,0:T(8,128)(2,1)S(1)}, bf16[2,64,128]{2,1,0:T(8,128)(2,1)S(1)}, u32[]{:S(2)}, u32[]{:S(2)}) collective-permute-start(bf16[2,64,128]{2,1,0:T(8,128)(2,1)S(1)} %get-tuple-element.53), channel_id=1, source_target_pairs={{0,96},{32,64},{64,32},{96,0},{128,224},{160,192},{192,160},{224,1... | collective-permute-start | bytes 98312 | tf_op jit(solution)/shard_map/ppermute | solution.py:330
  85.6 9.4 %collective-permute-start.9 = (bf16[2,64,128]{2,1,0:T(8,128)(2,1)S(1)}, bf16[2,64,128]{2,1,0:T(8,128)(2,1)S(1)}, u32[]{:S(2)}, u32[]{:S(2)}) collective-permute-start(bf16[2,64,128]{2,1,0:T(8,128)(2,1)S(1)} %get-tuple-element.54), channel_id=1, source_target_pairs={{0,128},{32,160},{64,192},{96,224},{128,0},{160,32},{192,64},{224,... | collective-permute-start | bytes 98312 | tf_op jit(solution)/shard_map/ppermute | solution.py:330
  87.9 7.0 %collective-permute-start.10 = (bf16[2,64,128]{2,1,0:T(8,128)(2,1)S(1)}, bf16[2,64,128]{2,1,0:T(8,128)(2,1)S(1)}, u32[]{:S(2)}, u32[]{:S(2)}) collective-permute-start(bf16[2,64,128]{2,1,0:T(8,128)(2,1)S(1)} %get-tuple-element.55), channel_id=1, source_target_pairs={{0,160},{32,128},{64,224},{96,192},{128,32},{160,0},{192,96},{224,... | collective-permute-start | bytes 98312 | tf_op jit(solution)/shard_map/ppermute | solution.py:330
  88.8 6.2 %collective-permute-start.11 = (bf16[2,64,128]{2,1,0:T(8,128)(2,1)S(1)}, bf16[2,64,128]{2,1,0:T(8,128)(2,1)S(1)}, u32[]{:S(2)}, u32[]{:S(2)}) collective-permute-start(bf16[2,64,128]{2,1,0:T(8,128)(2,1)S(1)} %get-tuple-element.56), channel_id=1, source_target_pairs={{0,192},{32,224},{64,128},{96,160},{128,64},{160,96},{192,0},{224,... | collective-permute-start | bytes 98312 | tf_op jit(solution)/shard_map/ppermute | solution.py:330
  92.2 4.6 %collective-permute-start.12 = (bf16[2,64,128]{2,1,0:T(8,128)(2,1)S(1)}, bf16[2,64,128]{2,1,0:T(8,128)(2,1)S(1)}, u32[]{:S(2)}, u32[]{:S(2)}) collective-permute-start(bf16[2,64,128]{2,1,0:T(8,128)(2,1)S(1)} %get-tuple-element.57), channel_id=1, source_target_pairs={{0,224},{32,192},{64,160},{96,128},{128,96},{160,64},{192,32},{224... | collective-permute-start | bytes 98312 | tf_op jit(solution)/shard_map/ppermute | solution.py:330

commit v5 on v4

--- a/solution.py
+++ b/solution.py
@@ -163,29 +163,48 @@
         me = lax.axis_index("head")
         for j in range(src):
             at = me ^ j
-            outs[j][...] = sum(r[at].astype(f32) for r in ins).astype(bf16)
+            outs[j % 2][j // 2] = sum(r[at].astype(f32) for r in ins).astype(bf16)
 
     vmem = pl.BlockSpec(memory_space=pltpu.VMEM)
     return pl.pallas_call(
         body,
-        out_shape=[jax.ShapeDtypeStruct(rest, bf16)] * src,
+        out_shape=[jax.ShapeDtypeStruct((src // 2, *rest), bf16)] * 2,
         in_specs=[vmem] * len(arrays),
-        out_specs=[vmem] * src,
+        out_specs=[vmem] * 2,
         cost_estimate=pl.CostEstimate(flops=10**10, bytes_accessed=1, transcendentals=0),
         compiler_params=PARAMS,
         name="add_by_peer",
     )(*arrays)
 
 
-def gather_grads(pieces):
-    src = len(pieces)
-    _, T, D = pieces[0].shape
+def pair_up(own, mate):
+    n, *rest = own.shape
+
+    def body(own_ref, mate_ref, *outs):
+        for k in range(n):
+            outs[k][0] = own_ref[k]
+            outs[k][1] = mate_ref[k]
+
+    vmem = pl.BlockSpec(memory_space=pltpu.VMEM)
+    return pl.pallas_call(
+        body,
+        out_shape=[jax.ShapeDtypeStruct((2, *rest), own.dtype)] * n,
+        in_specs=[vmem] * 2,
+        out_specs=[vmem] * n,
+        compiler_params=PARAMS,
+        name="pair_up",
+    )(own, mate)
+
+
+def gather_grads(pairs):
+    src = 2 * len(pairs)
+    _, _, T, D = pairs[0].shape
 
     def body(*refs):
         me = lax.axis_index("head")
-        ins, outs, held, wide = refs[:src], refs[src : src + 2], refs[-2], refs[-1]
+        ins, outs, held, wide = refs[: src // 2], refs[src // 2 : src // 2 + 2], refs[-2], refs[-1]
         for j in range(src):
-            held[me ^ j] = ins[j][...]
+            held[me ^ j] = ins[j // 2][j % 2]
         for c in range(2):
             for g in range(src):
                 wide[:, g, :] = held[g, c].astype(f32)
@@ -195,12 +214,12 @@
     return pl.pallas_call(
         body,
         out_shape=[jax.ShapeDtypeStruct((T, src, D), bf16)] * 2,
-        in_specs=[vmem] * src,
+        in_specs=[vmem] * (src // 2),
         out_specs=[vmem] * 2,
         scratch_shapes=[pltpu.VMEM((src, 2, T, D), bf16), pltpu.VMEM((T, src, D), f32)],
         compiler_params=PARAMS,
         name="gather_grads",
-    )(*pieces)
+    )(*pairs)
 
 
 def order_tables(block_order, spots_of, heads, inners, outers, keys_step):
@@ -325,11 +344,8 @@
             name,
         )
 
-    def to_peers(blocks):
-        return [blocks[0]] + [
-            lax.ppermute(blocks[j], "head", [(h, h ^ j) for h in range(heads)])
-            for j in range(1, heads)
-        ]
+    def to_head(x, turn):
+        return lax.ppermute(x, "head", [(h, h ^ turn) for h in range(heads)])
 
     dq, far_partner = part("far_partner", [kv_far_partner], [], False, [bf16])
     far_partner = lax.ppermute(far_partner, ring, back)
@@ -344,7 +360,9 @@
     partner = lax.ppermute(partner, ring, swap)
     dq, near = part("near", [kv], [dq], True, [f32])
     dq = exchange(dq)
-    grad = to_peers(add_by_peer(near, partner, far))
+    own, mate = add_by_peer(near, partner, far)
+    pairs = pair_up(own, to_head(mate, 1))
+    grad = [pairs[0]] + [to_head(pairs[k], 2 * k) for k in range(1, heads // 2)]
     dq = dq.reshape(q_heads, T, D).transpose(1, 0, 2)
     dq, grad = lax.optimization_barrier((dq, grad))
     return dq, *gather_grads(grad)

time: 98.2 us -> 97.3 us (level)
  waiting for transfers between devices: 26.5 us -> 29.8 us
  starting transfers between devices: 38.5 us -> 35.2 us
  Pallas kernels: 24.5 us -> 23.3 us
    ppermute x7 -> x4, starting transfers between devices: 8.12 us -> 4.88 us  [to_head(): return lax.ppermute(x, 'head', [(h, h ^ turn) for h in range(heads)])]
    all_to_all x3, waiting for transfers between devices: 2.58 us -> 5.66 us  [exchange(): return lax.all_to_all(x, 'head', split_axis=0, concat_axis=0, tiled=True)]
    pallas_call x4, Pallas kernels: 22.6 us -> 21.3 us  [attention_part(): pl.pallas_call(body, out_shape=(dq_out, *g_outs), in_specs=[smem] + [vmem...]
    ppermute x1, waiting for transfers between devices: 0.32 us -> 1.55 us  [shards(): kv_partner = lax.ppermute(kv_after, ring, swap)]
    ppermute x7 -> x4, waiting for transfers between devices: 3.59 us -> 2.55 us  [to_head(): return lax.ppermute(x, 'head', [(h, h ^ turn) for h in range(heads)])]
  transfers between devices with their start and end apart: 16 -> 13, of which waited for: 7 -> 8; matrix products, arithmetic and copies ran while one was open for 5% -> 5% of each run, Pallas kernels for 24% -> 23%
where the time goes in v5:
time: 97.3 us; the launch traced here: 96.5 us
  starting transfers between devices  35.2 us (36%)
  waiting for transfers between devices  29.8 us (31%)
  Pallas kernels  23.3 us (24%)
  local copies, waits for them, and re-layouts  3.95 us (4%)
  other arithmetic  3.39 us (3%)
    pallas_call x4, Pallas kernels, attention_part(): pl.pallas_call(body, out_shape=(dq_out, *g_outs), in_specs=[smem] + [vmem...  21.3 us
    ppermute x1, waiting for transfers between devices, shards(): kv_far_partner = lax.ppermute(kv, ring, across)  15.8 us
    all_to_all x3, starting transfers between devices, exchange(): return lax.all_to_all(x, 'head', split_axis=0, concat_axis=0, tiled=True)  12.4 us
    ppermute x1, starting transfers between devices, shards(): kv_far_partner = lax.ppermute(kv, ring, across)  7.29 us
    ppermute x1, starting transfers between devices, shards(): kv_partner = lax.ppermute(kv_after, ring, swap)  6.75 us
    all_to_all x3, waiting for transfers between devices, exchange(): return lax.all_to_all(x, 'head', split_axis=0, concat_axis=0, tiled=True)  5.66 us
    ppermute x4, starting transfers between devices, to_head(): return lax.ppermute(x, 'head', [(h, h ^ turn) for h in range(heads)])  4.88 us
    ppermute x1, waiting for transfers between devices, shards(): partner = lax.ppermute(partner, ring, swap)  4.2 us
  transfers between devices with their start and end apart: 13, of which 8 were waited for; matrix products, arithmetic and copies ran while one was open for 5% of the time, Pallas kernels for 23%

profile of v5, /device:TPU:32, one launch (start us, length us, event | category | flops | bytes accessed | tf_op | source)
XLA Modules:
  0.0 96.5 jit_solution(1578645015392727438)
XLA Ops:
  0.7 1.1 %copy_bitcast_fusion.1 = (bf16[8,1,64,128]{3,2,1,0:T(8,128)(2,1)S(1)}, bf16[8,1,64,128]{3,2,1,0:T(8,128)(2,1)S(1)}) fusion(bf16[64,8,128]{2,1,0:T(8,128)(2,1)} %param.9, bf16[64,8,128]{2,1,0:T(8,128)(2,1)} %param.8), kind=kLoop, calls=%fused_computation.9 | loop fusion | bytes 524288 | tf_op jit(solution)/shard_map/transpose | solution.py:303
  1.8 0.7 pad_maximum_fusion.1
  2.5 4.5 %all-to-all-start.1 = ((bf16[8,2,64,128]{3,2,1,0:T(8,128)(2,1)}), bf16[8,2,64,128]{3,2,1,0:T(8,128)(2,1)S(1)}, u32[]{:S(2)}, u32[]{:S(2)}) async-start(bf16[8,2,64,128]{3,2,1,0:T(8,128)(2,1)} %pad_maximum_fusion.1), calls=%async_computation.1 | async-start | bytes 524288 | tf_op jit(solution)/shard_map/all_to_all | solution.py:300
  7.0 0.7 copy-done
  7.7 0.9 order_tables.1.table
  8.5 0.7 broadcast_multiply_fusion
  9.3 0.2 copy.25
  9.5 0.5 multiply_reduce_fusion
  10.4 0.2 copy.24
  10.6 1.3 %pad_maximum_fusion = bf16[8,800,128]{2,1,0:T(8,128)(2,1)} fusion(bf16[8,32,128]{2,1,0:T(8,128)(2,1)S(1)} %fusion.4, bf16[8,384,128]{2,1,0:T(8,128)(2,1)S(1)} %bitcast.29, bf16[8,384,128]{2,1,0:T(8,128)(2,1)S(1)} %bitcast.30), kind=kLoop, calls=%fused_computation | loop fusion | flops 4915200 | bytes 3276800 | tf_op jit(solution)/shard_map/concatenate | solution.py:331
  12.0 2.6 %all-to-all-done.1.rest_0_ = bf16[8,2,64,128]{3,2,1,0:T(8,128)(2,1)S(1)} async-done(((bf16[8,2,64,128]{3,2,1,0:T(8,128)(2,1)}), bf16[8,2,64,128]{3,2,1,0:T(8,128)(2,1)S(1)}, u32[]{:S(2)}, u32[]{:S(2)}) %all-to-all-start.1) | async-done | bytes 262176 | tf_op jit(solution)/shard_map/all_to_all | solution.py:300
  14.5 3.6 %all-to-all-start = ((bf16[8,800,128]{2,1,0:T(8,128)(2,1)}), bf16[8,800,128]{2,1,0:T(8,128)(2,1)S(1)}, u32[]{:S(2)}, u32[]{:S(2)}) async-start(bf16[8,800,128]{2,1,0:T(8,128)(2,1)} %pad_maximum_fusion), calls=%async_computation | async-start | bytes 3276800 | tf_op jit(solution)/shard_map/all_to_all | solution.py:300
  18.1 7.3 %collective-permute-start = (bf16[8,2,64,128]{3,2,1,0:T(8,128)(2,1)S(1)}, bf16[8,2,64,128]{3,2,1,0:T(8,128)(2,1)S(1)}, u32[]{:S(2)}, u32[]{:S(2)}) collective-permute-start(bf16[8,2,64,128]{3,2,1,0:T(8,128)(2,1)S(1)} %all-to-all-done.1.rest_0_), channel_id=1, source_target_pairs={{16,1},{17,2},{18,3},{19,4},{20,5},{21,6},{22,7},{23,8},{24,9},{25... | collective-permute-start | bytes 786440 | tf_op jit(solution)/shard_map/ppermute | solution.py:306
  25.4 1.5 %collective-permute-start.1 = (bf16[8,2,64,128]{3,2,1,0:T(8,128)(2,1)S(1)}, bf16[8,2,64,128]{3,2,1,0:T(8,128)(2,1)S(1)}, u32[]{:S(2)}, u32[]{:S(2)}) collective-permute-start(bf16[8,2,64,128]{3,2,1,0:T(8,128)(2,1)S(1)} %all-to-all-done.1.rest_0_), channel_id=1, source_target_pairs={{0,1},{1,2},{2,3},{3,4},{4,5},{5,6},{6,7},{7,8},{8,9},{9,10},{10,1... | collective-permute-start | bytes 786440 | tf_op jit(solution)/shard_map/ppermute | solution.py:307
  26.9 15.8 %collective-permute-done.rest_0_ = bf16[8,2,64,128]{3,2,1,0:T(8,128)(2,1)S(1)} collective-permute-done((bf16[8,2,64,128]{3,2,1,0:T(8,128)(2,1)S(1)}, bf16[8,2,64,128]{3,2,1,0:T(8,128)(2,1)S(1)}, u32[]{:S(2)}, u32[]{:S(2)}) %collective-permute-start) | collective-permute-done | bytes 262176 | tf_op jit(solution)/shard_map/ppermute | solution.py:306
  42.8 6.7 %collective-permute-start.2 = (bf16[8,2,64,128]{3,2,1,0:T(8,128)(2,1)S(1)}, bf16[8,2,64,128]{3,2,1,0:T(8,128)(2,1)S(1)}, u32[]{:S(2)}, u32[]{:S(2)}) collective-permute-start(bf16[8,2,64,128]{3,2,1,0:T(8,128)(2,1)S(1)} %all-to-all-done.1.rest_0_), channel_id=1, source_target_pairs={{16,0},{17,1},{18,2},{19,3},{20,4},{21,5},{22,6},{23,7},{24,8},{25... | collective-permute-start | bytes 786440 | tf_op jit(solution)/shard_map/ppermute | solution.py:309
  49.5 4.8 %far_partner.1 = (f32[128,3072]{1,0:T(8,128)S(1)}, bf16[8,2,64,128]{3,2,1,0:T(8,128)(2,1)S(1)}) custom-call(s32[16,128]{1,0:T(8,128)S(1)} %order_tables.1.table, bf16[8,800,128]{2,1,0:T(8,128)(2,1)S(1)} %all-to-all-done.packed_ref, bf16[8,2,64,128]{3,2,1,0:T(8,128)(2,1)S(1)} %collective-permute-done.rest_0_), custom_call_target="tpu_custom_call" | custom-call | flops 1 | bytes 1 | tf_op jit(solution)/shard_map/far_partner/pallas_call | solution.py:146
  54.4 4.8 %far.1 = (f32[128,3072]{1,0:T(8,128)S(1)}, bf16[8,2,64,128]{3,2,1,0:T(8,128)(2,1)S(1)}) custom-call(s32[16,128]{1,0:T(8,128)S(1)} %order_tables.1.table, bf16[8,800,128]{2,1,0:T(8,128)(2,1)S(1)} %all-to-all-done.packed_ref, bf16[8,2,64,128]{3,2,1,0:T(8,128)(2,1)S(1)} %collective-permute-done.1.rest_0_), custom_call_target="tpu_custom_call" | custom-call | flops 1 | bytes 1 | tf_op jit(solution)/shard_map/far/pallas_call | solution.py:146
  59.2 1.6 %collective-permute-done.2.rest_0_ = bf16[8,2,64,128]{3,2,1,0:T(8,128)(2,1)S(1)} collective-permute-done((bf16[8,2,64,128]{3,2,1,0:T(8,128)(2,1)S(1)}, bf16[8,2,64,128]{3,2,1,0:T(8,128)(2,1)S(1)}, u32[]{:S(2)}, u32[]{:S(2)}) %collective-permute-start.2) | collective-permute-done | bytes 262176 | tf_op jit(solution)/shard_map/ppermute | solution.py:309
  60.8 6.0 %near_partner.1 = (f32[128,3072]{1,0:T(8,128)S(1)}, f32[8,2,64,128]{3,2,1,0:T(8,128)S(1)}) custom-call(s32[16,128]{1,0:T(8,128)S(1)} %order_tables.1.table, bf16[8,800,128]{2,1,0:T(8,128)(2,1)S(1)} %all-to-all-done.packed_ref, bf16[8,2,64,128]{3,2,1,0:T(8,128)(2,1)S(1)} %collective-permute-done.2.rest_0_, f32[128,3072]{1,0:T(8,128)S(1)} %get-tuple-element.33.rest_1_, ...), custom_call_target="tpu_custom_call" | custom-call | flops 1 | bytes 1 | tf_op jit(solution)/shard_map/near_partner/pallas_call | solution.py:146
  66.9 2.3 %collective-permute-start.4 = (bf16[8,2,64,128]{3,2,1,0:T(8,128)(2,1)S(1)}, bf16[8,2,64,128]{3,2,1,0:T(8,128)(2,1)S(1)}, u32[]{:S(2)}, u32[]{:S(2)}) collective-permute-start(bf16[8,2,64,128]{3,2,1,0:T(8,128)(2,1)S(1)} %add_convert_fusion), channel_id=1, source_target_pairs={{16,0},{17,1},{18,2},{19,3},{20,4},{21,5},{22,6},{23,7},{24,8},{25... | collective-permute-start | bytes 786440 | tf_op jit(solution)/shard_map/ppermute | solution.py:360
  69.2 5.8 %near.1 = (bf16[8,384,128]{2,1,0:T(8,128)(2,1)}, f32[8,2,64,128]{3,2,1,0:T(8,128)S(1)}) custom-call(s32[16,128]{1,0:T(8,128)S(1)} %order_tables.1.table, bf16[8,800,128]{2,1,0:T(8,128)(2,1)S(1)} %all-to-all-done.packed_ref, bf16[8,2,64,128]{3,2,1,0:T(8,128)(2,1)S(1)} %all-to-all-done.1.rest_0_, f32[128,3072]{1,0:T(8,128)S(1)} %get-tuple-element.38.rest_1_), custom_call_target="tpu_custom_call" | custom-call | flops 1 | bytes 1 | tf_op jit(solution)/shard_map/near/pallas_call | solution.py:146
  75.0 4.3 %all-to-all-start.2 = ((bf16[8,384,128]{2,1,0:T(8,128)(2,1)}), bf16[8,384,128]{2,1,0:T(8,128)(2,1)S(1)}, u32[]{:S(2)}, u32[]{:S(2)}) async-start(bf16[8,384,128]{2,1,0:T(8,128)(2,1)} %get-tuple-element.39), calls=%async_computation.2 | async-start | bytes 1572864 | tf_op jit(solution)/shard_map/all_to_all | solution.py:300
  79.3 4.2 %collective-permute-done.4.refs_1_ = bf16[8,2,64,128]{3,2,1,0:T(8,128)(2,1)S(1)} collective-permute-done((bf16[8,2,64,128]{3,2,1,0:T(8,128)(2,1)S(1)}, bf16[8,2,64,128]{3,2,1,0:T(8,128)(2,1)S(1)}, u32[]{:S(2)}, u32[]{:S(2)}) %collective-permute-start.4) | collective-permute-done | bytes 262176 | tf_op jit(solution)/shard_map/ppermute | solution.py:360
  83.7 1.3 %collective-permute-done.6.mate_ref = bf16[4,2,64,128]{3,2,1,0:T(8,128)(2,1)S(1)} collective-permute-done((bf16[4,2,64,128]{3,2,1,0:T(8,128)(2,1)S(1)}, bf16[4,2,64,128]{3,2,1,0:T(8,128)(2,1)S(1)}, u32[]{:S(2)}, u32[]{:S(2)}) %collective-permute-start.6) | collective-permute-done | bytes 131104 | tf_op jit(solution)/shard_map/ppermute | solution.py:348
  85.1 1.0 %collective-permute-start.7 = (bf16[2,2,64,128]{3,2,1,0:T(8,128)(2,1)S(1)}, bf16[2,2,64,128]{3,2,1,0:T(8,128)(2,1)S(1)}, u32[]{:S(2)}, u32[]{:S(2)}) collective-permute-start(bf16[2,2,64,128]{3,2,1,0:T(8,128)(2,1)S(1)} %get-tuple-element.47), channel_id=1, source_target_pairs={{0,64},{32,96},{64,0},{96,32},{128,192},{160,224},{192,128},{224,1... | collective-permute-start | bytes 196616 | tf_op jit(solution)/shard_map/ppermute | solution.py:348
  86.1 2.6 %collective-permute-start.8 = (bf16[2,2,64,128]{3,2,1,0:T(8,128)(2,1)S(1)}, bf16[2,2,64,128]{3,2,1,0:T(8,128)(2,1)S(1)}, u32[]{:S(2)}, u32[]{:S(2)}) collective-permute-start(bf16[2,2,64,128]{3,2,1,0:T(8,128)(2,1)S(1)} %get-tuple-element.48), channel_id=1, source_target_pairs={{0,128},{32,160},{64,192},{96,224},{128,0},{160,32},{192,64},{224,... | collective-permute-start | bytes 196616 | tf_op jit(solution)/shard_map/ppermute | solution.py:348
  88.7 1.1 %collective-permute-start.9 = (bf16[2,2,64,128]{3,2,1,0:T(8,128)(2,1)S(1)}, bf16[2,2,64,128]{3,2,1,0:T(8,128)(2,1)S(1)}, u32[]{:S(2)}, u32[]{:S(2)}) collective-permute-start(bf16[2,2,64,128]{3,2,1,0:T(8,128)(2,1)S(1)} %get-tuple-element.49), channel_id=1, source_target_pairs={{0,192},{32,224},{64,128},{96,160},{128,64},{160,96},{192,0},{224,... | collective-permute-start | bytes 196616 | tf_op jit(solution)/shard_map/ppermute | solution.py:348
  89.8 3.1 %all-to-all-done.2 = bf16[8,384,128]{2,1,0:T(8,128)(2,1)S(1)} async-done(((bf16[8,384,128]{2,1,0:T(8,128)(2,1)}), bf16[8,384,128]{2,1,0:T(8,128)(2,1)S(1)}, u32[]{:S(2)}, u32[]{:S(2)}) %all-to-all-start.2) | async-done | bytes 786464 | tf_op jit(solution)/shard_map/all_to_all | solution.py:300
  92.9 1.4 %copy.32 = bf16[48,64,128]{2,0,1:T(8,128)(2,1)} copy(bf16[48,64,128]{2,1,0:T(8,128)(2,1)S(1)} %bitcast.28) | data formatting | bytes 1572864 | tf_op jit(solution)/shard_map/reshape | solution.py:366
  94.3 1.0 %collective-permute-done.8.refs_2_ = bf16[2,2,64,128]{3,2,1,0:T(8,128)(2,1)S(1)} collective-permute-done((bf16[2,2,64,128]{3,2,1,0:T(8,128)(2,1)S(1)}, bf16[2,2,64,128]{3,2,1,0:T(8,128)(2,1)S(1)}, u32[]{:S(2)}, u32[]{:S(2)}) %collective-permute-start.8) | collective-permute-done | bytes 65568 | tf_op jit(solution)/shard_map/ppermute | solution.py:348
  95.5 1.0 %gather_grads.1 = (bf16[64,8,128]{2,1,0:T(8,128)(2,1)}, bf16[64,8,128]{2,1,0:T(8,128)(2,1)}) custom-call(bf16[2,2,64,128]{3,2,1,0:T(8,128)(2,1)S(1)} %get-tuple-element.51.refs_0_, bf16[2,2,64,128]{3,2,1,0:T(8,128)(2,1)S(1)} %collective-permute-done.7.refs_1_, bf16[2,2,64,128]{3,2,1,0:T(8,128)(2,1)S(1)} %collective-permute-done.8.refs_2_, ...), custom_call_target="tpu_custom_call" | custom-call | tf_op jit(solution)/shard_map/gather_grads/pallas_call | solution.py:214
  (27 shorter events, 1.0 us)
Async XLA Ops:
  0.6 8.7 %copy-start.1 = (bf16[64,48,128]{2,1,0:T(8,128)(2,1)S(1)}, bf16[64,48,128]{2,1,0:T(8,128)(2,1)}, u32[]{:S(2)}) copy-start(bf16[64,48,128]{2,1,0:T(8,128)(2,1)} %param.11) | copy-start | bytes 2359300
  0.6 8.9 %copy-start.2 = (bf16[64,48,128]{2,1,0:T(8,128)(2,1)S(1)}, bf16[64,48,128]{2,1,0:T(8,128)(2,1)}, u32[]{:S(2)}) copy-start(bf16[64,48,128]{2,1,0:T(8,128)(2,1)} %param.10) | copy-start | bytes 2359300
  2.5 12.0 %all-to-all-start.1 = ((bf16[8,2,64,128]{3,2,1,0:T(8,128)(2,1)}), bf16[8,2,64,128]{3,2,1,0:T(8,128)(2,1)S(1)}, u32[]{:S(2)}, u32[]{:S(2)}) async-start(bf16[8,2,64,128]{3,2,1,0:T(8,128)(2,1)} %pad_maximum_fusion.1), calls=%async_computation.1 | async-start | bytes 524288 | tf_op jit(solution)/shard_map/all_to_all | solution.py:300
  7.0 0.7 copy-start
  9.3 1.1 %copy-start.3 = (bf16[64,48,128]{2,1,0:T(8,128)(2,1)S(1)}, bf16[64,48,128]{2,1,0:T(8,128)(2,1)}, u32[]{:S(2)}) copy-start(bf16[64,48,128]{2,1,0:T(8,128)(2,1)} %param.7) | copy-start | bytes 2359300
  14.5 35.0 %all-to-all-start = ((bf16[8,800,128]{2,1,0:T(8,128)(2,1)}), bf16[8,800,128]{2,1,0:T(8,128)(2,1)S(1)}, u32[]{:S(2)}, u32[]{:S(2)}) async-start(bf16[8,800,128]{2,1,0:T(8,128)(2,1)} %pad_maximum_fusion), calls=%async_computation | async-start | bytes 3276800 | tf_op jit(solution)/shard_map/all_to_all | solution.py:300
  18.1 24.6 %collective-permute-start = (bf16[8,2,64,128]{3,2,1,0:T(8,128)(2,1)S(1)}, bf16[8,2,64,128]{3,2,1,0:T(8,128)(2,1)S(1)}, u32[]{:S(2)}, u32[]{:S(2)}) collective-permute-start(bf16[8,2,64,128]{3,2,1,0:T(8,128)(2,1)S(1)} %all-to-all-done.1.rest_0_), channel_id=1, source_target_pairs={{16,1},{17,2},{18,3},{19,4},{20,5},{21,6},{22,7},{23,8},{24,9},{25... | collective-permute-start | bytes 786440 | tf_op jit(solution)/shard_map/ppermute | solution.py:306
  25.4 28.9 %collective-permute-start.1 = (bf16[8,2,64,128]{3,2,1,0:T(8,128)(2,1)S(1)}, bf16[8,2,64,128]{3,2,1,0:T(8,128)(2,1)S(1)}, u32[]{:S(2)}, u32[]{:S(2)}) collective-permute-start(bf16[8,2,64,128]{3,2,1,0:T(8,128)(2,1)S(1)} %all-to-all-done.1.rest_0_), channel_id=1, source_target_pairs={{0,1},{1,2},{2,3},{3,4},{4,5},{5,6},{6,7},{7,8},{8,9},{9,10},{10,1... | collective-permute-start | bytes 786440 | tf_op jit(solution)/shard_map/ppermute | solution.py:307
  42.8 18.0 %collective-permute-start.2 = (bf16[8,2,64,128]{3,2,1,0:T(8,128)(2,1)S(1)}, bf16[8,2,64,128]{3,2,1,0:T(8,128)(2,1)S(1)}, u32[]{:S(2)}, u32[]{:S(2)}) collective-permute-start(bf16[8,2,64,128]{3,2,1,0:T(8,128)(2,1)S(1)} %all-to-all-done.1.rest_0_), channel_id=1, source_target_pairs={{16,0},{17,1},{18,2},{19,3},{20,4},{21,5},{22,6},{23,7},{24,8},{25... | collective-permute-start | bytes 786440 | tf_op jit(solution)/shard_map/ppermute | solution.py:309
  54.3 12.6 %collective-permute-start.3 = (bf16[8,2,64,128]{3,2,1,0:T(8,128)(2,1)S(1)}, bf16[8,2,64,128]{3,2,1,0:T(8,128)(2,1)S(1)}, u32[]{:S(2)}, u32[]{:S(2)}) collective-permute-start(bf16[8,2,64,128]{3,2,1,0:T(8,128)(2,1)S(1)} %get-tuple-element.42), channel_id=1, source_target_pairs={{1,0},{2,1},{3,2},{4,3},{5,4},{6,5},{7,6},{8,7},{9,8},{10,9},{11,1... | collective-permute-start | bytes 786440 | tf_op jit(solution)/shard_map/ppermute | solution.py:351
  59.1 20.2 %collective-permute-start.5 = (bf16[8,2,64,128]{3,2,1,0:T(8,128)(2,1)S(1)}, bf16[8,2,64,128]{3,2,1,0:T(8,128)(2,1)S(1)}, u32[]{:S(2)}, u32[]{:S(2)}) collective-permute-start(bf16[8,2,64,128]{3,2,1,0:T(8,128)(2,1)S(1)} %get-tuple-element.43), channel_id=1, source_target_pairs={{1,0},{2,1},{3,2},{4,3},{5,4},{6,5},{7,6},{8,7},{9,8},{10,9},{11,1... | collective-permute-start | bytes 786440 | tf_op jit(solution)/shard_map/ppermute | solution.py:355
  66.9 16.6 %collective-permute-start.4 = (bf16[8,2,64,128]{3,2,1,0:T(8,128)(2,1)S(1)}, bf16[8,2,64,128]{3,2,1,0:T(8,128)(2,1)S(1)}, u32[]{:S(2)}, u32[]{:S(2)}) collective-permute-start(bf16[8,2,64,128]{3,2,1,0:T(8,128)(2,1)S(1)} %add_convert_fusion), channel_id=1, source_target_pairs={{16,0},{17,1},{18,2},{19,3},{20,4},{21,5},{22,6},{23,7},{24,8},{25... | collective-permute-start | bytes 786440 | tf_op jit(solution)/shard_map/ppermute | solution.py:360
  75.0 18.0 %all-to-all-start.2 = ((bf16[8,384,128]{2,1,0:T(8,128)(2,1)}), bf16[8,384,128]{2,1,0:T(8,128)(2,1)S(1)}, u32[]{:S(2)}, u32[]{:S(2)}) async-start(bf16[8,384,128]{2,1,0:T(8,128)(2,1)} %get-tuple-element.39), calls=%async_computation.2 | async-start | bytes 1572864 | tf_op jit(solution)/shard_map/all_to_all | solution.py:300
  83.6 1.4 %collective-permute-start.6 = (bf16[4,2,64,128]{3,2,1,0:T(8,128)(2,1)S(1)}, bf16[4,2,64,128]{3,2,1,0:T(8,128)(2,1)S(1)}, u32[]{:S(2)}, u32[]{:S(2)}) collective-permute-start(bf16[4,2,64,128]{3,2,1,0:T(8,128)(2,1)S(1)} %get-tuple-element.45), channel_id=1, source_target_pairs={{0,32},{32,0},{64,96},{96,64},{128,160},{160,128},{192,224},{224,1... | collective-permute-start | bytes 393224 | tf_op jit(solution)/shard_map/ppermute | solution.py:348
  85.1 9.3 %collective-permute-start.7 = (bf16[2,2,64,128]{3,2,1,0:T(8,128)(2,1)S(1)}, bf16[2,2,64,128]{3,2,1,0:T(8,128)(2,1)S(1)}, u32[]{:S(2)}, u32[]{:S(2)}) collective-permute-start(bf16[2,2,64,128]{3,2,1,0:T(8,128)(2,1)S(1)} %get-tuple-element.47), channel_id=1, source_target_pairs={{0,64},{32,96},{64,0},{96,32},{128,192},{160,224},{192,128},{224,1... | collective-permute-start | bytes 196616 | tf_op jit(solution)/shard_map/ppermute | solution.py:348
  86.1 9.3 %collective-permute-start.8 = (bf16[2,2,64,128]{3,2,1,0:T(8,128)(2,1)S(1)}, bf16[2,2,64,128]{3,2,1,0:T(8,128)(2,1)S(1)}, u32[]{:S(2)}, u32[]{:S(2)}) collective-permute-start(bf16[2,2,64,128]{3,2,1,0:T(8,128)(2,1)S(1)} %get-tuple-element.48), channel_id=1, source_target_pairs={{0,128},{32,160},{64,192},{96,224},{128,0},{160,32},{192,64},{224,... | collective-permute-start | bytes 196616 | tf_op jit(solution)/shard_map/ppermute | solution.py:348
  88.7 6.8 %collective-permute-start.9 = (bf16[2,2,64,128]{3,2,1,0:T(8,128)(2,1)S(1)}, bf16[2,2,64,128]{3,2,1,0:T(8,128)(2,1)S(1)}, u32[]{:S(2)}, u32[]{:S(2)}) collective-permute-start(bf16[2,2,64,128]{3,2,1,0:T(8,128)(2,1)S(1)} %get-tuple-element.49), channel_id=1, source_target_pairs={{0,192},{32,224},{64,128},{96,160},{128,64},{160,96},{192,0},{224,... | collective-permute-start | bytes 196616 | tf_op jit(solution)/shard_map/ppermute | solution.py:348

commit v6 on v5

--- a/solution.py
+++ b/solution.py
@@ -81,9 +81,10 @@
                     for j in range(keys_step):
                         behind = (kord(g * keys_step + j) - place) * T
                         cut = (slice(j * T, (j + 1) * T), slice(h * R, (h + 1) * R))
-                        p = jnp.where(
-                            lead >= behind, jnp.exp2(s[cut] * (scale * LOG2E) - lse), 0.0
-                        )
+                        shift = lse if last else lse + jnp.where(behind > 0, 1e30, 0.0)
+                        p = jnp.exp2(s[cut] * (scale * LOG2E) - shift)
+                        if last:
+                            p = jnp.where(lead >= behind, p, 0.0)
                         ds_rows.append((p * (dp[cut] - delta)).astype(bf16))
                         p_rows.append(p.astype(bf16))
                     p_cols.append(jnp.concatenate(p_rows, axis=0))

time: 97.3 us -> 97.3 us (level)
  starting transfers between devices: 35.2 us -> 37.7 us
  waiting for transfers between devices: 29.8 us -> 28.6 us
    ppermute x1, starting transfers between devices: 2.28 us -> 4.7 us  [shards(): partner = lax.ppermute(partner, ring, swap)]
    ppermute x1, waiting for transfers between devices: 4.2 us -> 2.94 us  [shards(): partner = lax.ppermute(partner, ring, swap)]
    all_to_all x3, waiting for transfers between devices: 5.66 us -> 6.75 us  [exchange(): return lax.all_to_all(x, 'head', split_axis=0, concat_axis=0, tiled=True)]
  transfers between devices with their start and end apart: 13 -> 13, of which waited for: 8 -> 7; matrix products, arithmetic and copies ran while one was open for 5% -> 5% of each run, Pallas kernels for 23% -> 22%
where the time goes in v6:
time: 97.3 us; the launch traced here: 97.2 us
  starting transfers between devices  37.7 us (39%)
  waiting for transfers between devices  28.6 us (29%)
  Pallas kernels  22.6 us (23%)
  local copies, waits for them, and re-layouts  3.95 us (4%)
  other arithmetic  3.39 us (3%)
    pallas_call x4, Pallas kernels, attention_part(): pl.pallas_call(body, out_shape=(dq_out, *g_outs), in_specs=[smem] + [vmem...  20.7 us
    ppermute x1, waiting for transfers between devices, shards(): kv_far_partner = lax.ppermute(kv, ring, across)  15.8 us
    all_to_all x3, starting transfers between devices, exchange(): return lax.all_to_all(x, 'head', split_axis=0, concat_axis=0, tiled=True)  12.3 us
    ppermute x1, starting transfers between devices, shards(): kv_far_partner = lax.ppermute(kv, ring, across)  7.29 us
    ppermute x1, starting transfers between devices, shards(): kv_partner = lax.ppermute(kv_after, ring, swap)  6.75 us
    all_to_all x3, waiting for transfers between devices, exchange(): return lax.all_to_all(x, 'head', split_axis=0, concat_axis=0, tiled=True)  6.75 us
    ppermute x4, starting transfers between devices, to_head(): return lax.ppermute(x, 'head', [(h, h ^ turn) for h in range(heads)])  5.07 us
    ppermute x1, starting transfers between devices, shards(): partner = lax.ppermute(partner, ring, swap)  4.7 us
  transfers between devices with their start and end apart: 13, of which 7 were waited for; matrix products, arithmetic and copies ran while one was open for 5% of the time, Pallas kernels for 22%

profile of v6, /device:TPU:32, one launch (start us, length us, event | category | flops | bytes accessed | tf_op | source)
XLA Modules:
  0.0 97.2 jit_solution(11343456191932746233)
XLA Ops:
  0.7 1.1 %copy_bitcast_fusion.1 = (bf16[8,1,64,128]{3,2,1,0:T(8,128)(2,1)S(1)}, bf16[8,1,64,128]{3,2,1,0:T(8,128)(2,1)S(1)}) fusion(bf16[64,8,128]{2,1,0:T(8,128)(2,1)} %param.9, bf16[64,8,128]{2,1,0:T(8,128)(2,1)} %param.8), kind=kLoop, calls=%fused_computation.9 | loop fusion | bytes 524288 | tf_op jit(solution)/shard_map/transpose | solution.py:304
  1.8 0.7 pad_maximum_fusion.1
  2.5 4.5 %all-to-all-start.1 = ((bf16[8,2,64,128]{3,2,1,0:T(8,128)(2,1)}), bf16[8,2,64,128]{3,2,1,0:T(8,128)(2,1)S(1)}, u32[]{:S(2)}, u32[]{:S(2)}) async-start(bf16[8,2,64,128]{3,2,1,0:T(8,128)(2,1)} %pad_maximum_fusion.1), calls=%async_computation.1 | async-start | bytes 524288 | tf_op jit(solution)/shard_map/all_to_all | solution.py:301
  7.0 0.7 copy-done
  7.7 0.9 order_tables.1.table
  8.5 0.7 broadcast_multiply_fusion
  9.3 0.2 copy.25
  9.5 0.5 multiply_reduce_fusion
  10.6 1.3 %pad_maximum_fusion = bf16[8,800,128]{2,1,0:T(8,128)(2,1)} fusion(bf16[8,32,128]{2,1,0:T(8,128)(2,1)S(1)} %fusion.4, bf16[8,384,128]{2,1,0:T(8,128)(2,1)S(1)} %bitcast.29, bf16[8,384,128]{2,1,0:T(8,128)(2,1)S(1)} %bitcast.30), kind=kLoop, calls=%fused_computation | loop fusion | flops 4915200 | bytes 3276800 | tf_op jit(solution)/shard_map/concatenate | solution.py:332
  12.0 2.6 %all-to-all-done.1.rest_0_ = bf16[8,2,64,128]{3,2,1,0:T(8,128)(2,1)S(1)} async-done(((bf16[8,2,64,128]{3,2,1,0:T(8,128)(2,1)}), bf16[8,2,64,128]{3,2,1,0:T(8,128)(2,1)S(1)}, u32[]{:S(2)}, u32[]{:S(2)}) %all-to-all-start.1) | async-done | bytes 262176 | tf_op jit(solution)/shard_map/all_to_all | solution.py:301
  14.5 3.6 %all-to-all-start = ((bf16[8,800,128]{2,1,0:T(8,128)(2,1)}), bf16[8,800,128]{2,1,0:T(8,128)(2,1)S(1)}, u32[]{:S(2)}, u32[]{:S(2)}) async-start(bf16[8,800,128]{2,1,0:T(8,128)(2,1)} %pad_maximum_fusion), calls=%async_computation | async-start | bytes 3276800 | tf_op jit(solution)/shard_map/all_to_all | solution.py:301
  18.1 7.3 %collective-permute-start = (bf16[8,2,64,128]{3,2,1,0:T(8,128)(2,1)S(1)}, bf16[8,2,64,128]{3,2,1,0:T(8,128)(2,1)S(1)}, u32[]{:S(2)}, u32[]{:S(2)}) collective-permute-start(bf16[8,2,64,128]{3,2,1,0:T(8,128)(2,1)S(1)} %all-to-all-done.1.rest_0_), channel_id=1, source_target_pairs={{16,1},{17,2},{18,3},{19,4},{20,5},{21,6},{22,7},{23,8},{24,9},{25... | collective-permute-start | bytes 786440 | tf_op jit(solution)/shard_map/ppermute | solution.py:307
  25.4 1.5 %collective-permute-start.1 = (bf16[8,2,64,128]{3,2,1,0:T(8,128)(2,1)S(1)}, bf16[8,2,64,128]{3,2,1,0:T(8,128)(2,1)S(1)}, u32[]{:S(2)}, u32[]{:S(2)}) collective-permute-start(bf16[8,2,64,128]{3,2,1,0:T(8,128)(2,1)S(1)} %all-to-all-done.1.rest_0_), channel_id=1, source_target_pairs={{0,1},{1,2},{2,3},{3,4},{4,5},{5,6},{6,7},{7,8},{8,9},{9,10},{10,1... | collective-permute-start | bytes 786440 | tf_op jit(solution)/shard_map/ppermute | solution.py:308
  26.9 15.8 %collective-permute-done.rest_0_ = bf16[8,2,64,128]{3,2,1,0:T(8,128)(2,1)S(1)} collective-permute-done((bf16[8,2,64,128]{3,2,1,0:T(8,128)(2,1)S(1)}, bf16[8,2,64,128]{3,2,1,0:T(8,128)(2,1)S(1)}, u32[]{:S(2)}, u32[]{:S(2)}) %collective-permute-start) | collective-permute-done | bytes 262176 | tf_op jit(solution)/shard_map/ppermute | solution.py:307
  42.8 6.7 %collective-permute-start.2 = (bf16[8,2,64,128]{3,2,1,0:T(8,128)(2,1)S(1)}, bf16[8,2,64,128]{3,2,1,0:T(8,128)(2,1)S(1)}, u32[]{:S(2)}, u32[]{:S(2)}) collective-permute-start(bf16[8,2,64,128]{3,2,1,0:T(8,128)(2,1)S(1)} %all-to-all-done.1.rest_0_), channel_id=1, source_target_pairs={{16,0},{17,1},{18,2},{19,3},{20,4},{21,5},{22,6},{23,7},{24,8},{25... | collective-permute-start | bytes 786440 | tf_op jit(solution)/shard_map/ppermute | solution.py:310
  49.5 4.5 %far_partner.1 = (f32[128,3072]{1,0:T(8,128)S(1)}, bf16[8,2,64,128]{3,2,1,0:T(8,128)(2,1)S(1)}) custom-call(s32[16,128]{1,0:T(8,128)S(1)} %order_tables.1.table, bf16[8,800,128]{2,1,0:T(8,128)(2,1)S(1)} %all-to-all-done.packed_ref, bf16[8,2,64,128]{3,2,1,0:T(8,128)(2,1)S(1)} %collective-permute-done.rest_0_), custom_call_target="tpu_custom_call" | custom-call | flops 1 | bytes 1 | tf_op jit(solution)/shard_map/far_partner/pallas_call | solution.py:147
  54.2 5.7 %far.1 = (f32[128,3072]{1,0:T(8,128)S(1)}, bf16[8,2,64,128]{3,2,1,0:T(8,128)(2,1)S(1)}) custom-call(s32[16,128]{1,0:T(8,128)S(1)} %order_tables.1.table, bf16[8,800,128]{2,1,0:T(8,128)(2,1)S(1)} %all-to-all-done.packed_ref, bf16[8,2,64,128]{3,2,1,0:T(8,128)(2,1)S(1)} %collective-permute-done.1.rest_0_), custom_call_target="tpu_custom_call" | custom-call | flops 1 | bytes 1 | tf_op jit(solution)/shard_map/far/pallas_call | solution.py:147
  60.0 0.8 collective-permute-done.2.rest_0_
  60.8 4.6 %near_partner.1 = (f32[128,3072]{1,0:T(8,128)S(1)}, f32[8,2,64,128]{3,2,1,0:T(8,128)S(1)}) custom-call(s32[16,128]{1,0:T(8,128)S(1)} %order_tables.1.table, bf16[8,800,128]{2,1,0:T(8,128)(2,1)S(1)} %all-to-all-done.packed_ref, bf16[8,2,64,128]{3,2,1,0:T(8,128)(2,1)S(1)} %collective-permute-done.2.rest_0_, f32[128,3072]{1,0:T(8,128)S(1)} %get-tuple-element.33.rest_1_, ...), custom_call_target="tpu_custom_call" | custom-call | flops 1 | bytes 1 | tf_op jit(solution)/shard_map/near_partner/pallas_call | solution.py:147
  65.5 4.7 %collective-permute-start.4 = (bf16[8,2,64,128]{3,2,1,0:T(8,128)(2,1)S(1)}, bf16[8,2,64,128]{3,2,1,0:T(8,128)(2,1)S(1)}, u32[]{:S(2)}, u32[]{:S(2)}) collective-permute-start(bf16[8,2,64,128]{3,2,1,0:T(8,128)(2,1)S(1)} %add_convert_fusion), channel_id=1, source_target_pairs={{16,0},{17,1},{18,2},{19,3},{20,4},{21,5},{22,6},{23,7},{24,8},{25... | collective-permute-start | bytes 786440 | tf_op jit(solution)/shard_map/ppermute | solution.py:361
  70.2 5.8 %near.1 = (bf16[8,384,128]{2,1,0:T(8,128)(2,1)}, f32[8,2,64,128]{3,2,1,0:T(8,128)S(1)}) custom-call(s32[16,128]{1,0:T(8,128)S(1)} %order_tables.1.table, bf16[8,800,128]{2,1,0:T(8,128)(2,1)S(1)} %all-to-all-done.packed_ref, bf16[8,2,64,128]{3,2,1,0:T(8,128)(2,1)S(1)} %all-to-all-done.1.rest_0_, f32[128,3072]{1,0:T(8,128)S(1)} %get-tuple-element.38.rest_1_), custom_call_target="tpu_custom_call" | custom-call | flops 1 | bytes 1 | tf_op jit(solution)/shard_map/near/pallas_call | solution.py:147
  76.0 4.2 %all-to-all-start.2 = ((bf16[8,384,128]{2,1,0:T(8,128)(2,1)}), bf16[8,384,128]{2,1,0:T(8,128)(2,1)S(1)}, u32[]{:S(2)}, u32[]{:S(2)}) async-start(bf16[8,384,128]{2,1,0:T(8,128)(2,1)} %get-tuple-element.39), calls=%async_computation.2 | async-start | bytes 1572864 | tf_op jit(solution)/shard_map/all_to_all | solution.py:301
  80.2 2.9 %collective-permute-done.4.refs_1_ = bf16[8,2,64,128]{3,2,1,0:T(8,128)(2,1)S(1)} collective-permute-done((bf16[8,2,64,128]{3,2,1,0:T(8,128)(2,1)S(1)}, bf16[8,2,64,128]{3,2,1,0:T(8,128)(2,1)S(1)}, u32[]{:S(2)}, u32[]{:S(2)}) %collective-permute-start.4) | collective-permute-done | bytes 262176 | tf_op jit(solution)/shard_map/ppermute | solution.py:361
  83.2 0.3 collective-permute-start.6
  83.5 1.3 %collective-permute-done.6.mate_ref = bf16[4,2,64,128]{3,2,1,0:T(8,128)(2,1)S(1)} collective-permute-done((bf16[4,2,64,128]{3,2,1,0:T(8,128)(2,1)S(1)}, bf16[4,2,64,128]{3,2,1,0:T(8,128)(2,1)S(1)}, u32[]{:S(2)}, u32[]{:S(2)}) %collective-permute-start.6) | collective-permute-done | bytes 131104 | tf_op jit(solution)/shard_map/ppermute | solution.py:349
  84.9 1.3 %collective-permute-start.7 = (bf16[2,2,64,128]{3,2,1,0:T(8,128)(2,1)S(1)}, bf16[2,2,64,128]{3,2,1,0:T(8,128)(2,1)S(1)}, u32[]{:S(2)}, u32[]{:S(2)}) collective-permute-start(bf16[2,2,64,128]{3,2,1,0:T(8,128)(2,1)S(1)} %get-tuple-element.47), channel_id=1, source_target_pairs={{0,64},{32,96},{64,0},{96,32},{128,192},{160,224},{192,128},{224,1... | collective-permute-start | bytes 196616 | tf_op jit(solution)/shard_map/ppermute | solution.py:349
  86.2 2.7 %collective-permute-start.8 = (bf16[2,2,64,128]{3,2,1,0:T(8,128)(2,1)S(1)}, bf16[2,2,64,128]{3,2,1,0:T(8,128)(2,1)S(1)}, u32[]{:S(2)}, u32[]{:S(2)}) collective-permute-start(bf16[2,2,64,128]{3,2,1,0:T(8,128)(2,1)S(1)} %get-tuple-element.48), channel_id=1, source_target_pairs={{0,128},{32,160},{64,192},{96,224},{128,0},{160,32},{192,64},{224,... | collective-permute-start | bytes 196616 | tf_op jit(solution)/shard_map/ppermute | solution.py:349
  88.8 0.8 collective-permute-start.9
  89.6 4.2 %all-to-all-done.2 = bf16[8,384,128]{2,1,0:T(8,128)(2,1)S(1)} async-done(((bf16[8,384,128]{2,1,0:T(8,128)(2,1)}), bf16[8,384,128]{2,1,0:T(8,128)(2,1)S(1)}, u32[]{:S(2)}, u32[]{:S(2)}) %all-to-all-start.2) | async-done | bytes 786464 | tf_op jit(solution)/shard_map/all_to_all | solution.py:301
  93.8 1.4 %copy.32 = bf16[48,64,128]{2,0,1:T(8,128)(2,1)} copy(bf16[48,64,128]{2,1,0:T(8,128)(2,1)S(1)} %bitcast.28) | data formatting | bytes 1572864 | tf_op jit(solution)/shard_map/reshape | solution.py:367
  95.2 0.9 collective-permute-done.8.refs_2_
  96.2 1.0 %gather_grads.1 = (bf16[64,8,128]{2,1,0:T(8,128)(2,1)}, bf16[64,8,128]{2,1,0:T(8,128)(2,1)}) custom-call(bf16[2,2,64,128]{3,2,1,0:T(8,128)(2,1)S(1)} %get-tuple-element.51.refs_0_, bf16[2,2,64,128]{3,2,1,0:T(8,128)(2,1)S(1)} %collective-permute-done.7.refs_1_, bf16[2,2,64,128]{3,2,1,0:T(8,128)(2,1)S(1)} %collective-permute-done.8.refs_2_, ...), custom_call_target="tpu_custom_call" | custom-call | tf_op jit(solution)/shard_map/gather_grads/pallas_call | solution.py:215
  (27 shorter events, 0.9 us)
Async XLA Ops:
  0.6 8.7 %copy-start.1 = (bf16[64,48,128]{2,1,0:T(8,128)(2,1)S(1)}, bf16[64,48,128]{2,1,0:T(8,128)(2,1)}, u32[]{:S(2)}) copy-start(bf16[64,48,128]{2,1,0:T(8,128)(2,1)} %param.11) | copy-start | bytes 2359300
  0.6 8.9 %copy-start.2 = (bf16[64,48,128]{2,1,0:T(8,128)(2,1)S(1)}, bf16[64,48,128]{2,1,0:T(8,128)(2,1)}, u32[]{:S(2)}) copy-start(bf16[64,48,128]{2,1,0:T(8,128)(2,1)} %param.10) | copy-start | bytes 2359300
  2.5 12.0 %all-to-all-start.1 = ((bf16[8,2,64,128]{3,2,1,0:T(8,128)(2,1)}), bf16[8,2,64,128]{3,2,1,0:T(8,128)(2,1)S(1)}, u32[]{:S(2)}, u32[]{:S(2)}) async-start(bf16[8,2,64,128]{3,2,1,0:T(8,128)(2,1)} %pad_maximum_fusion.1), calls=%async_computation.1 | async-start | bytes 524288 | tf_op jit(solution)/shard_map/all_to_all | solution.py:301
  7.0 0.7 copy-start
  9.3 1.1 %copy-start.3 = (bf16[64,48,128]{2,1,0:T(8,128)(2,1)S(1)}, bf16[64,48,128]{2,1,0:T(8,128)(2,1)}, u32[]{:S(2)}) copy-start(bf16[64,48,128]{2,1,0:T(8,128)(2,1)} %param.7) | copy-start | bytes 2359300
  14.5 35.0 %all-to-all-start = ((bf16[8,800,128]{2,1,0:T(8,128)(2,1)}), bf16[8,800,128]{2,1,0:T(8,128)(2,1)S(1)}, u32[]{:S(2)}, u32[]{:S(2)}) async-start(bf16[8,800,128]{2,1,0:T(8,128)(2,1)} %pad_maximum_fusion), calls=%async_computation | async-start | bytes 3276800 | tf_op jit(solution)/shard_map/all_to_all | solution.py:301
  18.1 24.6 %collective-permute-start = (bf16[8,2,64,128]{3,2,1,0:T(8,128)(2,1)S(1)}, bf16[8,2,64,128]{3,2,1,0:T(8,128)(2,1)S(1)}, u32[]{:S(2)}, u32[]{:S(2)}) collective-permute-start(bf16[8,2,64,128]{3,2,1,0:T(8,128)(2,1)S(1)} %all-to-all-done.1.rest_0_), channel_id=1, source_target_pairs={{16,1},{17,2},{18,3},{19,4},{20,5},{21,6},{22,7},{23,8},{24,9},{25... | collective-permute-start | bytes 786440 | tf_op jit(solution)/shard_map/ppermute | solution.py:307
  25.4 28.7 %collective-permute-start.1 = (bf16[8,2,64,128]{3,2,1,0:T(8,128)(2,1)S(1)}, bf16[8,2,64,128]{3,2,1,0:T(8,128)(2,1)S(1)}, u32[]{:S(2)}, u32[]{:S(2)}) collective-permute-start(bf16[8,2,64,128]{3,2,1,0:T(8,128)(2,1)S(1)} %all-to-all-done.1.rest_0_), channel_id=1, source_target_pairs={{0,1},{1,2},{2,3},{3,4},{4,5},{5,6},{6,7},{7,8},{8,9},{9,10},{10,1... | collective-permute-start | bytes 786440 | tf_op jit(solution)/shard_map/ppermute | solution.py:308
  42.8 18.0 %collective-permute-start.2 = (bf16[8,2,64,128]{3,2,1,0:T(8,128)(2,1)S(1)}, bf16[8,2,64,128]{3,2,1,0:T(8,128)(2,1)S(1)}, u32[]{:S(2)}, u32[]{:S(2)}) collective-permute-start(bf16[8,2,64,128]{3,2,1,0:T(8,128)(2,1)S(1)} %all-to-all-done.1.rest_0_), channel_id=1, source_target_pairs={{16,0},{17,1},{18,2},{19,3},{20,4},{21,5},{22,6},{23,7},{24,8},{25... | collective-permute-start | bytes 786440 | tf_op jit(solution)/shard_map/ppermute | solution.py:310
  54.1 11.3 %collective-permute-start.3 = (bf16[8,2,64,128]{3,2,1,0:T(8,128)(2,1)S(1)}, bf16[8,2,64,128]{3,2,1,0:T(8,128)(2,1)S(1)}, u32[]{:S(2)}, u32[]{:S(2)}) collective-permute-start(bf16[8,2,64,128]{3,2,1,0:T(8,128)(2,1)S(1)} %get-tuple-element.42), channel_id=1, source_target_pairs={{1,0},{2,1},{3,2},{4,3},{5,4},{6,5},{7,6},{8,7},{9,8},{10,9},{11,1... | collective-permute-start | bytes 786440 | tf_op jit(solution)/shard_map/ppermute | solution.py:352
  59.9 20.3 %collective-permute-start.5 = (bf16[8,2,64,128]{3,2,1,0:T(8,128)(2,1)S(1)}, bf16[8,2,64,128]{3,2,1,0:T(8,128)(2,1)S(1)}, u32[]{:S(2)}, u32[]{:S(2)}) collective-permute-start(bf16[8,2,64,128]{3,2,1,0:T(8,128)(2,1)S(1)} %get-tuple-element.43), channel_id=1, source_target_pairs={{1,0},{2,1},{3,2},{4,3},{5,4},{6,5},{7,6},{8,7},{9,8},{10,9},{11,1... | collective-permute-start | bytes 786440 | tf_op jit(solution)/shard_map/ppermute | solution.py:356
  65.5 17.7 %collective-permute-start.4 = (bf16[8,2,64,128]{3,2,1,0:T(8,128)(2,1)S(1)}, bf16[8,2,64,128]{3,2,1,0:T(8,128)(2,1)S(1)}, u32[]{:S(2)}, u32[]{:S(2)}) collective-permute-start(bf16[8,2,64,128]{3,2,1,0:T(8,128)(2,1)S(1)} %add_convert_fusion), channel_id=1, source_target_pairs={{16,0},{17,1},{18,2},{19,3},{20,4},{21,5},{22,6},{23,7},{24,8},{25... | collective-permute-start | bytes 786440 | tf_op jit(solution)/shard_map/ppermute | solution.py:361
  76.0 17.8 %all-to-all-start.2 = ((bf16[8,384,128]{2,1,0:T(8,128)(2,1)}), bf16[8,384,128]{2,1,0:T(8,128)(2,1)S(1)}, u32[]{:S(2)}, u32[]{:S(2)}) async-start(bf16[8,384,128]{2,1,0:T(8,128)(2,1)} %get-tuple-element.39), calls=%async_computation.2 | async-start | bytes 1572864 | tf_op jit(solution)/shard_map/all_to_all | solution.py:301
  83.2 1.6 %collective-permute-start.6 = (bf16[4,2,64,128]{3,2,1,0:T(8,128)(2,1)S(1)}, bf16[4,2,64,128]{3,2,1,0:T(8,128)(2,1)S(1)}, u32[]{:S(2)}, u32[]{:S(2)}) collective-permute-start(bf16[4,2,64,128]{3,2,1,0:T(8,128)(2,1)S(1)} %get-tuple-element.45), channel_id=1, source_target_pairs={{0,32},{32,0},{64,96},{96,64},{128,160},{160,128},{192,224},{224,1... | collective-permute-start | bytes 393224 | tf_op jit(solution)/shard_map/ppermute | solution.py:349
  84.9 10.4 %collective-permute-start.7 = (bf16[2,2,64,128]{3,2,1,0:T(8,128)(2,1)S(1)}, bf16[2,2,64,128]{3,2,1,0:T(8,128)(2,1)S(1)}, u32[]{:S(2)}, u32[]{:S(2)}) collective-permute-start(bf16[2,2,64,128]{3,2,1,0:T(8,128)(2,1)S(1)} %get-tuple-element.47), channel_id=1, source_target_pairs={{0,64},{32,96},{64,0},{96,32},{128,192},{160,224},{192,128},{224,1... | collective-permute-start | bytes 196616 | tf_op jit(solution)/shard_map/ppermute | solution.py:349
  86.2 10.0 %collective-permute-start.8 = (bf16[2,2,64,128]{3,2,1,0:T(8,128)(2,1)S(1)}, bf16[2,2,64,128]{3,2,1,0:T(8,128)(2,1)S(1)}, u32[]{:S(2)}, u32[]{:S(2)}) collective-permute-start(bf16[2,2,64,128]{3,2,1,0:T(8,128)(2,1)S(1)} %get-tuple-element.48), channel_id=1, source_target_pairs={{0,128},{32,160},{64,192},{96,224},{128,0},{160,32},{192,64},{224,... | collective-permute-start | bytes 196616 | tf_op jit(solution)/shard_map/ppermute | solution.py:349
  88.8 7.3 %collective-permute-start.9 = (bf16[2,2,64,128]{3,2,1,0:T(8,128)(2,1)S(1)}, bf16[2,2,64,128]{3,2,1,0:T(8,128)(2,1)S(1)}, u32[]{:S(2)}, u32[]{:S(2)}) collective-permute-start(bf16[2,2,64,128]{3,2,1,0:T(8,128)(2,1)S(1)} %get-tuple-element.49), channel_id=1, source_target_pairs={{0,192},{32,224},{64,128},{96,160},{128,64},{160,96},{192,0},{224,... | collective-permute-start | bytes 196616 | tf_op jit(solution)/shard_map/ppermute | solution.py:349
